TPU v7x, 32 devices: a whole 2x2x4 slice. The times are simulated.
32 devices in a mesh: dp: 16 (over z, y, core), tensor: 2 (over x).
Axes of the slice: x: 2, y: 2, z: 4, core: 2. Of those that a mesh axis runs over, the one named last changes fastest.
Arguments:
- tokens: bfloat16 [16384, 2048], P(('dp', 'tensor')), may hold values from -6 to 6
- cotangent: bfloat16 [16384, 2048], P(('dp', 'tensor')), may hold values from -6 to 6
- lengths: int32 [16], P('dp'), may hold values from 640 to 1024, as said below
- w_query: float32 [2048, 2048], P('dp', 'tensor'), may hold values from -0.125 to 0.125
- query_mean: float32 [2048, 2048], P('dp', 'tensor'), may hold values from -80 to 80
- query_square: float32 [2048, 2048], P('dp', 'tensor'), may hold values from 655.36 to 2621.44
- w_keyval: float32 [2048, 2, 1024], P('dp', None, 'tensor'), may hold values from -0.125 to 0.125
- keyval_mean: float32 [2048, 2, 1024], P('dp', None, 'tensor'), may hold values from -80 to 80
- keyval_square: float32 [2048, 2, 1024], P('dp', None, 'tensor'), may hold values from 655.36 to 2621.44
- w_out: float32 [2048, 2048], P('tensor', 'dp'), may hold values from -2 to 2
- out_mean: float32 [2048, 2048], P('tensor', 'dp'), may hold values from -5 to 5
- out_square: float32 [2048, 2048], P('tensor', 'dp'), may hold values from 2.72 to 10.88
- w_gateup: float32 [2048, 2, 6144], P('dp', None, 'tensor'), may hold values from -0.125 to 0.125
- gateup_mean: float32 [2048, 2, 6144], P('dp', None, 'tensor'), may hold values from -28 to 28
- gateup_square: float32 [2048, 2, 6144], P('dp', None, 'tensor'), may hold values from 81.92 to 327.68
- w_down: float32 [6144, 2048], P('tensor', 'dp'), may hold values from -0.078125 to 0.078125
- down_mean: float32 [6144, 2048], P('tensor', 'dp'), may hold values from -48 to 48
- down_square: float32 [6144, 2048], P('tensor', 'dp'), may hold values from 245.76 to 983.04
- norm_gains: float32 [2, 2048], replicated, may hold values from 0.5 to 1.5
- norm_mean: float32 [2, 2048], replicated, may hold values from -80 to 80
- norm_square: float32 [2, 2048], replicated, may hold values from 819.2 to 3276.8
- head_gains: float32 [2, 128], replicated, may hold values from 0.5 to 1.5
- head_mean: float32 [2, 128], replicated, may hold values from -320 to 320
- head_square: float32 [2, 128], replicated, may hold values from 13107.2 to 52428.8
Outputs:
- layer_out: float32 [16384, 2048], P(('dp', 'tensor'))
- tokens_grad: float32 [16384, 2048], P(('dp', 'tensor'))
- query_next: float32 [2048, 2048], P('dp', 'tensor')
- query_mean_next: float32 [2048, 2048], P('dp', 'tensor')
- query_square_next: float32 [2048, 2048], P('dp', 'tensor')
- keyval_next: float32 [2048, 2, 1024], P('dp', None, 'tensor')
- keyval_mean_next: float32 [2048, 2, 1024], P('dp', None, 'tensor')
- keyval_square_next: float32 [2048, 2, 1024], P('dp', None, 'tensor')
- out_next: float32 [2048, 2048], P('tensor', 'dp')
- out_mean_next: float32 [2048, 2048], P('tensor', 'dp')
- out_square_next: float32 [2048, 2048], P('tensor', 'dp')
- gateup_next: float32 [2048, 2, 6144], P('dp', None, 'tensor')
- gateup_mean_next: float32 [2048, 2, 6144], P('dp', None, 'tensor')
- gateup_square_next: float32 [2048, 2, 6144], P('dp', None, 'tensor')
- down_next: float32 [6144, 2048], P('tensor', 'dp')
- down_mean_next: float32 [6144, 2048], P('tensor', 'dp')
- down_square_next: float32 [6144, 2048], P('tensor', 'dp')
- norm_next: float32 [2, 2048], replicated
- norm_mean_next: float32 [2, 2048], replicated
- norm_square_next: float32 [2, 2048], replicated
- head_next: float32 [2, 128], replicated
- head_mean_next: float32 [2, 128], replicated
- head_square_next: float32 [2, 128], replicated
Inputs may be any that keep to these rules, and one draw needn't show every extreme that they name: Group g holds one sequence of lengths[g] tokens from its first row, the rest of its 1024 rows are padding; in every draw some group's sequence fills all 1024 rows.
All inputs are finite; a program needn't handle non-finite values.
Results may differ from a plain program's by a relative error of at most 0.015.
Values may be sent and summed in bfloat16 or wider, within the bound.
No kernel may reach another device: no remote copies, remote signals or barrier semaphores. Data moves between devices by JAX's collectives and lax.ppermute only.
A program may use at most 320 MiB of HBM per device.

v0:
```python
import jax
import jax.numpy as jnp
from jax import lax
from jax.sharding import PartitionSpec as P

D = 2048
HD = 128
FF = 6144
STEP = 10


EPS_NORM = 1e-06
ROPE_BASE = 1000000.0
BETA_ONE = 0.9
BETA_TWO = 0.95
ADAM_EPS = 1e-08
WEIGHT_DECAY = 0.1
RATE_SCALE = 2.0
GAIN_RATE = 0.6
OUT_FAN = 8.0


def rms_norm(values, gain_vec):
    return (
        values * lax.rsqrt(jnp.mean(values * values, axis=-1, keepdims=True) + EPS_NORM) * gain_vec
    )


def rope_tables(row_count):
    places = jnp.arange(row_count).astype(jnp.float32)
    inverse_freq = ROPE_BASE ** (-(jnp.arange(HD // 2).astype(jnp.float32) * 2.0) / HD)
    angles = places[:, None] * inverse_freq[None, :]
    angles = jnp.concatenate([angles, angles], axis=1)
    return (jnp.cos(angles)[:, None, :], jnp.sin(angles)[:, None, :])


def rotate(values, cosine, sine_part):
    half_size = values.shape[-1] // 2
    turned = jnp.concatenate([-values[..., half_size:], values[..., :half_size]], axis=-1)
    return values * cosine + turned * sine_part


def adam_step(weight, mean_old, square, gradient, step_rate, decay_rate):
    new_mean = BETA_ONE * mean_old + (1.0 - BETA_ONE) * gradient
    new_square = BETA_TWO * square + (1.0 - BETA_TWO) * gradient * gradient
    fix_one = 1.0 - BETA_ONE**STEP
    fix_two = 1.0 - BETA_TWO**STEP
    update = new_mean / fix_one / (jnp.sqrt(new_square / fix_two) + ADAM_EPS)
    return (weight - step_rate * (update + decay_rate * weight), new_mean, new_square)


def group_rows(piece):
    return lax.all_gather(piece, "tensor", axis=0, tiled=True)


def group_sums(piece):
    return lax.psum_scatter(piece, "tensor", scatter_dimension=0, tiled=True)


def on_device(
    tokens,
    cotangent,
    lengths,
    w_query,
    query_mean,
    query_square,
    w_keyval,
    keyval_mean,
    keyval_square,
    w_out,
    out_mean,
    out_square,
    w_gateup,
    gateup_mean,
    gateup_square,
    w_down,
    down_mean,
    down_square,
    norm_gains,
    norm_mean,
    norm_square,
    head_gains,
    head_mean,
    head_square,
):
    tensor_count = lax.axis_size("tensor")
    tensor_index = lax.axis_index("tensor")
    tok_rows = tokens.shape[0]
    cap_rows = tok_rows * tensor_count
    length = lengths[0]
    own_places = tensor_index * tok_rows + jnp.arange(tok_rows)
    live_flag = (own_places < length).astype(jnp.float32)[:, None]
    stream = tokens.astype(jnp.float32)
    scale = HD ** (-0.5)

    def fetch_attn():
        return (
            lax.all_gather(w_query.astype(jnp.bfloat16), "dp", axis=0, tiled=True),
            lax.all_gather(w_keyval.astype(jnp.bfloat16), "dp", axis=0, tiled=True),
            lax.all_gather(w_out.astype(jnp.bfloat16), "dp", axis=1, tiled=True),
        )

    def fetch_mlp():
        return (
            lax.all_gather(w_gateup.astype(jnp.bfloat16), "dp", axis=0, tiled=True),
            lax.all_gather(w_down.astype(jnp.bfloat16), "dp", axis=1, tiled=True),
        )

    query_full, keyval_full, out_full = fetch_attn()
    normed_one = group_rows(rms_norm(stream, norm_gains[0]).astype(jnp.bfloat16))
    queries = jnp.dot(normed_one, query_full, preferred_element_type=jnp.float32)
    keyvals = jnp.einsum("td,dsk->tsk", normed_one, keyval_full, preferred_element_type=jnp.float32)
    heads_here = queries.shape[1] // HD
    pair_heads = keyvals.shape[2] // HD
    group_size = heads_here // pair_heads
    cosine, sine_part = rope_tables(cap_rows)

    def shape_qk(query_rows, key_rows, gain_pair):
        query_turned = rotate(
            rms_norm(query_rows.reshape(cap_rows, heads_here, HD), gain_pair[0]), cosine, sine_part
        )
        key_turned = rotate(
            rms_norm(key_rows.reshape(cap_rows, pair_heads, HD), gain_pair[1]), cosine, sine_part
        )
        return (query_turned, key_turned)

    query_turned, key_turned = shape_qk(queries, keyvals[:, 0], head_gains)
    query_low = query_turned.astype(jnp.bfloat16).reshape(cap_rows, pair_heads, group_size, HD)
    key_low = key_turned.astype(jnp.bfloat16)
    value_low = keyvals[:, 1].reshape(cap_rows, pair_heads, HD).astype(jnp.bfloat16)
    block_rows = min(512, cap_rows)
    block_count = cap_rows // block_rows
    key_places = jnp.arange(cap_rows)
    starts = jnp.arange(block_count) * block_rows

    def masked_scores(query_blk, offset):
        scores = (
            jnp.einsum("tngh,snh->ngts", query_blk, key_low, preferred_element_type=jnp.float32)
            * scale
        )
        query_places = offset + jnp.arange(block_rows)
        allowed = (key_places[None, :] <= query_places[:, None]) & (key_places[None, :] < length)
        return jnp.where(allowed, scores, -1e30)

    def attend(offset):
        query_blk = lax.dynamic_slice_in_dim(query_low, offset, block_rows, 0)
        scores = masked_scores(query_blk, offset)
        row_top = jnp.max(scores, axis=-1, keepdims=True)
        raised = jnp.exp(scores - row_top)
        row_total = jnp.sum(raised, axis=-1, keepdims=True)
        chances = (raised / row_total).astype(jnp.bfloat16)
        mixed_blk = jnp.einsum(
            "ngts,snh->tngh", chances, value_low, preferred_element_type=jnp.float32
        )
        return (mixed_blk, (row_top + jnp.log(row_total))[..., 0])

    mixed_blocks, log_total = lax.map(attend, starts)
    attended = mixed_blocks.reshape(cap_rows, heads_here * HD).astype(jnp.bfloat16)
    middle = stream + group_sums(jnp.dot(attended, out_full, preferred_element_type=jnp.float32))
    gateup_full, down_full = fetch_mlp()
    second = group_rows(rms_norm(middle, norm_gains[1]).astype(jnp.bfloat16))
    gate_up = jnp.einsum("td,dsf->tsf", second, gateup_full, preferred_element_type=jnp.float32)

    def swiglu(pair_rows):
        return jax.nn.silu(pair_rows[:, 0]) * pair_rows[:, 1]

    hidden_f, swiglu_back = jax.vjp(swiglu, gate_up)
    hidden = hidden_f.astype(jnp.bfloat16)
    layer_out = middle + group_sums(jnp.dot(hidden, down_full, preferred_element_type=jnp.float32))
    upstream = cotangent.astype(jnp.float32) * live_flag
    back_all = group_rows(upstream.astype(jnp.bfloat16))
    gateup_full, down_full = fetch_mlp()
    d_hidden = jnp.einsum("td,fd->tf", back_all, down_full, preferred_element_type=jnp.float32)
    g_down = jnp.einsum("tf,td->fd", hidden, back_all, preferred_element_type=jnp.float32)
    d_gateup = swiglu_back(d_hidden)[0].astype(jnp.bfloat16)
    g_gateup = jnp.einsum("td,tsf->dsf", second, d_gateup, preferred_element_type=jnp.float32)
    d_second = group_sums(
        jnp.einsum("tsf,dsf->td", d_gateup, gateup_full, preferred_element_type=jnp.float32)
    )
    _, second_back = jax.vjp(rms_norm, middle, norm_gains[1])
    d_middle, g_second_gain = second_back(d_second)
    d_middle = d_middle + upstream
    branch_all = group_rows(d_middle.astype(jnp.bfloat16))
    query_full, keyval_full, out_full = fetch_attn()
    g_out = jnp.einsum("tq,td->qd", attended, branch_all, preferred_element_type=jnp.float32)
    d_attended = jnp.einsum("td,qd->tq", branch_all, out_full, preferred_element_type=jnp.float32)
    d_attended = d_attended.astype(jnp.bfloat16).reshape(cap_rows, pair_heads, group_size, HD)

    def attend_back(sums_in, item):
        key_grad, value_grad = sums_in
        offset, total_blk = item
        query_blk = lax.dynamic_slice_in_dim(query_low, offset, block_rows, 0)
        grad_blk = lax.dynamic_slice_in_dim(d_attended, offset, block_rows, 0)
        scores = masked_scores(query_blk, offset)
        chances = jnp.exp(scores - total_blk[..., None])
        d_chances = jnp.einsum(
            "tngh,snh->ngts", grad_blk, value_low, preferred_element_type=jnp.float32
        )
        inner = jnp.sum(chances * d_chances, axis=-1, keepdims=True)
        d_scores = (chances * (d_chances - inner) * scale).astype(jnp.bfloat16)
        value_grad = value_grad + jnp.einsum(
            "ngts,tngh->snh",
            chances.astype(jnp.bfloat16),
            grad_blk,
            preferred_element_type=jnp.float32,
        )
        key_grad = key_grad + jnp.einsum(
            "ngts,tngh->snh", d_scores, query_blk, preferred_element_type=jnp.float32
        )
        query_grad = jnp.einsum(
            "ngts,snh->tngh", d_scores, key_low, preferred_element_type=jnp.float32
        )
        return ((key_grad, value_grad), query_grad)

    zeros_kv = jnp.zeros((cap_rows, pair_heads, HD), jnp.float32)
    (key_grad, value_grad), query_grad = lax.scan(
        attend_back, (zeros_kv, zeros_kv), (starts, log_total)
    )
    _, turn_back = jax.vjp(shape_qk, queries, keyvals[:, 0], head_gains)
    d_queries, d_keys, g_head = turn_back((query_grad.reshape(cap_rows, heads_here, HD), key_grad))
    d_queries = d_queries.astype(jnp.bfloat16)
    d_keyvals = jnp.stack([d_keys, value_grad.reshape(cap_rows, pair_heads * HD)], axis=1).astype(
        jnp.bfloat16
    )
    g_query = jnp.einsum("td,tq->dq", normed_one, d_queries, preferred_element_type=jnp.float32)
    g_keyval = jnp.einsum("td,tsk->dsk", normed_one, d_keyvals, preferred_element_type=jnp.float32)
    d_first = jnp.einsum("tq,dq->td", d_queries, query_full, preferred_element_type=jnp.float32)
    d_first = d_first + jnp.einsum(
        "tsk,dsk->td", d_keyvals, keyval_full, preferred_element_type=jnp.float32
    )
    d_first = group_sums(d_first)
    _, first_back = jax.vjp(rms_norm, stream, norm_gains[0])
    d_stream, g_first_gain = first_back(d_first)
    tokens_grad = d_stream + d_middle
    query_sum, keyval_sum, out_sum, gateup_sum, down_sum = (
        lax.psum_scatter(g_query, "dp", scatter_dimension=0, tiled=True),
        lax.psum_scatter(g_keyval, "dp", scatter_dimension=0, tiled=True),
        lax.psum_scatter(g_out, "dp", scatter_dimension=1, tiled=True),
        lax.psum_scatter(g_gateup, "dp", scatter_dimension=0, tiled=True),
        lax.psum_scatter(g_down, "dp", scatter_dimension=1, tiled=True),
    )
    norm_sum, head_sum = lax.psum(
        (jnp.stack([g_first_gain, g_second_gain]), g_head), ("dp", "tensor")
    )
    wide_rate = RATE_SCALE * D ** (-0.5)
    query_new = adam_step(w_query, query_mean, query_square, query_sum, wide_rate, WEIGHT_DECAY)
    keyval_new = adam_step(
        w_keyval, keyval_mean, keyval_square, keyval_sum, wide_rate, WEIGHT_DECAY
    )
    out_new = adam_step(
        w_out, out_mean, out_square, out_sum, RATE_SCALE * OUT_FAN ** (-0.5), WEIGHT_DECAY
    )
    gateup_new = adam_step(
        w_gateup, gateup_mean, gateup_square, gateup_sum, wide_rate, WEIGHT_DECAY
    )
    down_new = adam_step(
        w_down, down_mean, down_square, down_sum, RATE_SCALE * FF ** (-0.5), WEIGHT_DECAY
    )
    norm_new = adam_step(norm_gains, norm_mean, norm_square, norm_sum, GAIN_RATE, 0.0)
    head_new = adam_step(head_gains, head_mean, head_square, head_sum, GAIN_RATE, 0.0)
    return (
        layer_out,
        tokens_grad,
        query_new[0],
        query_new[1],
        query_new[2],
        keyval_new[0],
        keyval_new[1],
        keyval_new[2],
        out_new[0],
        out_new[1],
        out_new[2],
        gateup_new[0],
        gateup_new[1],
        gateup_new[2],
        down_new[0],
        down_new[1],
        down_new[2],
        norm_new[0],
        norm_new[1],
        norm_new[2],
        head_new[0],
        head_new[1],
        head_new[2],
    )


def solution(mesh):
    placed = (
        P(("dp", "tensor"), None),
        P(("dp", "tensor"), None),
        P("dp"),
        P("dp", "tensor"),
        P("dp", "tensor"),
        P("dp", "tensor"),
        P("dp", None, "tensor"),
        P("dp", None, "tensor"),
        P("dp", None, "tensor"),
        P("tensor", "dp"),
        P("tensor", "dp"),
        P("tensor", "dp"),
        P("dp", None, "tensor"),
        P("dp", None, "tensor"),
        P("dp", None, "tensor"),
        P("tensor", "dp"),
        P("tensor", "dp"),
        P("tensor", "dp"),
        P(),
        P(),
        P(),
        P(),
        P(),
        P(),
    )
    return jax.shard_map(
        on_device,
        mesh=mesh,
        in_specs=placed,
        out_specs=(
            P(("dp", "tensor"), None),
            P(("dp", "tensor"), None),
            P("dp", "tensor"),
            P("dp", "tensor"),
            P("dp", "tensor"),
            P("dp", None, "tensor"),
            P("dp", None, "tensor"),
            P("dp", None, "tensor"),
            P("tensor", "dp"),
            P("tensor", "dp"),
            P("tensor", "dp"),
            P("dp", None, "tensor"),
            P("dp", None, "tensor"),
            P("dp", None, "tensor"),
            P("tensor", "dp"),
            P("tensor", "dp"),
            P("tensor", "dp"),
            P(),
            P(),
            P(),
            P(),
            P(),
            P(),
        ),
        check_vma=False,
    )
```

profile of v0, /device:TPU:0, one launch (start us, length us, event | category | flops | bytes accessed | tf_op | source)
XLA Modules:
  0.0 2424.4 jit_solution(6181762749703331011)
XLA Ops:
  20.6 54.0 %all-gather.10.cloned.1.call-done = bf16[1024,2048]{1,0:T(8,128)(2,1)} async-done(((bf16[512,2048]{1,0:T(8,128)(2,1)}), bf16[1024,2048]{1,0:T(8,128)(2,1)}) %all-gather.10.cloned.1.call-update) | async-done | bytes 4194320 | tf_op jit(solution)/shard_map/all_gather | solution.py:53
  74.5 56.0 %all-gather.14.cloned.1.call-done = bf16[2048,2,512]{0,2,1:T(8,128)(2,1)} async-done(((bf16[128,2,512]{0,2,1:T(8,128)(2,1)}), bf16[2048,2,512]{0,2,1:T(8,128)(2,1)}) %all-gather.14.cloned.1.call-update) | async-done | bytes 4194320 | tf_op jit(solution)/shard_map/all_gather | solution.py:99
  142.6 39.4 %all-gather.12.cloned.1.call-done = bf16[2048,1024]{1,0:T(8,128)(2,1)} async-done(((bf16[128,1024]{1,0:T(8,128)(2,1)}), bf16[2048,1024]{1,0:T(8,128)(2,1)}) %all-gather.12.cloned.1.call-update) | async-done | bytes 4194320 | tf_op jit(solution)/shard_map/all_gather | solution.py:98
  219.2 43.0 %while.30 = (s32[]{:T(128)}, bf16[2,512,4,2,128]{4,1,3,2,0:T(8,128)(2,1)}, f32[2,4,2,512]{3,2,1,0:T(2,128)S(1)}, s32[2]{0:T(128)S(1)}, s32[]{:T(128)}, /*index=5...) while((s32[]{:T(128)}, ...), condition=%wide.region_6.7_spmd.clone.clone, body=%wide.region_3.6_spmd.clone.clone.sunk | while | flops 2198861312 | bytes 74586336 | solution.py:157
  269.1 10.7 fusion.105
  279.8 98.4 %reduce-scatter.10.cloned.1.call-done = f32[512,2048]{1,0:T(8,128)} async-done(((f32[1024,2048]{1,0:T(8,128)}), f32[512,2048]{1,0:T(8,128)}) %reduce-scatter.10.cloned.1.call-update) | async-done | bytes 4194320 | tf_op jit(solution)/shard_map/reduce_scatter | solution.py:57
  393.6 48.1 %all-gather.18.cloned.1.call-done = bf16[1024,2048]{1,0:T(8,128)(2,1)} async-done(((bf16[512,2048]{1,0:T(8,128)(2,1)}), bf16[1024,2048]{1,0:T(8,128)(2,1)}) %all-gather.18.cloned.1.call-update) | async-done | bytes 4194320 | tf_op jit(solution)/shard_map/all_gather | solution.py:53
  441.7 130.8 %all-gather.20.cloned.1.call-done = bf16[2048,2,3072]{2,0,1:T(8,128)(2,1)} async-done(((bf16[128,2,3072]{2,0,1:T(8,128)(2,1)}), bf16[2048,2,3072]{2,0,1:T(8,128)(2,1)}) %all-gather.20.cloned.1.call-update) | async-done | bytes 25165840 | tf_op jit(solution)/shard_map/all_gather | solution.py:105
  572.5 32.7 %fusion.61 = f32[1024,2,3072]{2,0,1:T(8,128)} fusion(bf16[2048,2,3072]{2,0,1:T(8,128)(2,1)} %all-gather.20.cloned.1.call-done, bf16[1024,2048]{1,0:T(8,128)(2,1)} %all-gather.18.cloned.1.call-done), kind=kOutput, calls=%fused_computation.97 | convolution fusion | flops 25769803776 | bytes 54525952 | tf_op jit(solution)/shard_map/td,dsf->tsf/dot_general | solution.py:162
  605.2 26.3 %all-gather.24.cloned.1.call-done = bf16[1024,2048]{1,0:T(8,128)(2,1)} async-done(((bf16[512,2048]{1,0:T(8,128)(2,1)}), bf16[1024,2048]{1,0:T(8,128)(2,1)}) %all-gather.24.cloned.1.call-update) | async-done | bytes 4194320 | tf_op jit(solution)/shard_map/all_gather | solution.py:53
  631.5 106.4 %all-gather.22.cloned.1.call-done = bf16[3072,2048]{1,0:T(8,128)(2,1)} async-done(((bf16[3072,128]{1,0:T(8,128)(2,1)}), bf16[3072,2048]{1,0:T(8,128)(2,1)}) %all-gather.22.cloned.1.call-update) | async-done | bytes 12582928 | tf_op jit(solution)/shard_map/all_gather | solution.py:106
  737.9 34.4 %multiply_bitcast_fusion = (f32[1024,1,3072]{2,0,1:T(8,128)}, f32[1024,1,3072]{2,0,1:T(8,128)}, bf16[1024,3072]{1,0:T(8,128)(2,1)}) fusion(f32[1024,2,3072]{2,0,1:T(8,128)} %fusion.61, bf16[1024,2048]{1,0:T(8,128)(2,1)} %all-gather.24.cloned.1.call-done, bf16[3072,2048]{1,0:T(8,128)(2,1)} %all-gather.22.cloned.1.call-done), kind=kOutput, calls=%fused_computation.66 | convolution fusion | flops 12928942080 | bytes 73400320 | tf_op jit(solution)/shard_map/td,fd->tf/dot_general | solution.py:173
  772.3 34.2 %convolution_bitcast_fusion = f32[1024,2048]{1,0:T(8,128)} fusion(bf16[2048,2,3072]{2,0,1:T(8,128)(2,1)} %all-gather.20.cloned.1.call-done, f32[1024,1,3072]{2,0,1:T(8,128)} %get-tuple-element.456, f32[1024,1,3072]{2,0,1:T(8,128)} %get-tuple-element.455), kind=kOutput, calls=%fused_computation.82 | convolution fusion | flops 25782386688 | bytes 58720256 | tf_op jit(solution)/shard_map/tsf,dsf->td/dot_general | solution.py:178
  806.6 19.0 fusion.106
  825.7 78.4 %reduce-scatter.14.cloned.1.call-done = f32[512,2048]{1,0:T(8,128)} async-done(((f32[1024,2048]{1,0:T(8,128)}), f32[512,2048]{1,0:T(8,128)}) %reduce-scatter.14.cloned.1.call-update) | async-done | bytes 4194320 | tf_op jit(solution)/shard_map/reduce_scatter | solution.py:57
  909.2 96.5 %reduce-scatter.12.cloned.1.call-done = f32[512,2048]{1,0:T(8,128)} async-done(((f32[1024,2048]{1,0:T(8,128)}), f32[512,2048]{1,0:T(8,128)}) %reduce-scatter.12.cloned.1.call-update) | async-done | bytes 4194320 | tf_op jit(solution)/shard_map/reduce_scatter | solution.py:57
  1013.6 56.8 %all-gather.26.cloned.1.call-done = bf16[1024,2048]{1,0:T(8,128)(2,1)} async-done(((bf16[512,2048]{1,0:T(8,128)(2,1)}), bf16[1024,2048]{1,0:T(8,128)(2,1)}) %all-gather.26.cloned.1.call-update) | async-done | bytes 4194320 | tf_op jit(solution)/shard_map/all_gather | solution.py:53
  1079.8 155.7 %while.31 = (s32[]{:T(128)}, f32[1024,4,128]{0,2,1:T(8,128)}, f32[1024,4,128]{0,2,1:T(8,128)S(1)}, f32[2,512,4,2,128]{4,1,0,3,2:T(8,128)}, s32[2]{0:T(128)S(1)},...) while((s32[]{:T(128)}, f32[1024,4,128]{0,2,1:T(8,128)}, ...), condition=%wide.region_14.15_spmd.clone.clone, body=%wide.region_12.14_spmd.clone.clone.sunk | while | flops 5430586880 | bytes 211868416 | solution.py:216
  1102.4 23.5 bitcast_dynamic-update-slice_fusion.8
  1125.9 23.9 bitcast_add_fusion.5
  1179.7 23.4 bitcast_dynamic-update-slice_fusion.8
  1203.2 24.4 %bitcast_add_fusion.5 = f32[1024,4,128]{0,2,1:T(8,128)} fusion(f32[1024,4,128]{0,2,1:T(8,128)} %get-tuple-element.643, f32[4,2,512,1024]{3,2,1,0:T(8,128)} %fusion.159, f32[4,512,2,1024]{3,1,2,0:T(8,128)} %fusion.160, pred[]{:T(512)S(6)} %compare.11, bf16[1024,4,2,128]{3,0,2,1:T(8,128)(2,1)} %get-tuple-element.661, s32[]{:T(128)S(6)} %select_n.56), kind=kOutput, calls=%fused_computation.37.clone.1 | convolution fusion | flops 1095767040 | bytes 72351752 | tf_op jit(solution)/shard_map/while/body/eval_jaxpr/ngts,tngh->snh/dot_general | solution.py:207
  1242.5 10.7 fusion.63
  1281.6 10.8 fusion.108
  1292.5 20.0 fusion.110
  1328.0 38.7 %fusion.59 = f32[2048,2,3072]{2,0,1:T(8,128)} fusion(bf16[1024,2048]{1,0:T(8,128)(2,1)} %all-gather.18.cloned.1.call-done, f32[1024,1,3072]{2,0,1:T(8,128)} %get-tuple-element.456, f32[1024,1,3072]{2,0,1:T(8,128)} %get-tuple-element.455), kind=kOutput, calls=%fused_computation.95 | convolution fusion | flops 25782386688 | bytes 79691776 | tf_op jit(solution)/shard_map/td,tsf->dsf/dot_general | solution.py:176
  1373.6 93.6 %reduce-scatter.22.cloned.1.call-done = f32[1024,128]{1,0:T(8,128)} async-done(((f32[1024,2048]{1,0:T(8,128)}), f32[1024,128]{1,0:T(8,128)}) %reduce-scatter.22.cloned.1.call-update) | async-done | bytes 524304 | tf_op jit(solution)/shard_map/reduce_scatter | solution.py:238
  1469.6 106.5 %reduce-scatter.18.cloned.1.call-done = f32[128,1024]{1,0:T(8,128)} async-done(((f32[2048,1024]{1,0:T(8,128)}), f32[128,1024]{1,0:T(8,128)}) %reduce-scatter.18.cloned.1.call-update) | async-done | bytes 524304 | tf_op jit(solution)/shard_map/reduce_scatter | solution.py:236
  1578.6 245.6 %reduce-scatter.26.cloned.1.call-done = f32[3072,128]{1,0:T(8,128)} async-done(((f32[3072,2048]{1,0:T(8,128)}), f32[3072,128]{1,0:T(8,128)}) %reduce-scatter.26.cloned.1.call-update) | async-done | bytes 1572880 | tf_op jit(solution)/shard_map/reduce_scatter | solution.py:240
  1830.0 94.8 %reduce-scatter.16.cloned.1.call-done = f32[512,2048]{1,0:T(8,128)} async-done(((f32[1024,2048]{1,0:T(8,128)}), f32[512,2048]{1,0:T(8,128)}) %reduce-scatter.16.cloned.1.call-update) | async-done | bytes 4194320 | tf_op jit(solution)/shard_map/reduce_scatter | solution.py:57
  1928.4 39.6 %all-reduce.8 = (f32[2,2048]{1,0:T(2,128)S(1)}, f32[2,128]{1,0:T(2,128)S(1)}) all-reduce(f32[2,2048]{1,0:T(2,128)S(1)} %pad_maximum_fusion.4, f32[2,128]{1,0:T(2,128)S(1)} %pad_add_fusion.2), channel_id=1, replica_groups=mesh['dp'=16,'tensor'=2] {'dp','tensor'}, use_global_device_ids=true, to_apply=%region_26.27 | all-reduce | flops 4352 | bytes 34816 | tf_op jit(solution)/shard_map/psum | solution.py:242
  1978.2 418.5 %reduce-scatter.24.cloned.1.call-done = f32[128,2,3072]{2,0,1:T(8,128)} async-done(((f32[2048,2,3072]{2,0,1:T(8,128)}), f32[128,2,3072]{2,0,1:T(8,128)}) %reduce-scatter.24.cloned.1.call-update) | async-done | bytes 3145744 | tf_op jit(solution)/shard_map/reduce_scatter | solution.py:239
  (322 shorter events, 303.4 us)
Async XLA Ops:
  7.2 67.3 %all-gather.10.cloned.1.call-start = ((), (), s32[]{:S(2)}) async-start(), calls=%async_computation.9 | async-start | bytes 6291456 | tf_op jit(solution)/shard_map/all_gather | solution.py:53
  14.9 115.6 %all-gather.14.cloned.1.call-start = ((), (), s32[]{:S(2)}) async-start(), calls=%async_computation.11 | async-start | bytes 4456448 | tf_op jit(solution)/shard_map/all_gather | solution.py:99
  15.9 166.1 %all-gather.12.cloned.1.call-start = ((), (), s32[]{:S(2)}) async-start(), calls=%async_computation.10 | async-start | bytes 4456448 | tf_op jit(solution)/shard_map/all_gather | solution.py:98
  16.7 252.3 %all-gather.16.cloned.1.call-start = ((), (), s32[]{:S(2)}) async-start(), calls=%async_computation.12 | async-start | bytes 4456448 | tf_op jit(solution)/shard_map/all_gather | solution.py:100
  17.5 360.7 %reduce-scatter.10.cloned.1.call-start = ((), (), s32[]{:S(2)}) async-start(), calls=%async_computation.13 | async-start | bytes 12582912 | tf_op jit(solution)/shard_map/reduce_scatter | solution.py:57
  17.7 194.6 %copy-start.69 = (f32[128]{0:T(128)}, f32[128]{0:T(128)S(1)}, u32[]{:S(2)}) copy-start(f32[128]{0:T(128)S(1)} %get-tuple-element.472) | copy-start | bytes 1540
  20.1 192.2 %copy-start.11 = (f32[1024,128]{1,0:T(8,128)}, f32[1024,128]{1,0:T(8,128)S(1)}, u32[]{:S(2)}) copy-start(f32[1024,128]{1,0:T(8,128)S(1)} %get-tuple-element.467) | copy-start | bytes 1572868
  20.1 192.2 %copy-start.13 = (f32[1024,128]{1,0:T(8,128)}, f32[1024,128]{1,0:T(8,128)S(1)}, u32[]{:S(2)}) copy-start(f32[1024,128]{1,0:T(8,128)S(1)} %get-tuple-element.468) | copy-start | bytes 1572868
  279.8 161.9 %all-gather.18.cloned.1.call-start = ((), (), s32[]{:S(2)}) async-start(), calls=%async_computation.14 | async-start | bytes 6291456 | tf_op jit(solution)/shard_map/all_gather | solution.py:53
  384.8 187.7 %all-gather.20.cloned.1.call-start = ((), (), s32[]{:S(2)}) async-start(), calls=%async_computation.15 | async-start | bytes 26738688 | tf_op jit(solution)/shard_map/all_gather | solution.py:105
  387.7 243.7 %all-gather.24.cloned.1.call-start = ((), (), s32[]{:S(2)}) async-start(), calls=%async_computation.18 | async-start | bytes 6291456 | tf_op jit(solution)/shard_map/all_gather | solution.py:53
  392.5 345.4 %all-gather.22.cloned.1.call-start = ((), (), s32[]{:S(2)}) async-start(), calls=%async_computation.16 | async-start | bytes 13369344 | tf_op jit(solution)/shard_map/all_gather | solution.py:106
  393.6 510.6 %reduce-scatter.14.cloned.1.call-start = ((), (), s32[]{:S(2)}) async-start(), calls=%async_computation.19 | async-start | bytes 12582912 | tf_op jit(solution)/shard_map/reduce_scatter | solution.py:57
  806.5 199.1 %reduce-scatter.12.cloned.1.call-start = ((), (), s32[]{:S(2)}) async-start(), calls=%async_computation.17 | async-start | bytes 12582912 | tf_op jit(solution)/shard_map/reduce_scatter | solution.py:57
  825.7 180.0 %copy-start.16 = (bf16[512,2048]{1,0:T(8,128)(2,1)S(1)}, bf16[512,2048]{1,0:T(8,128)(2,1)}, u32[]{:S(2)}) copy-start(bf16[512,2048]{1,0:T(8,128)(2,1)} %param.29) | copy-start | bytes 6291460
  825.7 180.0 %copy-start.62 = (f32[512]{0:T(512)S(1)}, f32[512]{0:T(512)}, u32[]{:S(2)}) copy-start(f32[512]{0:T(512)} %copy-done.61) | copy-start | bytes 6148
  825.7 244.7 %all-gather.26.cloned.1.call-start = ((), (), s32[]{:S(2)}) async-start(), calls=%async_computation.20 | async-start | bytes 6291456 | tf_op jit(solution)/shard_map/all_gather | solution.py:53
  1013.5 353.4 %reduce-scatter.20.cloned.1.call-start = ((), (), s32[]{:S(2)}) async-start(), calls=%async_computation.23 | async-start | bytes 8912896 | tf_op jit(solution)/shard_map/reduce_scatter | solution.py:237
  1253.2 213.9 %reduce-scatter.22.cloned.1.call-start = ((), (), s32[]{:S(2)}) async-start(), calls=%async_computation.24 | async-start | bytes 8912896 | tf_op jit(solution)/shard_map/reduce_scatter | solution.py:238
  1263.8 312.3 %reduce-scatter.18.cloned.1.call-start = ((), (), s32[]{:S(2)}) async-start(), calls=%async_computation.22 | async-start | bytes 8912896 | tf_op jit(solution)/shard_map/reduce_scatter | solution.py:236
  1292.4 531.8 %reduce-scatter.26.cloned.1.call-start = ((), (), s32[]{:S(2)}) async-start(), calls=%async_computation.26 | async-start | bytes 26738688 | tf_op jit(solution)/shard_map/reduce_scatter | solution.py:240
  1312.5 612.4 %reduce-scatter.16.cloned.1.call-start = ((), (), s32[]{:S(2)}) async-start(), calls=%async_computation.21 | async-start | bytes 12582912 | tf_op jit(solution)/shard_map/reduce_scatter | solution.py:57
  1328.0 1068.8 %reduce-scatter.24.cloned.1.call-start = ((), (), s32[]{:S(2)}) async-start(), calls=%async_computation.25 | async-start | bytes 53477376 | tf_op jit(solution)/shard_map/reduce_scatter | solution.py:239
  1370.0 206.2 %copy-start.27 = (f32[128,1024]{1,0:T(8,128)S(1)}, f32[128,1024]{1,0:T(8,128)}, u32[]{:S(2)}) copy-start(f32[128,1024]{1,0:T(8,128)} %param.31) | copy-start | bytes 1572868
  1370.0 206.2 %copy-start.41 = (f32[128,1024]{1,0:T(8,128)S(1)}, f32[128,1024]{1,0:T(8,128)}, u32[]{:S(2)}) copy-start(f32[128,1024]{1,0:T(8,128)} %param.32) | copy-start | bytes 1572868
  1370.0 206.2 %copy-start.42 = (f32[128,1024]{1,0:T(8,128)S(1)}, f32[128,1024]{1,0:T(8,128)}, u32[]{:S(2)}) copy-start(f32[128,1024]{1,0:T(8,128)} %param.33) | copy-start | bytes 1572868
  1578.6 346.3 %copy-start.5 = (bf16[512,2048]{1,0:T(8,128)(2,1)S(1)}, bf16[512,2048]{1,0:T(8,128)(2,1)}, u32[]{:S(2)}) copy-start(bf16[512,2048]{1,0:T(8,128)(2,1)} %param.28) | copy-start | bytes 6291460
  1578.6 346.3 %copy-start.52 = (f32[1,2048]{1,0:T(1,128)S(1)}, f32[1,2048]{1,0:T(1,128)}, u32[]{:S(2)}) copy-start(f32[1,2048]{1,0:T(1,128)} %copy-done.51) | copy-start | bytes 24580
  1578.6 346.3 %copy-start.60 = (f32[512]{0:T(512)S(1)}, f32[512]{0:T(512)}, u32[]{:S(2)}) copy-start(f32[512]{0:T(512)} %copy-done.59) | copy-start | bytes 6148
  1830.0 138.6 %copy-start.55 = (f32[2,2048]{1,0:T(2,128)S(1)}, f32[2,2048]{1,0:T(2,128)}, u32[]{:S(2)}) copy-start(f32[2,2048]{1,0:T(2,128)} %param.46) | copy-start | bytes 49156
  1830.0 138.6 %copy-start.67 = (f32[2,2048]{1,0:T(2,128)S(1)}, f32[2,2048]{1,0:T(2,128)}, u32[]{:S(2)}) copy-start(f32[2,2048]{1,0:T(2,128)} %param.47) | copy-start | bytes 49156
  1830.0 138.6 %copy-start.68 = (f32[2,2048]{1,0:T(2,128)S(1)}, f32[2,2048]{1,0:T(2,128)}, u32[]{:S(2)}) copy-start(f32[2,2048]{1,0:T(2,128)} %param.48) | copy-start | bytes 49156
  (69 other events, 2148.5 us)
Sparse Core Ops, SparseCore 0:
  15.1 59.4 all-gather.9
  77.3 53.2 all-gather.13
  133.2 48.7 all-gather.11
  184.6 51.6 all-gather.15
  279.9 98.2 reduce-scatter.9
  384.9 56.7 all-gather.17
  443.9 128.5 all-gather.19
  574.7 56.7 all-gather.23
  633.9 103.9 all-gather.21
  806.7 97.4 reduce-scatter.13
  906.4 99.2 reduce-scatter.11
  1013.6 56.7 all-gather.25
  1253.4 104.6 reduce-scatter.19
  1362.5 104.6 reduce-scatter.21
  1471.6 104.4 reduce-scatter.17
  1580.6 243.5 reduce-scatter.25
  1826.5 98.3 reduce-scatter.15
  1928.9 467.7 reduce-scatter.23
where the time goes:
time: 2440 us; the launch traced here: 2420 us
  waiting for transfers between devices  1750 us (72%)
  matrix products  430 us (18%)
  other arithmetic  114 us (5%)
  local copies, waits for them, and re-layouts  64.9 us (3%)
  blocking collectives  39.6 us (2%)
    reduce_scatter x1, waiting for transfers between devices, on_device(): lax.psum_scatter(g_gateup, 'dp', scatter_dimension=0, tiled=True)  419 us
    reduce_scatter x4, waiting for transfers between devices, group_sums(): return lax.psum_scatter(piece, 'tensor', scatter_dimension=0, tiled=True)  368 us
    reduce_scatter x1, waiting for transfers between devices, on_device(): lax.psum_scatter(g_down, 'dp', scatter_dimension=1, tiled=True)  246 us
    all_gather x4, waiting for transfers between devices, group_rows(): return lax.all_gather(piece, 'tensor', axis=0, tiled=True)  185 us
    all_gather x1, waiting for transfers between devices, fetch_mlp(): lax.all_gather(w_gateup.astype(jnp.bfloat16), 'dp', axis=0, tiled=True)  131 us
    reduce_scatter x1, waiting for transfers between devices, on_device(): lax.psum_scatter(g_query, 'dp', scatter_dimension=0, tiled=True)  107 us
    all_gather x1, waiting for transfers between devices, fetch_mlp(): lax.all_gather(w_down.astype(jnp.bfloat16), 'dp', axis=1, tiled=True)  106 us
    reduce_scatter x1, waiting for transfers between devices, on_device(): lax.psum_scatter(g_out, 'dp', scatter_dimension=1, tiled=True)  93.6 us
  transfers between devices with their start and end apart: 18, of which 16 were waited for; matrix products, arithmetic and copies ran while one was open for 12% of the time, Pallas kernels for 0%

commit v1 on v0

v1 whole, which is shorter than its diff:
```python
import functools

import jax
import jax.numpy as jnp
from jax import lax
from jax.experimental import pallas as pl
from jax.experimental.pallas import tpu as pltpu
from jax.sharding import Mesh
from jax.sharding import PartitionSpec as P

D = 2048
HD = 128
FF = 6144
STEP = 10
LEN_MIN = 640

EPS_NORM = 1e-06
ROPE_BASE = 1000000.0
BETA_ONE = 0.9
BETA_TWO = 0.95
ADAM_EPS = 1e-08
WEIGHT_DECAY = 0.1
RATE_SCALE = 2.0
GAIN_RATE = 0.6
OUT_FAN = 8.0
LOG2_E = 1.4426950408889634

BF = jnp.bfloat16
F32 = jnp.float32
ROWS = 256
TILE = 256
CHUNKS = 3
WORK = 5 * 10**8

NN = (((1,), (0,)), ((), ()))
NT = (((1,), (1,)), ((), ()))
TN = (((0,), (0,)), ((), ()))


def mm(a, b, dims=NN):
    return lax.dot_general(a, b, dims, preferred_element_type=F32)


class Order:
    def __init__(self, side, length, core):
        one = jnp.ones_like(side)
        self.scalars = jnp.stack([side, 1 - side, length, 0 * one, one, core, 1 - core]).astype(jnp.int32)

    def call(self, kernel, grid, ins, outs, operands, *, after=(), through=(), vmem=48, scratch=(), work, name):
        count, later, made = len(ins), len(after) + len(through), len(outs)
        anywhere = pl.BlockSpec(memory_space=pl.ANY)

        def run(scalars, *refs):
            first = count + later
            token = refs[first + made]
            for i in range(token.shape[0]):
                token[i] = scalars[i]
            kernel(scalars, *refs[:count], *refs[first : first + made], *refs[first + made + 1 + len(through) :])

        results = pl.pallas_call(
            run,
            grid_spec=pltpu.PrefetchScalarGridSpec(
                num_scalar_prefetch=1,
                grid=grid,
                in_specs=[*ins, *[anywhere] * later],
                out_specs=[spec for spec, _ in outs] + [pl.BlockSpec(memory_space=pltpu.SMEM)] + [anywhere] * len(through),
                scratch_shapes=scratch,
            ),
            out_shape=[shape for _, shape in outs]
            + [shaped(self.scalars.shape, jnp.int32)]
            + [shaped(v.shape, v.dtype) for v in through],
            input_output_aliases={1 + count + len(after) + i: made + 1 + i for i in range(len(through))},
            compiler_params=pltpu.CompilerParams(vmem_limit_bytes=vmem * 2**20),
            cost_estimate=pl.CostEstimate(flops=int(work * WORK), bytes_accessed=1, transcendentals=0),
            name=name,
        )(self.scalars, *operands, *after, *through)
        self.scalars = results[made]
        return results[:made] + results[made + 1 :]


SIDE, OTHER_SIDE, LENGTH, FIRST, SECOND, CORE, OTHER_CORE = range(7)


def shaped(shape, dtype):
    return jax.ShapeDtypeStruct(shape, dtype)


def held(shape):
    return pl.BlockSpec(shape, lambda *_: (0,) * len(shape), pipeline_mode=pl.Buffered(1))


def turn(values, gain, cosine, sine):
    scale = lax.rsqrt(jnp.mean(values * values, axis=-1, keepdims=True) + EPS_NORM)
    normed = values * scale * gain
    return normed * cosine + pltpu.roll(normed, HD // 2, 1) * sine


def turn_back(grad, values, gain, cosine, sine):
    scale = lax.rsqrt(jnp.mean(values * values, axis=-1, keepdims=True) + EPS_NORM)
    d_normed = grad * cosine + pltpu.roll(grad * sine, HD // 2, 1)
    hat = values * scale
    d_gain = jnp.sum(d_normed * hat, axis=0, keepdims=True)
    d_hat = d_normed * gain
    inner = jnp.mean(d_hat * hat, axis=-1, keepdims=True)
    return scale * (d_hat - hat * inner), d_gain


def key_spans(block):
    start = block * ROWS
    free = min(start, LEN_MIN // ROWS * ROWS)
    spans = []
    if free:
        spans.append((0, free, False, False))
    if start > free:
        spans.append((free, start, False, True))
    spans.append((start, start + ROWS, True, start + ROWS > LEN_MIN))
    return spans


def raised_scores(query, keys, span, length):
    first, last, causal, ragged = span
    scores = mm(query, keys[first:last], NT) * (HD**-0.5 * LOG2_E)
    raised = jnp.exp2(scores)
    allowed = None
    shape = raised.shape
    if causal:
        place = lax.broadcasted_iota(jnp.int32, shape, 0) % ROWS
        allowed = lax.broadcasted_iota(jnp.int32, shape, 1) <= place
    if ragged:
        live = lax.broadcasted_iota(jnp.int32, shape, 1) + first < length
        allowed = live if allowed is None else allowed & live
    return raised if allowed is None else jnp.where(allowed, raised, 0.0)


def split_heads(qkv_ref, group):
    width = group * HD
    queries = [qkv_ref[:, h * HD : (h + 1) * HD] for h in range(group)]
    return queries, qkv_ref[:, width : width + HD], qkv_ref[:, width + HD : width + 2 * HD]


def attend_kernel(group, place_ref, own_ref, other_ref, weight_ref, cos_ref, sin_ref, gain_ref, qkv_ref, out_ref):
    side, length = place_ref[SIDE], place_ref[LENGTH]
    half = own_ref.shape[0]
    qkv_ref[pl.ds(pl.multiple_of(side * half, half), half), :] = mm(own_ref[...], weight_ref[...])
    qkv_ref[pl.ds(pl.multiple_of((1 - side) * half, half), half), :] = mm(other_ref[...], weight_ref[...])
    cosine, sine = cos_ref[...], sin_ref[...]
    queries, keys, values = split_heads(qkv_ref, group)
    turned = [turn(q, gain_ref[0:1], cosine, sine).astype(BF) for q in queries]
    keys = turn(keys, gain_ref[1:2], cosine, sine).astype(BF)
    values = values.astype(BF)
    for block in range(qkv_ref.shape[0] // ROWS):
        rows = slice(block * ROWS, (block + 1) * ROWS)
        query = jnp.concatenate([t[rows] for t in turned], axis=0)
        total, mixed = 0.0, 0.0
        for span in key_spans(block):
            raised = raised_scores(query, keys, span, length)
            total = total + jnp.sum(raised, axis=-1, keepdims=True)
            mixed = mixed + mm(raised.astype(BF), values[span[0] : span[1]])
        mixed = (mixed / total).astype(BF)
        for h in range(group):
            out_ref[rows, h * HD : (h + 1) * HD] = mixed[h * ROWS : (h + 1) * ROWS]


def attend_back_kernel(
    group,
    place_ref,
    qkv_ref,
    own_ref,
    other_ref,
    cos_ref,
    sin_ref,
    gain_ref,
    out_ref,
    gain_out,
    grad_ref,
    dk_ref,
    dv_ref,
):
    side, length = place_ref[SIDE], place_ref[LENGTH]
    half = own_ref.shape[0]
    grad_ref[pl.ds(pl.multiple_of(side * half, half), half), :] = own_ref[...]
    grad_ref[pl.ds(pl.multiple_of((1 - side) * half, half), half), :] = other_ref[...]
    cosine, sine = cos_ref[...], sin_ref[...]
    queries, raw_keys, values = split_heads(qkv_ref, group)
    turned = [turn(q, gain_ref[0:1], cosine, sine).astype(BF) for q in queries]
    keys = turn(raw_keys, gain_ref[1:2], cosine, sine).astype(BF)
    values = values.astype(BF)
    dk_ref[...] = jnp.zeros_like(dk_ref)
    dv_ref[...] = jnp.zeros_like(dv_ref)
    q_gain = jnp.zeros((1, HD), F32)
    for block in range(qkv_ref.shape[0] // ROWS):
        rows = slice(block * ROWS, (block + 1) * ROWS)
        query = jnp.concatenate([t[rows] for t in turned], axis=0)
        grad = jnp.concatenate([grad_ref[rows, h * HD : (h + 1) * HD] for h in range(group)], axis=0)
        spans = key_spans(block)
        raised = [raised_scores(query, keys, span, length) for span in spans]
        total = sum(jnp.sum(r, axis=-1, keepdims=True) for r in raised)
        fix = 1.0 / total
        chances = [r * fix for r in raised]
        d_chances = [mm(grad, values[s[0] : s[1]], NT) for s in spans]
        inner = sum(jnp.sum(c * d, axis=-1, keepdims=True) for c, d in zip(chances, d_chances, strict=True))
        d_query = 0.0
        for span, chance, d_chance in zip(spans, chances, d_chances, strict=True):
            d_score = (chance * (d_chance - inner) * (HD**-0.5)).astype(BF)
            part = slice(span[0], span[1])
            d_query = d_query + mm(d_score, keys[part])
            dk_ref[part, :] += mm(d_score, query, TN)
            dv_ref[part, :] += mm(chance.astype(BF), grad, TN)
        for h in range(group):
            cols = slice(h * HD, (h + 1) * HD)
            d_raw, d_gain = turn_back(
                d_query[h * ROWS : (h + 1) * ROWS], qkv_ref[rows, cols], gain_ref[0:1], cosine[rows], sine[rows]
            )
            out_ref[rows, cols] = d_raw.astype(BF)
            q_gain = q_gain + d_gain
    width = group * HD
    d_raw, k_gain = turn_back(dk_ref[...], raw_keys, gain_ref[1:2], cosine, sine)
    out_ref[:, width : width + HD] = d_raw.astype(BF)
    out_ref[:, width + HD : width + 2 * HD] = dv_ref[...].astype(BF)

    @pl.when(pl.program_id(0) == 0)
    def _():
        gain_out[...] = jnp.zeros_like(gain_out)

    gain_out[0:1, :] += q_gain
    gain_out[1:2, :] += k_gain


def attend(order, own, other, weights, cosine, sine, gains, heads, group):
    half, width = own.shape
    cap, cols = 2 * half, (group + 2) * HD
    return order.call(
        functools.partial(attend_kernel, group),
        (heads,),
        [
            held((half, width)),
            held((half, width)),
            pl.BlockSpec((width, cols), lambda n, s: (0, n)),
            held((cap, HD)),
            held((cap, HD)),
            held((2, HD)),
        ],
        [
            (pl.BlockSpec((cap, cols), lambda n, s: (0, n)), shaped((cap, heads * cols), F32)),
            (pl.BlockSpec((cap, group * HD), lambda n, s: (0, n)), shaped((cap, heads * group * HD), BF)),
        ],
        (own, other, weights, cosine, sine, gains),
        work=24,
        name="attend",
    )


def attend_back(order, qkv, own, other, cosine, sine, gains, span, group, after=(), through=()):
    half, cap, cols = own.shape[0], 2 * own.shape[0], (group + 2) * HD
    first, heads = span
    rows = pl.BlockSpec((half, group * HD), lambda n, s: (0, n))
    return order.call(
        functools.partial(attend_back_kernel, group),
        (heads,),
        [
            pl.BlockSpec((cap, cols), lambda n, s: (0, first + n)),
            rows,
            rows,
            held((cap, HD)),
            held((cap, HD)),
            held((2, HD)),
        ],
        [
            (pl.BlockSpec((cap, cols), lambda n, s: (0, n)), shaped((cap, heads * cols), BF)),
            (pl.BlockSpec((8, HD), lambda n, s: (0, 0)), shaped((8, HD), F32)),
        ],
        (qkv, own, other, cosine, sine, gains),
        after=after,
        through=through,
        scratch=[pltpu.VMEM((cap, group * HD), BF), pltpu.VMEM((cap, HD), F32), pltpu.VMEM((cap, HD), F32)],
        work=17,
        name="attend_back",
    )


def project_kernel(count, place_ref, *refs):
    for out_ref, at in ((refs[-2], 0), (refs[-1], refs[-2].shape[1])):
        cols = slice(at, at + out_ref.shape[1])
        out_ref[...] = sum(mm(refs[i][...], refs[count + i][:, cols]) for i in range(count)).astype(BF)


def project(order, rows, weights, cols, through=()):
    half, depth = rows.shape[0], weights[0][0].shape[0]
    left = [pl.BlockSpec((half, depth), functools.partial(lambda at, j, s: (0, s[at]), at)) for _, _, at in weights]
    right = [pl.BlockSpec((depth, cols), functools.partial(lambda at, j, s: (0, at), at)) for _, at, _ in weights]
    out = pl.BlockSpec((half, cols // 2), lambda j, s: (0, 0))
    return order.call(
        functools.partial(project_kernel, len(weights)),
        (1,),
        left + right,
        [(out, shaped((half, cols // 2), BF))] * 2,
        (*[rows] * len(weights), *[w for w, _, _ in weights]),
        through=through,
        work=5,
        name="project",
    )


WIDE = 3 * TILE
PAIR = 2 * TILE


def swiglu_kernel(place_ref, second_own, second_other, back_own, back_other, weight_ref, out_ref):
    half = second_own.shape[0]
    for at, second_ref, back_ref in ((0, second_own, back_own), (half, second_other, back_other)):
        rows = slice(at, at + half)
        pair = mm(second_ref[...], weight_ref[:, :PAIR])
        d_hidden = mm(back_ref[...], weight_ref[:, PAIR:])
        gate, up = pair[:, :TILE], pair[:, TILE:]
        sigmoid = 1.0 / (1.0 + jnp.exp(-gate))
        silu = gate * sigmoid
        d_gate = d_hidden * up * (sigmoid * (1.0 + gate * (1.0 - sigmoid)))
        out_ref[rows, :TILE] = d_gate.astype(BF)
        out_ref[rows, TILE:PAIR] = (d_hidden * silu).astype(BF)
        out_ref[rows, PAIR:] = (silu * up).astype(BF)


def swiglu(order, second, back, weights, first_tile, tiles, after=(), through=()):
    half, width = second[0].shape
    rows = held((half, width))
    return order.call(
        swiglu_kernel,
        (tiles,),
        [rows, rows, rows, rows, pl.BlockSpec((width, WIDE), lambda j, s: (0, first_tile + j))],
        [(pl.BlockSpec((2 * half, WIDE), lambda j, s: (0, j)), shaped((2 * half, tiles * WIDE), BF))],
        (*second, *back, weights),
        after=after,
        through=through,
        work=5 * tiles,
        name="swiglu",
    )


def turn_columns_kernel(which, place_ref, own_keep, other_keep, own_send, other_send, keep_ref, send_ref):
    half = own_keep.shape[0]
    if which is None:
        own_at, other_at = slice(0, half), slice(half, 2 * half)
    else:
        own_at = pl.ds(pl.multiple_of(place_ref[which] * half, half), half)
        other_at = pl.ds(pl.multiple_of((1 - place_ref[which]) * half, half), half)
    keep_ref[:, own_at] = own_keep[...].T
    keep_ref[:, other_at] = other_keep[...].T
    send_ref[:, own_at] = own_send[...].T
    send_ref[:, other_at] = other_send[...].T


def turn_columns(order, own, other, which, axes, after=()):
    half = own.shape[0]
    owned = own.shape[1] // 16
    y, c = lax.axis_index(axes[1]), lax.axis_index(axes[2])
    at = lambda j, mine: (j % 4) * 4 + jnp.where(j < 4, 1 - y, y) * 2 + jnp.where(mine, c, 1 - c)
    lines = jnp.arange(8, dtype=jnp.int32)
    table = jnp.concatenate([at(lines, True), at(lines, False)]).astype(jnp.int32)
    scalars = jnp.concatenate([order.scalars, table])
    base = order.scalars.shape[0]
    keep = pl.BlockSpec((half, owned), lambda j, s: (0, s[base + j]))
    send = pl.BlockSpec((half, owned), lambda j, s: (0, s[base + 8 + j]))
    out = pl.BlockSpec((owned, 2 * half), lambda j, s: (j, 0))
    held_back, order.scalars = order.scalars, scalars
    keep_cols, send_cols = order.call(
        functools.partial(turn_columns_kernel, which),
        (8,),
        [keep, keep, send, send],
        [(out, shaped((8 * owned, 2 * half), BF))] * 2,
        (own, other, own, other),
        after=after,
        work=7,
        name="turn_columns",
    )
    order.scalars = order.scalars[:base]
    return keep_cols, send_cols


def weight_grad_kernel(splits, place_ref, *refs):
    lefts, (own_ref, other_ref, *outs) = refs[: 2 * len(splits)], refs[2 * len(splits) :]
    half = lefts[0].shape[0] // 2
    for i, (first, last) in enumerate(splits):
        cols = slice(first, last)
        product = mm(lefts[2 * i][...], own_ref[:, cols]) + mm(lefts[2 * i + 1][...], other_ref[:, cols])
        if len(outs) == 2:
            outs[0][:, cols] = product[:half].astype(BF)
            outs[1][:, cols] = product[half:].astype(BF)
            continue
        for line in range(4):
            at, owned = line * half // 2, half // 4
            outs[0][at : at + owned, cols] = product[line * owned : (line + 1) * owned].astype(BF)
            outs[0][at + owned : at + 2 * owned, cols] = product[half + line * owned : half + (line + 1) * owned].astype(BF)


def weight_grad(order, lefts, splits, own, other, step, by_line=False, after=(), through=()):
    rows, cap = lefts[0][0].shape
    cols = own.shape[1]
    right = pl.BlockSpec((cap, step), lambda j, s: (0, j))
    outs = [(pl.BlockSpec((rows // 2, step), lambda j, s: (0, j)), shaped((rows // 2, cols), BF))] * 2
    if by_line:
        outs = [(pl.BlockSpec((rows, step), lambda j, s: (0, j)), shaped((rows, cols), BF))]
    return order.call(
        functools.partial(weight_grad_kernel, splits),
        (cols // step,),
        [held((rows, cap))] * (2 * len(lefts)) + [right, right],
        outs,
        (*[part for pair in lefts for part in pair], own, other),
        after=after,
        through=through,
        work=cols // 160,
        name="weight_grad",
    )


def contract_kernel(count, ranges, adds, place_ref, *refs):
    outs = refs[2 * count + adds :]
    for out_ref, spans in zip(outs, ranges, strict=True):
        total = 0.0
        for i in range(count):
            for first, last in spans:
                total = total + mm(refs[i][:, first:last], refs[count + i][:, first:last], NT)
        for i in range(adds):
            total = total + refs[2 * count + i][...].astype(F32)
        out_ref[...] = total.astype(out_ref.dtype)


def contract(order, which, lefts, weights, ranges, dtypes, adds=(), after=()):
    half, step = lefts[0].shape[0] // 2, 256
    width = weights[0][0].shape[0]
    ins = [pl.BlockSpec((half, a.shape[1]), lambda j, s: (s[which], 0), pipeline_mode=pl.Buffered(1)) for a in lefts]
    ins += [
        pl.BlockSpec((step, a.shape[1]), functools.partial(lambda block, j, s: (j, block), block))
        for a, (_, block) in zip(lefts, weights, strict=True)
    ]
    across = pl.BlockSpec((half, step), lambda j, s: (0, j))
    ins += [across] * len(adds)
    return order.call(
        functools.partial(contract_kernel, len(lefts), ranges, len(adds)),
        (width // step,),
        ins,
        [(across, shaped((half, width), t)) for t in dtypes],
        (*lefts, *[w for w, _ in weights], *adds),
        after=after,
        work=sum(a.shape[1] for a in lefts) // 400,
        name="contract",
    )


LINES = 128


def lines_spec(width):
    return pl.BlockSpec((LINES, width), lambda j, s: (j, 0))


def middle_kernel(place_ref, tokens_ref, own_ref, sent_ref, gain_ref, middle_ref, second_ref):
    middle = tokens_ref[...].astype(F32) + own_ref[...] + sent_ref[...].astype(F32)
    middle_ref[...] = middle
    second_ref[...] = (middle * rms_parts(middle) * gain_ref[1:2, :]).astype(BF)


def middle_rows(order, tokens, own, sent, gains, after=()):
    rows, width = tokens.shape
    spec = lines_spec(width)
    return order.call(
        middle_kernel,
        (rows // LINES,),
        [spec, spec, spec, held((2, width))],
        [(spec, shaped((rows, width), F32)), (spec, shaped((rows, width), BF))],
        (tokens, own, sent, gains),
        after=after,
        work=6,
        name="middle_rows",
    )


def norm_back_kernel(which, place_ref, own_ref, sent_ref, value_ref, extra_ref, gain_ref, *outs):
    grad = own_ref[...] + sent_ref[...].astype(F32)
    values = value_ref[...].astype(F32)
    scale = rms_parts(values)
    hat = values * scale
    d_hat = grad * gain_ref[which : which + 1, :]
    inner = jnp.mean(d_hat * hat, axis=-1, keepdims=True)
    total = extra_ref[...].astype(F32) + scale * (d_hat - hat * inner)
    outs[0][...] = total
    for out in outs[1:-1]:
        out[...] = total.astype(BF)

    @pl.when(pl.program_id(0) == 0)
    def _():
        outs[-1][...] = jnp.zeros_like(outs[-1])

    outs[-1][0:1, :] += jnp.sum(grad * hat, axis=0, keepdims=True)


def norm_back(order, which, own, sent, values, extra, gains, low):
    rows, width = own.shape
    spec = lines_spec(width)
    outs = [(spec, shaped((rows, width), F32))]
    outs += [(spec, shaped((rows, width), BF))] * low
    outs.append((pl.BlockSpec((8, width), lambda j, s: (0, 0)), shaped((8, width), F32)))
    return order.call(
        functools.partial(norm_back_kernel, which),
        (rows // LINES,),
        [spec, spec, spec, spec, held((2, width))],
        outs,
        (own, sent, values, extra, gains),
        work=8,
        name="norm_back",
    )


def add_kernel(place_ref, *refs):
    at = 0
    for i in range(len(refs) // 2):
        a, b = refs[2 * i], refs[2 * i + 1]
        refs[-1][:, at : at + a.shape[1]] = (a[...].astype(F32) + b[...].astype(F32)).astype(BF)
        at += a.shape[1]


def add_pairs(order, pairs, skip=0):
    rows = pairs[0][1].shape[0]
    lines = min(LINES, rows)
    flat = [part for pair in pairs for part in pair]
    width = sum(a.shape[1] for a, _ in pairs)
    spec = lambda width, skip: pl.BlockSpec((lines, width), lambda j, s: (j + skip, 0))
    return order.call(
        add_kernel,
        (rows // lines,),
        [spec(a.shape[1], skip * (i == 0)) for pair in pairs for i, a in enumerate(pair)],
        [(spec(width, 0), shaped((rows, width), BF))],
        flat,
        work=5,
        name="add_pairs",
    )[0]


def take_kernel(place_ref, from_ref, out_ref):
    out_ref[...] = from_ref[...]


def take_rows(order, array):
    rows, width = array.shape
    block = pl.BlockSpec((rows // 2, width), lambda j, s: (0, 0))
    return order.call(
        take_kernel, (1,), [block], [(block, shaped((rows // 2, width), array.dtype))], [array], work=2, name="take_rows"
    )[0]


def beside_kernel(place_ref, *refs):
    at = 0
    for ref in refs[:-1]:
        refs[-1][:, at : at + ref.shape[1]] = ref[...]
        at += ref.shape[1]


def beside(order, arrays):
    rows, width = arrays[0].shape[0], sum(a.shape[1] for a in arrays)
    whole = [pl.BlockSpec(a.shape, lambda j, s: (0, 0)) for a in arrays]
    out = (pl.BlockSpec((rows, width), lambda j, s: (0, 0)), shaped((rows, width), arrays[0].dtype))
    return order.call(beside_kernel, (1,), whole, [out], arrays, work=2, name="beside")


def adam_kernel(rates, place_ref, *refs):
    pair, down, sums, pair_out, down_out = refs[0:3], refs[3:6], refs[6], refs[7:10], refs[10:13]
    for i in range(2):
        new = adam_step(*[r[:, i, :] for r in pair], sums[:, i * TILE : (i + 1) * TILE].astype(F32), rates[0], WEIGHT_DECAY)
        for out, value in zip(pair_out, new, strict=True):
            out[:, i, :] = value
    new = adam_step(*[r[...] for r in down], sums[:, PAIR:].astype(F32).T, rates[1], WEIGHT_DECAY)
    for out, value in zip(down_out, new, strict=True):
        out[...] = value


def adam_mlp(order, pair, down, sums, rates):
    shard, _, units = pair[0].shape
    wide = pl.BlockSpec((shard, 2, TILE), lambda j, s: (0, 0, j))
    tall = pl.BlockSpec((TILE, shard), lambda j, s: (j, 0))
    return order.call(
        functools.partial(adam_kernel, rates),
        (units // TILE,),
        [wide] * 3 + [tall] * 3 + [pl.BlockSpec((shard, WIDE), lambda j, s: (0, j))],
        [(wide, shaped(pair[0].shape, F32))] * 3 + [(tall, shaped(down[0].shape, F32))] * 3,
        (*pair, *down, sums),
        work=20,
        name="adam_mlp",
    )


def rms_parts(values):
    return lax.rsqrt(jnp.mean(values * values, axis=-1, keepdims=True) + EPS_NORM)


def rope_tables(row_count):
    places = jnp.arange(row_count).astype(F32)
    inverse_freq = ROPE_BASE ** (-(jnp.arange(HD // 2).astype(F32) * 2.0) / HD)
    angles = places[:, None] * inverse_freq[None, :]
    sine = jnp.sin(angles)
    cosine = jnp.cos(angles)
    return jnp.concatenate([cosine, cosine], axis=1), jnp.concatenate([-sine, sine], axis=1)


def adam_step(weight, mean_old, square, gradient, step_rate, decay_rate):
    new_mean = BETA_ONE * mean_old + (1.0 - BETA_ONE) * gradient
    new_square = BETA_TWO * square + (1.0 - BETA_TWO) * gradient * gradient
    fix_one = 1.0 - BETA_ONE**STEP
    fix_two = 1.0 - BETA_TWO**STEP
    update = new_mean / fix_one / (jnp.sqrt(new_square / fix_two) + ADAM_EPS)
    return (weight - step_rate * (update + decay_rate * weight), new_mean, new_square)


class Summer:
    def __init__(self, axes, order, side):
        self.axes, self.order, self.side = axes, order, side
        self.lines = len(axes) == 3

    def other_core(self, piece):
        return lax.ppermute(piece, self.axes[2], [(0, 1), (1, 0)]) if self.lines else None

    def columns(self, own, other, in_order, after=()):
        if not self.lines:
            if not in_order:
                return jnp.concatenate([own, other], axis=0)
            first = self.side == 0
            return jnp.concatenate([jnp.where(first, own, other), jnp.where(first, other, own)], axis=0)
        keep, send = turn_columns(self.order, own, other, SIDE if in_order else None, self.axes, after)
        return keep, self.other_core(send)

    def grad(self, lefts, splits, right, from_core, step, after=(), through=()):
        if not self.lines:
            tiled = right.reshape(right.shape[0], -1, step)
            parts = [
                mm(left, tiled[:, :, first:last].reshape(right.shape[0], -1), TN).reshape(left.shape[1], -1, last - first)
                for left, (first, last) in zip(lefts, splits, strict=True)
            ]
            return jnp.concatenate(parts, axis=2).reshape(lefts[0].shape[1], -1).astype(BF), *through
        near, keep, *handed = weight_grad(self.order, lefts, splits, right, from_core, step, after=after, through=through)
        return keep, lax.ppermute(near, self.axes[1], [(0, 1), (1, 0)]), *handed

    def grad_by_line(self, lefts, splits, right, from_core, step, after=(), through=()):
        if not self.lines:
            first, *handed = self.grad(lefts, splits, right, from_core, step, after, through)
            return self.finish((first,)), *handed
        whole, *handed = weight_grad(self.order, lefts, splits, right, from_core, step, True, after, through)
        return lax.psum_scatter(whole, self.axes[0], scatter_dimension=0, tiled=True), *handed

    def trade_by_line(self, summed):
        if not self.lines:
            return None
        return lax.ppermute(take_rows(self.order, summed), self.axes[1], [(0, 1), (1, 0)])

    def finish_by_line(self, summed, got):
        return add_pairs(self.order, [(summed, got)], 1) if self.lines else summed

    def finish(self, *grads):
        if not self.lines:
            return lax.psum_scatter(jnp.concatenate([g for g, in grads], axis=1), self.axes, scatter_dimension=0, tiled=True)
        line = add_pairs(self.order, grads)
        return lax.psum_scatter(line, self.axes[0], scatter_dimension=0, tiled=True)

    def everywhere(self, values):
        if not self.lines:
            return lax.psum(values, (*self.axes, "tensor"))
        pair = [(0, 1), (1, 0)]
        steps = [(self.axes[2], pair), ("tensor", pair), (self.axes[1], pair)]
        steps += [(self.axes[0], [(0, 1), (1, 0), (2, 3), (3, 2)]), (self.axes[0], [(0, 2), (2, 0), (1, 3), (3, 1)])]
        for axis, pairs in steps:
            values = values + lax.ppermute(values, axis, pairs)
        return values


def on_device(
    axes,
    tokens,
    cotangent,
    lengths,
    w_query,
    query_mean,
    query_square,
    w_keyval,
    keyval_mean,
    keyval_square,
    w_out,
    out_mean,
    out_square,
    w_gateup,
    gateup_mean,
    gateup_square,
    w_down,
    down_mean,
    down_square,
    norm_gains,
    norm_mean,
    norm_square,
    head_gains,
    head_mean,
    head_square,
):
    side = lax.axis_index("tensor")
    tok_rows = tokens.shape[0]
    cap = 2 * tok_rows
    length = lengths[0]
    order = Order(side, length, lax.axis_index(axes[2]) if len(axes) == 3 else jnp.zeros_like(side))
    summer = Summer(axes, order, side)

    def swap(piece):
        return lax.ppermute(piece, "tensor", [(0, 1), (1, 0)])

    def there(*arrays):
        return [v for v in arrays if v is not None]

    def gather(shard):
        return lax.all_gather(shard, axes, axis=0, tiled=True)

    shard = w_query.shape[0]
    heads = w_keyval.shape[2] // HD
    group = w_query.shape[1] // HD // heads
    units = w_gateup.shape[2]
    tiles = units // TILE
    part = tiles // CHUNKS
    kv_low = w_keyval.astype(BF).reshape(shard, 2, heads, HD)
    qkv_shard = jnp.concatenate(
        [w_query.astype(BF).reshape(shard, heads, group * HD), kv_low[:, 0], kv_low[:, 1]], axis=2
    ).reshape(shard, heads * (group + 2) * HD)
    out_shard = w_out.astype(BF).T
    pair_low = w_gateup.astype(BF).reshape(shard, 2, tiles, TILE)
    down_low = w_down.astype(BF).T.reshape(shard, tiles, TILE)
    mlp_shard = jnp.concatenate([pair_low[:, 0], pair_low[:, 1], down_low], axis=2).reshape(shard, tiles * WIDE)

    stream = tokens.astype(F32)
    normed_own = (stream * rms_parts(stream) * norm_gains[0]).astype(BF)
    normed_other = swap(normed_own)
    qkv_cols, out_cols = qkv_shard.shape[1], out_shard.shape[1]
    early = gather(jnp.concatenate([qkv_shard, out_shard], axis=1))
    most = gather(mlp_shard[:, : (CHUNKS - 1) * part * WIDE])
    late = gather(mlp_shard[:, (CHUNKS - 1) * part * WIDE :])
    parts = [(most, part * p) for p in range(CHUNKS - 1)] + [(late, 0)]

    own_places = side * tok_rows + jnp.arange(tok_rows)
    live = (own_places < length)[:, None]
    back_own = jnp.where(live, cotangent, jnp.zeros_like(cotangent))
    back_other = swap(back_own)
    cosine, sine = rope_tables(cap)

    def there(*arrays):
        return [v for v in arrays if v is not None]

    normed_cols = summer.columns(normed_own, normed_other, True)

    qkv, attended = attend(order, normed_own, normed_other, early, cosine, sine, head_gains, heads, group)
    attended_core = summer.other_core(attended)
    out_block = [(early, qkv_cols // out_cols)]
    whole_out = [[(0, out_cols)]]
    attended_sent = swap(contract(order, OTHER_SIDE, [attended], out_block, whole_out, [BF])[0])
    back_cols = summer.columns(back_own, back_other, False)
    (attended_here,) = contract(
        order, SIDE, [attended], out_block, whole_out, [F32], after=there(normed_cols[1], attended_core)
    )
    middle, second_own = middle_rows(order, tokens, attended_here, attended_sent, norm_gains)

    second = (second_own, swap(second_own))
    back = (back_own, back_other)
    pair_spans = [(t * WIDE, t * WIDE + PAIR) for t in range(part)]
    down_spans = [(t * WIDE + PAIR, (t + 1) * WIDE) for t in range(part)]
    blocks = [(w, at // part) for w, at in parts]

    def mlp(p, after=(), through=()):
        piece, *handed = swiglu(order, second, back, parts[p][0], parts[p][1], part, after, through)
        return (piece, summer.other_core(piece)), *handed

    def mlp_grad(p, after=(), through=()):
        return summer.grad([second_cols, back_cols], [(0, PAIR), (PAIR, WIDE)], *mlp_pieces[p], WIDE, after, through)

    out_rows = early.shape[0] // 2
    core = order.scalars[CORE]
    out_half = lax.dynamic_slice(early, (core * out_rows, qkv_cols), (out_rows, out_cols))

    second_cols = summer.columns(*second, False)
    mlp_pieces = [*mlp(0, there(back_cols[1])), *mlp(1)]
    splits = [(0, PAIR), (PAIR, WIDE)]
    first_sum, out_half = summer.grad_by_line([second_cols, back_cols], splits, *mlp_pieces[0], WIDE, through=[out_half])
    out_got = swap(out_half)
    pieces = [piece for piece, _ in mlp_pieces]
    (d_second_part,) = contract(order, SECOND, pieces, blocks[:2], [pair_spans], [BF])
    mlp_grads = [mlp_grad(1)]
    mlp_pieces += mlp(2, [out_got])
    pieces = [piece for piece, _ in mlp_pieces]
    d_second_sent = swap(contract(order, SECOND, pieces[2:], blocks[2:], [pair_spans], [BF], [d_second_part])[0])
    if summer.lines:
        out_other = [(out_got, 0, CORE), (summer.other_core(out_got), 0, OTHER_CORE)]
    else:
        out_other = [(swap(early[:, qkv_cols:]), 0, FIRST)]
    mlp_grads.append(mlp_grad(2))
    (d_second,) = contract(order, FIRST, pieces, blocks, [pair_spans], [F32])
    d_middle, branch_own, branch_again, g_second_gain = norm_back(
        order, 1, d_second, d_second_sent, middle, back_own, norm_gains, 2
    )

    there_a, there_b = project(order, branch_own, out_other, out_cols)
    sent_a, sent_b = swap(there_a), swap(there_b)
    mlp_sums = [summer.finish(mlp_grads[0])]
    here_a, here_b, branch_again = project(
        order, branch_own, [(early, qkv_cols // out_cols, FIRST)], out_cols, [branch_again]
    )
    branch_other = swap(branch_again)

    def attention_back(half, here, sent, after=(), through=()):
        span = (half * heads // 2, heads // 2)
        d_part, g_part, *handed = attend_back(
            order, qkv, here, sent, cosine, sine, head_gains, span, group, after, through
        )
        return d_part, summer.other_core(d_part), g_part[:2], *handed

    d_qkv_a, core_a, g_head_a = attention_back(0, here_a, sent_a)
    d_qkv_b, core_b, g_head_b = attention_back(1, here_b, sent_b)
    (out_there,) = contract(order, SECOND, pieces, blocks, [down_spans], [BF])
    out_sent = swap(out_there)
    branch_cols = summer.columns(branch_again, branch_other, True)
    mlp_sums.append(summer.finish(mlp_grads[1]))
    first_got = summer.trade_by_line(first_sum)
    qkv_grad_a = summer.grad([normed_cols], [(0, 512)], d_qkv_a, core_a, 512)
    qkv_grad_b = summer.grad([normed_cols], [(0, 512)], d_qkv_b, core_b, 512)
    out_grad = summer.grad([branch_cols], [(0, 512)], attended, attended_core, 512)
    d_qkv = [d_qkv_a, d_qkv_b]
    qkv_blocks = [(early, 0), (early, 1)]
    whole_qkv = [[(0, qkv_cols // 2)]]
    d_first_sent = swap(contract(order, OTHER_SIDE, d_qkv, qkv_blocks, whole_qkv, [BF])[0])
    qkv_sum_a = summer.finish(qkv_grad_a)
    (d_first,) = contract(order, SIDE, d_qkv, qkv_blocks, whole_qkv, [F32], after=mlp_sums[:1])
    (layer_out,) = contract(order, FIRST, pieces, blocks, [down_spans], [F32], [middle, out_sent])
    last_sum = summer.finish(qkv_grad_b, out_grad)
    mlp_sums.insert(0, summer.finish_by_line(first_sum, first_got))
    tokens_grad, g_first_gain = norm_back(order, 0, d_first, d_first_sent, tokens, d_middle, norm_gains, 0)
    wide_rate = RATE_SCALE * D ** (-0.5)
    mlp_new = adam_mlp(
        order,
        (w_gateup, gateup_mean, gateup_square),
        (w_down, down_mean, down_square),
        jnp.concatenate(mlp_sums, axis=1),
        (wide_rate, RATE_SCALE * FF ** (-0.5)),
    )
    (qkv_sum,) = beside(order, [qkv_sum_a, last_sum[:, : qkv_cols // 2]])
    out_sum = last_sum[:, qkv_cols // 2 :]
    g_head = g_head_a + g_head_b

    out_sum = out_sum.astype(F32).T
    qkv_sum = qkv_sum.astype(F32).reshape(shard, heads, (group + 2) * HD)
    query_sum = qkv_sum[:, :, : group * HD].reshape(shard, heads * group * HD)
    keyval_sum = jnp.stack(
        [
            qkv_sum[:, :, group * HD : (group + 1) * HD].reshape(shard, heads * HD),
            qkv_sum[:, :, (group + 1) * HD :].reshape(shard, heads * HD),
        ],
        axis=1,
    )
    gains_here = jnp.concatenate([g_first_gain[0], g_second_gain[0], g_head.reshape(-1)]).reshape(-1, HD)
    gain_sums = summer.everywhere(gains_here).reshape(-1)
    norm_sum = gain_sums[: 2 * D].reshape(2, D)
    head_sum = gain_sums[2 * D :].reshape(2, HD)

    query_new = adam_step(w_query, query_mean, query_square, query_sum, wide_rate, WEIGHT_DECAY)
    keyval_new = adam_step(w_keyval, keyval_mean, keyval_square, keyval_sum, wide_rate, WEIGHT_DECAY)
    out_new = adam_step(w_out, out_mean, out_square, out_sum, RATE_SCALE * OUT_FAN ** (-0.5), WEIGHT_DECAY)
    norm_new = adam_step(norm_gains, norm_mean, norm_square, norm_sum, GAIN_RATE, 0.0)
    head_new = adam_step(head_gains, head_mean, head_square, head_sum, GAIN_RATE, 0.0)
    return (layer_out, tokens_grad, *query_new, *keyval_new, *out_new, *mlp_new, *norm_new, *head_new)


def solution(mesh):
    count, sides = mesh.shape["dp"], mesh.shape["tensor"]
    if count == 16:
        axes = ("z", "y", "core")
        grid = Mesh(mesh.devices.reshape(4, 2, 2, sides), (*axes, "tensor"))
    else:
        axes, grid = ("dp",), mesh
    rows = P((*axes, "tensor"), None)
    in_out = [P(axes, "tensor")] * 3 + [P(axes, None, "tensor")] * 3 + [P("tensor", axes)] * 3
    in_out += [P(axes, None, "tensor")] * 3 + [P("tensor", axes)] * 3 + [P()] * 6
    return jax.shard_map(
        functools.partial(on_device, axes),
        mesh=grid,
        in_specs=(rows, rows, P(axes), *in_out),
        out_specs=(rows, rows, *in_out),
        check_vma=False,
    )
```

time: 2440 us -> 804 us (0.33)
  waiting for transfers between devices: 1750 us -> 224 us
  Pallas kernels: 0 us -> 434 us
  matrix products: 430 us -> 0 us
  other arithmetic: 114 us -> 22 us
  blocking collectives: 39.6 us -> 0 us
  starting transfers between devices: 0.75 us -> 27.8 us
    reduce_scatter x9 -> x5, waiting for transfers between devices: 1230 us -> 0.05 us  [the longest x4 0.05 us: finish(): return lax.psum_scatter(line, self.axes[0], scatter_dimension=0, tiled=True)]
    all_gather x9 -> x3, waiting for transfers between devices: 518 us -> 31.8 us  [gather(): return lax.all_gather(shard, axes, axis=0, tiled=True)]
    pallas_call x0 -> x38, Pallas kernels: none -> 434 us  [call(): pl.pallas_call(run, grid_spec=pltpu.PrefetchScalarGridSpec(num_scalar_pre...]
    dot_general x29 -> x0, matrix products: 430 us -> none  [the longest x2 48.3 us: attend_back(): jnp.einsum('ngts,tngh->snh', d_scores, query_blk, preferred_element_type=...]
    ppermute x0 -> x33, waiting for transfers between devices: none -> 192 us  [the longest x11 153 us: swap(): return lax.ppermute(piece, 'tensor', [(0, 1), (1, 0)])]
    psum x1 -> x0, blocking collectives: 39.6 us -> none  [on_device(): lax.psum((jnp.stack([g_first_gain, g_second_gain]), g_head), ('dp', 'tens...]
    unnamed x164 -> x169, local copies, waits for them, and re-layouts: 34.3 us -> 64.2 us
    reduce_sum x9 -> x1, other arithmetic: 28 us -> 0.48 us  [rms_parts(): jnp.mean(values * values, axis=-1, keepdims=True) + EPS_NORM]
  transfers between devices with their start and end apart: 18 -> 41, of which waited for: 16 -> 14; matrix products, arithmetic and copies ran while one was open for 12% -> 4% of each run, Pallas kernels for 0% -> 54%
where the time goes in v1:
time: 804 us; the launch traced here: 796 us
  Pallas kernels  434 us (54%)
  waiting for transfers between devices  224 us (28%)
  local copies, waits for them, and re-layouts  71.4 us (9%)
  starting transfers between devices  27.8 us (3%)
  other arithmetic  22 us (3%)
  between operations  17 us (2%)
    pallas_call x38, Pallas kernels, call(): pl.pallas_call(run, grid_spec=pltpu.PrefetchScalarGridSpec(num_scalar_pre...  434 us
    ppermute x11, waiting for transfers between devices, swap(): return lax.ppermute(piece, 'tensor', [(0, 1), (1, 0)])  153 us
    unnamed x169, local copies, waits for them, and re-layouts  64.2 us
    all_gather x3, waiting for transfers between devices, gather(): return lax.all_gather(shard, axes, axis=0, tiled=True)  31.8 us
    ppermute x1, waiting for transfers between devices, trade_by_line(): lax.ppermute(take_rows(self.order, summed), self.axes[1], [(0, 1), (1, 0)])  18.1 us
  transfers between devices with their start and end apart: 41, of which 14 were waited for; matrix products, arithmetic and copies ran while one was open for 4% of the time, Pallas kernels for 54%

profile of v1, /device:TPU:0, one launch (start us, length us, event | category | flops | bytes accessed | tf_op | source)
XLA Modules:
  0.0 795.6 jit_solution(13517311486743242732)
XLA Ops:
  34.0 40.6 %collective-permute-done.refs_1_.refs_3_ = bf16[512,2048]{1,0:T(8,128)(2,1)} collective-permute-done((bf16[512,2048]{1,0:T(8,128)(2,1)}, bf16[512,2048]{1,0:T(8,128)(2,1)}, u32[]{:S(2)}, u32[]{:S(2)}) %collective-permute-start) | collective-permute-done | bytes 2097184 | tf_op jit(solution)/shard_map/ppermute | solution.py:707
  83.6 31.8 %all-gather.4.cloned.1.call-done.refs_2_.refs_1_.refs_3_ = bf16[2048,3072]{1,0:T(8,128)(2,1)} async-done(((bf16[128,3072]{1,0:T(8,128)(2,1)}), bf16[2048,3072]{1,0:T(8,128)(2,1)}) %all-gather.4.cloned.1.call-update) | async-done | bytes 12582928 | tf_op jit(solution)/shard_map/all_gather | solution.py:713
  115.3 23.9 %attend.1 = (f32[1024,2048]{1,0:T(8,128)}, bf16[1024,1024]{1,0:T(8,128)(2,1)S(1)}, s32[7]{0:T(128)S(1)}) custom-call(s32[7]{0:T(128)S(1)} %bitcast.56, bf16[512,2048]{1,0:T(8,128)(2,1)} %fusion.2.refs_0_.refs_2_, bf16[512,2048]{1,0:T(8,128)(2,1)} %collective-permute-done.refs_1_.refs_3_, ...), custom_call_target="tpu_custom_call" | custom-call | flops 12000000000 | bytes 1 | tf_op jit(solution)/shard_map/attend/pallas_call | solution.py:60
  139.5 8.0 %contract.9 = (bf16[512,2048]{1,0:T(8,128)(2,1)S(1)}, s32[7]{0:T(128)S(1)}) custom-call(s32[7]{0:T(128)S(1)} %get-tuple-element.125.scalars, bf16[1024,1024]{1,0:T(8,128)(2,1)S(1)} %get-tuple-element.126.refs_0_.refs_2_, bf16[2048,3072]{1,0:T(8,128)(2,1)} %all-gather.4.cloned.1.call-done.refs_2_.refs_1_.refs_3_), custom_call_target="tpu_custom_call" | custom-call | flops 1000000000 | bytes 1 | tf_op jit(solution)/shard_map/contract/pallas_call | solution.py:60
  157.3 8.7 %contract.10 = (f32[512,2048]{1,0:T(8,128)}, s32[7]{0:T(128)S(1)}) custom-call(s32[7]{0:T(128)S(1)} %bitcast.55, bf16[1024,1024]{1,0:T(8,128)(2,1)S(1)} %get-tuple-element.126.refs_0_.refs_2_, bf16[2048,3072]{1,0:T(8,128)(2,1)} %all-gather.4.cloned.1.call-done.refs_2_.refs_1_.refs_3_, bf16[1024,1024]{1,0:T(8,128)(2,1)} %collective-permute-done.2.refs_2_.refs_1_, ...), custom_call_target="tpu_custom_call" | custom-call | flops 1000000000 | bytes 1 | tf_op jit(solution)/shard_map/contract/pallas_call | solution.py:60
  166.0 29.6 %collective-permute-done.4.refs_2_ = bf16[512,2048]{1,0:T(8,128)(2,1)} collective-permute-done((bf16[512,2048]{1,0:T(8,128)(2,1)S(1)}, bf16[512,2048]{1,0:T(8,128)(2,1)}, u32[]{:S(2)}, u32[]{:S(2)}) %collective-permute-start.4) | collective-permute-done | bytes 2097184 | tf_op jit(solution)/shard_map/ppermute | solution.py:707
  203.5 45.5 %collective-permute-done.5.refs_1_.refs_3_ = bf16[512,2048]{1,0:T(8,128)(2,1)S(1)} collective-permute-done((bf16[512,2048]{1,0:T(8,128)(2,1)S(1)}, bf16[512,2048]{1,0:T(8,128)(2,1)S(1)}, u32[]{:S(2)}, u32[]{:S(2)}) %collective-permute-start.5) | collective-permute-done | bytes 2097184 | tf_op jit(solution)/shard_map/ppermute | solution.py:707
  262.4 19.1 %swiglu.3 = (bf16[1024,3072]{1,0:T(8,128)(2,1)}, s32[7]{0:T(128)S(1)}) custom-call(s32[7]{0:T(128)S(1)} %bitcast.58, bf16[512,2048]{1,0:T(8,128)(2,1)S(1)} %copy-done.23, bf16[512,2048]{1,0:T(8,128)(2,1)S(1)} %copy-done.26, bf16[512,2048]{1,0:T(8,128)(2,1)} %broadcast_select_fusion.refs_0_.refs_2_.refs_3_, ...), custom_call_target="tpu_custom_call" | custom-call | flops 10000000000 | bytes 1 | tf_op jit(solution)/shard_map/swiglu/pallas_call | solution.py:60
  281.5 19.5 %swiglu.4 = (bf16[1024,3072]{1,0:T(8,128)(2,1)}, s32[7]{0:T(128)S(1)}) custom-call(s32[7]{0:T(128)S(1)} %get-tuple-element.137.scalars, bf16[512,2048]{1,0:T(8,128)(2,1)S(1)} %copy-done.23, bf16[512,2048]{1,0:T(8,128)(2,1)S(1)} %copy-done.26, bf16[512,2048]{1,0:T(8,128)(2,1)} %broadcast_select_fusion.refs_0_.refs_2_.refs_3_, ...), custom_call_target="tpu_custom_call" | custom-call | flops 10000000000 | bytes 1 | tf_op jit(solution)/shard_map/swiglu/pallas_call | solution.py:60
  304.7 10.4 %collective-permute-done.7.refs_1_ = bf16[1024,1024]{1,0:T(8,128)(2,1)} collective-permute-done((bf16[1024,1024]{1,0:T(8,128)(2,1)}, bf16[1024,1024]{1,0:T(8,128)(2,1)}, u32[]{:S(2)}, u32[]{:S(2)}) %collective-permute-start.7) | collective-permute-done | bytes 2097184 | tf_op jit(solution)/shard_map/ppermute | solution.py:618
  315.1 19.5 %weight_grad.6 = (bf16[1024,3072]{1,0:T(8,128)(2,1)}, s32[7]{0:T(128)S(1)}, bf16[1024,1024]{1,0:T(8,128)(2,1)S(1)}) custom-call(s32[7]{0:T(128)S(1)} %get-tuple-element.138.scalars, bf16[1024,1024]{1,0:T(8,128)(2,1)S(1)} %copy-done.47, bf16[1024,1024]{1,0:T(8,128)(2,1)} %collective-permute-done.7.refs_1_, ...), custom_call_target="tpu_custom_call", output_to_operand_aliasing={{2}: (7, {})} | custom-call | flops 9500000256 | bytes 1 | tf_op jit(solution)/shard_map/weight_grad/pallas_call | solution.py:60
  337.5 18.2 %contract.11 = (bf16[512,2048]{1,0:T(8,128)(2,1)S(1)}, s32[7]{0:T(128)S(1)}) custom-call(s32[7]{0:T(128)S(1)} %get-tuple-element.143.scalars, bf16[1024,3072]{1,0:T(8,128)(2,1)} %get-tuple-element.142.refs_4_.refs_0_, bf16[1024,3072]{1,0:T(8,128)(2,1)} %get-tuple-element.144.refs_1_.refs_4_, ...), custom_call_target="tpu_custom_call" | custom-call | flops 7500000256 | bytes 1 | tf_op jit(solution)/shard_map/contract/pallas_call | solution.py:60
  357.0 19.2 %weight_grad.7 = (bf16[512,3072]{1,0:T(8,128)(2,1)}, bf16[512,3072]{1,0:T(8,128)(2,1)}, s32[7]{0:T(128)S(1)}) custom-call(s32[7]{0:T(128)S(1)} %get-tuple-element.145.scalars, bf16[1024,1024]{1,0:T(8,128)(2,1)S(1)} %copy-done.48, bf16[1024,1024]{1,0:T(8,128)(2,1)} %collective-permute-done.7.refs_1_, bf16[1024,1024]{1,0:T(8,128)(2,1)} %copy-done.45, ...), custom_call_target="tpu_custom_call" | custom-call | flops 9500000256 | bytes 1 | tf_op jit(solution)/shard_map/weight_grad/pallas_call | solution.py:60
  376.2 8.1 %collective-permute-done.10.refs_5_.refs_2_ = bf16[1024,1024]{1,0:T(8,128)(2,1)} collective-permute-done((bf16[1024,1024]{1,0:T(8,128)(2,1)}, bf16[1024,1024]{1,0:T(8,128)(2,1)}, u32[]{:S(2)}, u32[]{:S(2)}) %collective-permute-start.10) | collective-permute-done | bytes 2097184 | tf_op jit(solution)/shard_map/ppermute | solution.py:707
  387.5 19.4 %swiglu.5 = (bf16[1024,3072]{1,0:T(8,128)(2,1)}, s32[7]{0:T(128)S(1)}) custom-call(s32[7]{0:T(128)S(1)} %get-tuple-element.146.scalars, bf16[512,2048]{1,0:T(8,128)(2,1)S(1)} %copy-done.24, bf16[512,2048]{1,0:T(8,128)(2,1)S(1)} %copy-done.27, bf16[512,2048]{1,0:T(8,128)(2,1)} %broadcast_select_fusion.refs_0_.refs_2_.refs_3_, ...), custom_call_target="tpu_custom_call" | custom-call | flops 10000000000 | bytes 1 | tf_op jit(solution)/shard_map/swiglu/pallas_call | solution.py:60
  407.5 12.2 %contract.12 = (bf16[512,2048]{1,0:T(8,128)(2,1)S(1)}, s32[7]{0:T(128)S(1)}) custom-call(s32[7]{0:T(128)S(1)} %get-tuple-element.148.scalars, bf16[1024,3072]{1,0:T(8,128)(2,1)} %get-tuple-element.149.refs_0_.refs_4_.refs_2_, bf16[2048,3072]{1,0:T(8,128)(2,1)} %all-gather.8.cloned.1.call-done.refs_4_.refs_1_.refs_5_, bf16[512,2048]{1,0:T(8,128)(2,1)S(1)} %copy-done.14), custom_call_target="tpu_custom_call" | custom-call | flops 3500000000 | bytes 1 | tf_op jit(solution)/shard_map/contract/pallas_call | solution.py:60
  421.2 19.3 %weight_grad.8 = (bf16[512,3072]{1,0:T(8,128)(2,1)}, bf16[512,3072]{1,0:T(8,128)(2,1)}, s32[7]{0:T(128)S(1)}) custom-call(s32[7]{0:T(128)S(1)} %get-tuple-element.151.scalars, bf16[1024,1024]{1,0:T(8,128)(2,1)S(1)} %copy-done.49, bf16[1024,1024]{1,0:T(8,128)(2,1)} %collective-permute-done.7.refs_1_, bf16[1024,1024]{1,0:T(8,128)(2,1)} %copy-done.45, ...), custom_call_target="tpu_custom_call" | custom-call | flops 9500000256 | bytes 1 | tf_op jit(solution)/shard_map/weight_grad/pallas_call | solution.py:60
  440.5 23.6 %contract.13 = (f32[512,2048]{1,0:T(8,128)S(1)}, s32[7]{0:T(128)S(1)}) custom-call(s32[7]{0:T(128)S(1)} %get-tuple-element.152.scalars, bf16[1024,3072]{1,0:T(8,128)(2,1)} %get-tuple-element.142.refs_4_.refs_0_, bf16[1024,3072]{1,0:T(8,128)(2,1)} %get-tuple-element.144.refs_1_.refs_4_, bf16[1024,3072]{1,0:T(8,128)(2,1)} %get-tuple-element.149.refs_0_.refs_4_.refs_2_, ...), custom_call_target="tpu_custom_call" | custom-call | flops 11500000256 | bytes 1 | tf_op jit(solution)/shard_map/contract/pallas_call | solution.py:60
  468.7 9.2 %norm_back.2 = (f32[512,2048]{1,0:T(8,128)}, bf16[512,2048]{1,0:T(8,128)(2,1)S(1)}, bf16[512,2048]{1,0:T(8,128)(2,1)}, f32[8,2048]{1,0:T(8,128)S(1)}, s32[7]{0:T(128)S(1)}) custom-call(s32[7]{0:T(128)S(1)} %get-tuple-element.153.scalars, f32[512,2048]{1,0:T(8,128)} %copy-done.20, bf16[512,2048]{1,0:T(8,128)(2,1)} %copy-done.78, ...), custom_call_target="tpu_custom_call" | custom-call | flops 4000000000 | bytes 1 | tf_op jit(solution)/shard_map/norm_back/pallas_call | solution.py:60
  505.6 16.2 %attend_back.2 = (bf16[1024,1024]{1,0:T(8,128)(2,1)S(1)}, f32[8,128]{1,0:T(8,128)S(1)}, s32[7]{0:T(128)S(1)}) custom-call(s32[7]{0:T(128)S(1)} %get-tuple-element.164.scalars, f32[1024,2048]{1,0:T(8,128)} %get-tuple-element.165.refs_0_, bf16[512,512]{1,0:T(8,128)(2,1)S(1)} %get-tuple-element.166.refs_1_, ...), custom_call_target="tpu_custom_call" | custom-call | flops 8499999744 | bytes 1 | tf_op jit(solution)/shard_map/attend_back/pallas_call | solution.py:60
  523.2 16.5 %attend_back.3 = (bf16[1024,1024]{1,0:T(8,128)(2,1)S(1)}, f32[8,128]{1,0:T(8,128)S(1)}, s32[7]{0:T(128)S(1)}) custom-call(s32[7]{0:T(128)S(1)} %get-tuple-element.168.scalars, f32[1024,2048]{1,0:T(8,128)} %get-tuple-element.165.refs_0_, bf16[512,512]{1,0:T(8,128)(2,1)S(1)} %get-tuple-element.169.refs_1_, ...), custom_call_target="tpu_custom_call" | custom-call | flops 8499999744 | bytes 1 | tf_op jit(solution)/shard_map/attend_back/pallas_call | solution.py:60
  541.0 20.2 %contract.14 = (bf16[512,2048]{1,0:T(8,128)(2,1)S(1)}, s32[7]{0:T(128)S(1)}) custom-call(s32[7]{0:T(128)S(1)} %get-tuple-element.171.scalars, bf16[1024,3072]{1,0:T(8,128)(2,1)} %get-tuple-element.142.refs_4_.refs_0_, bf16[1024,3072]{1,0:T(8,128)(2,1)} %get-tuple-element.144.refs_1_.refs_4_, bf16[1024,3072]{1,0:T(8,128)(2,1)} %get-tuple-element.149.refs_0_.refs_4_.refs_2_, ...), custom_call_target="tpu_custom_call" | custom-call | flops 11500000256 | bytes 1 | tf_op jit(solution)/shard_map/contract/pallas_call | solution.py:60
  586.5 8.5 %weight_grad.9 = (bf16[512,1024]{1,0:T(8,128)(2,1)S(1)}, bf16[512,1024]{1,0:T(8,128)(2,1)S(1)}, s32[7]{0:T(128)S(1)}) custom-call(s32[7]{0:T(128)S(1)} %get-tuple-element.179.scalars, bf16[1024,1024]{1,0:T(8,128)(2,1)S(1)} %copy-done.38, bf16[1024,1024]{1,0:T(8,128)(2,1)} %collective-permute-done.2.refs_2_.refs_1_, bf16[1024,1024]{1,0:T(8,128)(2,1)} %copy-done.1, ...), custom_call_target="tpu_custom_call" | custom-call | flops 3000000000 | bytes 1 | tf_op jit(solution)/shard_map/weight_grad/pallas_call | solution.py:60
  596.6 8.6 %weight_grad.10 = (bf16[512,1024]{1,0:T(8,128)(2,1)}, bf16[512,1024]{1,0:T(8,128)(2,1)S(1)}, s32[7]{0:T(128)S(1)}) custom-call(s32[7]{0:T(128)S(1)} %get-tuple-element.182.scalars, bf16[1024,1024]{1,0:T(8,128)(2,1)S(1)} %copy-done.38, bf16[1024,1024]{1,0:T(8,128)(2,1)} %collective-permute-done.2.refs_2_.refs_1_, bf16[1024,1024]{1,0:T(8,128)(2,1)} %copy-done.4, ...), custom_call_target="tpu_custom_call" | custom-call | flops 3000000000 | bytes 1 | tf_op jit(solution)/shard_map/weight_grad/pallas_call | solution.py:60
  605.7 8.6 %weight_grad.11 = (bf16[512,1024]{1,0:T(8,128)(2,1)}, bf16[512,1024]{1,0:T(8,128)(2,1)S(1)}, s32[7]{0:T(128)S(1)}) custom-call(s32[7]{0:T(128)S(1)} %get-tuple-element.184.scalars, bf16[1024,1024]{1,0:T(8,128)(2,1)S(1)} %copy-done.40, bf16[1024,1024]{1,0:T(8,128)(2,1)} %collective-permute-done.21.refs_1_, bf16[1024,1024]{1,0:T(8,128)(2,1)} %copy-done.6, ...), custom_call_target="tpu_custom_call" | custom-call | flops 3000000000 | bytes 1 | tf_op jit(solution)/shard_map/weight_grad/pallas_call | solution.py:60
  616.9 10.5 %contract.15 = (bf16[512,2048]{1,0:T(8,128)(2,1)S(1)}, s32[7]{0:T(128)S(1)}) custom-call(s32[7]{0:T(128)S(1)} %get-tuple-element.187.scalars, bf16[1024,1024]{1,0:T(8,128)(2,1)S(1)} %copy-done.2, bf16[1024,1024]{1,0:T(8,128)(2,1)} %copy-done.4, bf16[2048,3072]{1,0:T(8,128)(2,1)} %all-gather.4.cloned.1.call-done.refs_2_.refs_1_.refs_3_, ...), custom_call_target="tpu_custom_call" | custom-call | flops 2500000000 | bytes 1 | tf_op jit(solution)/shard_map/contract/pallas_call | solution.py:60
  635.3 10.8 %contract.16 = (f32[512,2048]{1,0:T(8,128)}, s32[7]{0:T(128)S(1)}) custom-call(s32[7]{0:T(128)S(1)} %get-tuple-element.191.scalars, bf16[1024,1024]{1,0:T(8,128)(2,1)S(1)} %copy-done.3, bf16[1024,1024]{1,0:T(8,128)(2,1)S(1)} %copy-done.5, bf16[2048,3072]{1,0:T(8,128)(2,1)} %all-gather.4.cloned.1.call-done.refs_2_.refs_1_.refs_3_, ...), custom_call_target="tpu_custom_call" | custom-call | flops 2500000000 | bytes 1 | tf_op jit(solution)/shard_map/contract/pallas_call | solution.py:60
  646.1 22.0 %contract.17 = (f32[512,2048]{1,0:T(8,128)}, s32[7]{0:T(128)S(1)}) custom-call(s32[7]{0:T(128)S(1)} %get-tuple-element.193.scalars, bf16[1024,3072]{1,0:T(8,128)(2,1)} %get-tuple-element.142.refs_4_.refs_0_, bf16[1024,3072]{1,0:T(8,128)(2,1)} %get-tuple-element.144.refs_1_.refs_4_, bf16[1024,3072]{1,0:T(8,128)(2,1)} %get-tuple-element.149.refs_0_.refs_4_.refs_2_, ...), custom_call_target="tpu_custom_call" | custom-call | flops 11500000256 | bytes 1 | tf_op jit(solution)/shard_map/contract/pallas_call | solution.py:60
  674.4 18.1 %collective-permute-done.26.refs_1_ = bf16[128,3072]{1,0:T(8,128)(2,1)S(1)} collective-permute-done((bf16[128,3072]{1,0:T(8,128)(2,1)S(1)}, bf16[128,3072]{1,0:T(8,128)(2,1)S(1)}, u32[]{:S(2)}, u32[]{:S(2)}) %collective-permute-start.26) | collective-permute-done | bytes 786464 | tf_op jit(solution)/shard_map/ppermute | solution.py:650
  695.1 24.8 %collective-permute-done.27.refs_1_ = bf16[512,2048]{1,0:T(8,128)(2,1)S(1)} collective-permute-done((bf16[512,2048]{1,0:T(8,128)(2,1)}, bf16[512,2048]{1,0:T(8,128)(2,1)S(1)}, u32[]{:S(2)}, u32[]{:S(2)}) %collective-permute-start.27) | collective-permute-done | bytes 2097184 | tf_op jit(solution)/shard_map/ppermute | solution.py:707
  719.9 7.8 norm_back.3
  751.5 19.4 %adam_mlp.1 = (f32[128,2,3072]{2,1,0:T(2,128)}, f32[128,2,3072]{2,1,0:T(2,128)}, f32[128,2,3072]{2,1,0:T(2,128)}, f32[3072,128]{1,0:T(8,128)}, f32[3072,128]{1,0...) custom-call(s32[7]{0:T(128)S(1)} %get-tuple-element.208.scalars, f32[128,2,3072]{2,1,0:T(2,128)} %refs_0_.3, ...), custom_call_target="tpu_custom_call" | custom-call | flops 10000000000 | bytes 1 | tf_op jit(solution)/shard_map/adam_mlp/pallas_call | solution.py:60
  (318 shorter events, 200.9 us)
Async XLA Ops:
  7.2 108.2 %all-gather.4.cloned.1.call-start = ((), (), s32[]{:S(2)}) async-start(), calls=%async_computation.5 | async-start | bytes 13369344 | tf_op jit(solution)/shard_map/all_gather | solution.py:713
  11.7 247.5 %all-gather.6.cloned.1.call-start = ((), (), s32[]{:S(2)}) async-start(), calls=%async_computation.6 | async-start | bytes 26738688 | tf_op jit(solution)/shard_map/all_gather | solution.py:713
  19.8 356.4 %all-gather.8.cloned.1.call-start = ((), (), s32[]{:S(2)}) async-start(), calls=%async_computation.7 | async-start | bytes 13369344 | tf_op jit(solution)/shard_map/all_gather | solution.py:713
  22.4 561.1 %reduce-scatter.6.cloned.1.call-start = ((), (), s32[]{:S(2)}) async-start(), calls=%async_computation.8 | async-start | bytes 7864320 | tf_op jit(solution)/shard_map/reduce_scatter | solution.py:645
  24.8 49.8 %collective-permute-start = (bf16[512,2048]{1,0:T(8,128)(2,1)}, bf16[512,2048]{1,0:T(8,128)(2,1)}, u32[]{:S(2)}, u32[]{:S(2)}) collective-permute-start(bf16[512,2048]{1,0:T(8,128)(2,1)} %fusion.2.refs_0_.refs_2_), channel_id=1, source_target_pairs={{0,1},{1,0},{2,3},{3,2},{4,5},{5,4},{6,7},{7,6},{8,9},{9,8},{10,11... | collective-permute-start | bytes 6291464 | tf_op jit(solution)/shard_map/ppermute | solution.py:707
  31.6 117.6 %collective-permute-start.1 = (bf16[512,2048]{1,0:T(8,128)(2,1)}, bf16[512,2048]{1,0:T(8,128)(2,1)}, u32[]{:S(2)}, u32[]{:S(2)}) collective-permute-start(bf16[512,2048]{1,0:T(8,128)(2,1)} %broadcast_select_fusion.refs_0_.refs_2_.refs_3_), channel_id=1, source_target_pairs={{0,1},{1,0},{2,3},{3,2},{4,5},{5,4},{6,7},{7,6},{8,9},{9,8},{10,11... | collective-permute-start | bytes 6291464 | tf_op jit(solution)/shard_map/ppermute | solution.py:707
  83.6 72.4 %collective-permute-start.2 = (bf16[1024,1024]{1,0:T(8,128)(2,1)}, bf16[1024,1024]{1,0:T(8,128)(2,1)}, u32[]{:S(2)}, u32[]{:S(2)}) collective-permute-start(bf16[1024,1024]{1,0:T(8,128)(2,1)} %get-tuple-element.129), channel_id=1, source_target_pairs={{0,2},{2,0},{1,3},{3,1},{4,6},{6,4},{5,7},{7,5},{8,10},{10,8},{9,1... | collective-permute-start | bytes 6291464 | tf_op jit(solution)/shard_map/ppermute | solution.py:618
  139.2 16.7 %collective-permute-start.3 = (bf16[1024,1024]{1,0:T(8,128)(2,1)S(1)}, bf16[1024,1024]{1,0:T(8,128)(2,1)S(1)}, u32[]{:S(2)}, u32[]{:S(2)}) collective-permute-start(bf16[1024,1024]{1,0:T(8,128)(2,1)S(1)} %get-tuple-element.126.refs_0_.refs_2_), channel_id=1, source_target_pairs={{0,2},{2,0},{1,3},{3,1},{4,6},{6,4},{5,7},{7,5},{8,10},{10,8},{9,1... | collective-permute-start | bytes 6291464 | tf_op jit(solution)/shard_map/ppermute | solution.py:618
  147.6 48.1 %collective-permute-start.4 = (bf16[512,2048]{1,0:T(8,128)(2,1)S(1)}, bf16[512,2048]{1,0:T(8,128)(2,1)}, u32[]{:S(2)}, u32[]{:S(2)}) collective-permute-start(bf16[512,2048]{1,0:T(8,128)(2,1)S(1)} %get-tuple-element.132), channel_id=1, source_target_pairs={{0,1},{1,0},{2,3},{3,2},{4,5},{5,4},{6,7},{7,6},{8,9},{9,8},{10,11... | collective-permute-start | bytes 6291464 | tf_op jit(solution)/shard_map/ppermute | solution.py:707
  201.9 47.1 %collective-permute-start.5 = (bf16[512,2048]{1,0:T(8,128)(2,1)S(1)}, bf16[512,2048]{1,0:T(8,128)(2,1)S(1)}, u32[]{:S(2)}, u32[]{:S(2)}) collective-permute-start(bf16[512,2048]{1,0:T(8,128)(2,1)S(1)} %get-tuple-element.134.refs_0_.refs_2_), channel_id=1, source_target_pairs={{0,1},{1,0},{2,3},{3,2},{4,5},{5,4},{6,7},{7,6},{8,9},{9,8},{10,11... | collective-permute-start | bytes 6291464 | tf_op jit(solution)/shard_map/ppermute | solution.py:707
  203.4 55.8 %collective-permute-start.6 = (bf16[1024,1024]{1,0:T(8,128)(2,1)S(1)}, bf16[1024,1024]{1,0:T(8,128)(2,1)}, u32[]{:S(2)}, u32[]{:S(2)}) collective-permute-start(bf16[1024,1024]{1,0:T(8,128)(2,1)S(1)} %get-tuple-element.136), channel_id=1, source_target_pairs={{0,2},{2,0},{1,3},{3,1},{4,6},{6,4},{5,7},{7,5},{8,10},{10,8},{9,1... | collective-permute-start | bytes 6291464 | tf_op jit(solution)/shard_map/ppermute | solution.py:618
  281.5 33.6 %collective-permute-start.8 = (bf16[1024,3072]{1,0:T(8,128)(2,1)}, bf16[1024,3072]{1,0:T(8,128)(2,1)}, u32[]{:S(2)}, u32[]{:S(2)}) collective-permute-start(bf16[1024,3072]{1,0:T(8,128)(2,1)} %get-tuple-element.142.refs_4_.refs_0_), channel_id=1, source_target_pairs={{0,2},{2,0},{1,3},{3,1},{4,6},{6,4},{5,7},{7,5},{8,10},{10,8},{9,1... | collective-permute-start | bytes 18874376 | tf_op jit(solution)/shard_map/ppermute | solution.py:618
  301.0 56.0 %collective-permute-start.9 = (bf16[1024,3072]{1,0:T(8,128)(2,1)}, bf16[1024,3072]{1,0:T(8,128)(2,1)}, u32[]{:S(2)}, u32[]{:S(2)}) collective-permute-start(bf16[1024,3072]{1,0:T(8,128)(2,1)} %get-tuple-element.144.refs_1_.refs_4_), channel_id=1, source_target_pairs={{0,2},{2,0},{1,3},{3,1},{4,6},{6,4},{5,7},{7,5},{8,10},{10,8},{9,1... | collective-permute-start | bytes 18874376 | tf_op jit(solution)/shard_map/ppermute | solution.py:618
  336.0 295.0 %reduce-scatter.8.cloned.1.call-start = ((), (), s32[]{:S(2)}) async-start(), calls=%async_computation.9 | async-start | bytes 3932160 | tf_op jit(solution)/shard_map/reduce_scatter | solution.py:659
  336.0 48.3 %collective-permute-start.10 = (bf16[1024,1024]{1,0:T(8,128)(2,1)}, bf16[1024,1024]{1,0:T(8,128)(2,1)}, u32[]{:S(2)}, u32[]{:S(2)}) collective-permute-start(bf16[1024,1024]{1,0:T(8,128)(2,1)} %copy-done.15), channel_id=1, source_target_pairs={{0,1},{1,0},{2,3},{3,2},{4,5},{5,4},{6,7},{7,6},{8,9},{9,8},{10,11... | collective-permute-start | bytes 6291464 | tf_op jit(solution)/shard_map/ppermute | solution.py:707
  406.9 77.1 %collective-permute-start.14 = (bf16[512,3072]{1,0:T(8,128)(2,1)S(1)}, bf16[512,3072]{1,0:T(8,128)(2,1)}, u32[]{:S(2)}, u32[]{:S(2)}) collective-permute-start(bf16[512,3072]{1,0:T(8,128)(2,1)S(1)} %copy-done.75), channel_id=1, source_target_pairs={{0,4},{4,0},{1,5},{5,1},{2,6},{6,2},{3,7},{7,3},{8,12},{12,8},{9,1... | collective-permute-start | bytes 9437192 | tf_op jit(solution)/shard_map/ppermute | solution.py:638
  419.6 47.7 %collective-permute-start.12 = (bf16[512,2048]{1,0:T(8,128)(2,1)S(1)}, bf16[512,2048]{1,0:T(8,128)(2,1)S(1)}, u32[]{:S(2)}, u32[]{:S(2)}) collective-permute-start(bf16[512,2048]{1,0:T(8,128)(2,1)S(1)} %get-tuple-element.155), channel_id=1, source_target_pairs={{0,1},{1,0},{2,3},{3,2},{4,5},{5,4},{6,7},{7,6},{8,9},{9,8},{10,11... | collective-permute-start | bytes 6291464 | tf_op jit(solution)/shard_map/ppermute | solution.py:707
  421.2 56.8 %collective-permute-start.13 = (bf16[1024,1024]{1,0:T(8,128)(2,1)}, bf16[1024,1024]{1,0:T(8,128)(2,1)}, u32[]{:S(2)}, u32[]{:S(2)}) collective-permute-start(bf16[1024,1024]{1,0:T(8,128)(2,1)} %collective-permute-done.10.refs_5_.refs_2_), channel_id=1, source_target_pairs={{0,2},{2,0},{1,3},{3,1},{4,6},{6,4},{5,7},{7,5},{8,10},{10,8},{9,1... | collective-permute-start | bytes 6291464 | tf_op jit(solution)/shard_map/ppermute | solution.py:618
  490.4 257.5 %reduce-scatter.10.cloned.1.call-start = ((), (), s32[]{:S(2)}) async-start(), calls=%async_computation.10 | async-start | bytes 3932160 | tf_op jit(solution)/shard_map/reduce_scatter | solution.py:659
  492.0 81.2 %collective-permute-start.18 = (bf16[512,3072]{1,0:T(8,128)(2,1)}, bf16[512,3072]{1,0:T(8,128)(2,1)S(1)}, u32[]{:S(2)}, u32[]{:S(2)}) collective-permute-start(bf16[512,3072]{1,0:T(8,128)(2,1)} %get-tuple-element.176), channel_id=1, source_target_pairs={{0,4},{4,0},{1,5},{5,1},{2,6},{6,2},{3,7},{7,3},{8,12},{12,8},{9,1... | collective-permute-start | bytes 9437192 | tf_op jit(solution)/shard_map/ppermute | solution.py:638
  493.6 29.6 %collective-permute-start.16 = (bf16[512,512]{1,0:T(8,128)(2,1)}, bf16[512,512]{1,0:T(8,128)(2,1)S(1)}, u32[]{:S(2)}, u32[]{:S(2)}) collective-permute-start(bf16[512,512]{1,0:T(8,128)(2,1)} %copy-done.34), channel_id=1, source_target_pairs={{0,1},{1,0},{2,3},{3,2},{4,5},{5,4},{6,7},{7,6},{8,9},{9,8},{10,11... | collective-permute-start | bytes 1572872 | tf_op jit(solution)/shard_map/ppermute | solution.py:707
  500.9 61.7 %collective-permute-start.17 = (bf16[512,2048]{1,0:T(8,128)(2,1)}, bf16[512,2048]{1,0:T(8,128)(2,1)S(1)}, u32[]{:S(2)}, u32[]{:S(2)}) collective-permute-start(bf16[512,2048]{1,0:T(8,128)(2,1)} %get-tuple-element.173.refs_0_.refs_2_), channel_id=1, source_target_pairs={{0,1},{1,0},{2,3},{3,2},{4,5},{5,4},{6,7},{7,6},{8,9},{9,8},{10,11... | collective-permute-start | bytes 6291464 | tf_op jit(solution)/shard_map/ppermute | solution.py:707
  581.3 189.5 %reduce-scatter.14.cloned.1.call-start = ((), (), s32[]{:S(2)}) async-start(), calls=%async_computation.12 | async-start | bytes 2621440 | tf_op jit(solution)/shard_map/reduce_scatter | solution.py:659
  581.4 15.2 %collective-permute-start.20 = (bf16[1024,1024]{1,0:T(8,128)(2,1)}, bf16[1024,1024]{1,0:T(8,128)(2,1)}, u32[]{:S(2)}, u32[]{:S(2)}) collective-permute-start(bf16[1024,1024]{1,0:T(8,128)(2,1)} %copy-done.4), channel_id=1, source_target_pairs={{0,2},{2,0},{1,3},{3,1},{4,6},{6,4},{5,7},{7,5},{8,10},{10,8},{9,1... | collective-permute-start | bytes 6291464 | tf_op jit(solution)/shard_map/ppermute | solution.py:618
  581.9 23.8 %collective-permute-start.21 = (bf16[1024,1024]{1,0:T(8,128)(2,1)}, bf16[1024,1024]{1,0:T(8,128)(2,1)}, u32[]{:S(2)}, u32[]{:S(2)}) collective-permute-start(bf16[1024,1024]{1,0:T(8,128)(2,1)} %copy-done.29), channel_id=1, source_target_pairs={{0,2},{2,0},{1,3},{3,1},{4,6},{6,4},{5,7},{7,5},{8,10},{10,8},{9,1... | collective-permute-start | bytes 6291464 | tf_op jit(solution)/shard_map/ppermute | solution.py:618
  582.0 64.1 %collective-permute-start.23 = (bf16[512,2048]{1,0:T(8,128)(2,1)}, bf16[512,2048]{1,0:T(8,128)(2,1)}, u32[]{:S(2)}, u32[]{:S(2)}) collective-permute-start(bf16[512,2048]{1,0:T(8,128)(2,1)} %copy-done.21), channel_id=1, source_target_pairs={{0,1},{1,0},{2,3},{3,2},{4,5},{5,4},{6,7},{7,6},{8,9},{9,8},{10,11... | collective-permute-start | bytes 6291464 | tf_op jit(solution)/shard_map/ppermute | solution.py:707
  595.0 33.7 %collective-permute-start.22 = (bf16[512,1024]{1,0:T(8,128)(2,1)S(1)}, bf16[512,1024]{1,0:T(8,128)(2,1)S(1)}, u32[]{:S(2)}, u32[]{:S(2)}) collective-permute-start(bf16[512,1024]{1,0:T(8,128)(2,1)S(1)} %get-tuple-element.190), channel_id=1, source_target_pairs={{0,4},{4,0},{1,5},{5,1},{2,6},{6,2},{3,7},{7,3},{8,12},{12,8},{9,1... | collective-permute-start | bytes 3145736 | tf_op jit(solution)/shard_map/ppermute | solution.py:638
  605.2 62.9 %collective-permute-start.24 = (bf16[512,1024]{1,0:T(8,128)(2,1)}, bf16[512,1024]{1,0:T(8,128)(2,1)}, u32[]{:S(2)}, u32[]{:S(2)}) collective-permute-start(bf16[512,1024]{1,0:T(8,128)(2,1)} %get-tuple-element.198), channel_id=1, source_target_pairs={{0,4},{4,0},{1,5},{5,1},{2,6},{6,2},{3,7},{7,3},{8,12},{12,8},{9,1... | collective-permute-start | bytes 3145736 | tf_op jit(solution)/shard_map/ppermute | solution.py:638
  615.3 52.9 %collective-permute-start.25 = (bf16[512,1024]{1,0:T(8,128)(2,1)}, bf16[512,1024]{1,0:T(8,128)(2,1)}, u32[]{:S(2)}, u32[]{:S(2)}) collective-permute-start(bf16[512,1024]{1,0:T(8,128)(2,1)} %get-tuple-element.200), channel_id=1, source_target_pairs={{0,4},{4,0},{1,5},{5,1},{2,6},{6,2},{3,7},{7,3},{8,12},{12,8},{9,1... | collective-permute-start | bytes 3145736 | tf_op jit(solution)/shard_map/ppermute | solution.py:638
  672.7 99.1 %reduce-scatter.12.cloned.1.call-start = ((), (), s32[]{:S(2)}) async-start(), calls=%async_computation.11 | async-start | bytes 1310720 | tf_op jit(solution)/shard_map/reduce_scatter | solution.py:659
  672.8 47.2 %collective-permute-start.27 = (bf16[512,2048]{1,0:T(8,128)(2,1)}, bf16[512,2048]{1,0:T(8,128)(2,1)S(1)}, u32[]{:S(2)}, u32[]{:S(2)}) collective-permute-start(bf16[512,2048]{1,0:T(8,128)(2,1)} %copy-done.28), channel_id=1, source_target_pairs={{0,1},{1,0},{2,3},{3,2},{4,5},{5,4},{6,7},{7,6},{8,9},{9,8},{10,11... | collective-permute-start | bytes 6291464 | tf_op jit(solution)/shard_map/ppermute | solution.py:707
  674.0 18.5 %collective-permute-start.26 = (bf16[128,3072]{1,0:T(8,128)(2,1)S(1)}, bf16[128,3072]{1,0:T(8,128)(2,1)S(1)}, u32[]{:S(2)}, u32[]{:S(2)}) collective-permute-start(bf16[128,3072]{1,0:T(8,128)(2,1)S(1)} %get-tuple-element.202), channel_id=1, source_target_pairs={{0,4},{4,0},{1,5},{5,1},{2,6},{6,2},{3,7},{7,3},{8,12},{12,8},{9,1... | collective-permute-start | bytes 2359304 | tf_op jit(solution)/shard_map/ppermute | solution.py:650
  (90 other events, 1021.3 us)
Sparse Core Ops, SparseCore 0:
  11.8 103.4 all-gather.3
  117.5 126.7 all-gather.5
  247.2 100.7 all-gather.7
  350.1 108.9 reduce-scatter.5
  490.6 59.5 reduce-scatter.7
  581.4 59.5 reduce-scatter.9
  672.8 42.1 reduce-scatter.13
  746.7 24.3 reduce-scatter.11

commit v2 on v1

--- a/solution.py
+++ b/solution.py
@@ -29,8 +29,9 @@
 F32 = jnp.float32
 ROWS = 256
 TILE = 256
+BLOCK = 1024
 CHUNKS = 3
-WORK = 5 * 10**8
+WORK = 10**10
 
 NN = (((1,), (0,)), ((), ()))
 NT = (((1,), (1,)), ((), ()))
@@ -43,6 +44,7 @@
 
 class Order:
     def __init__(self, side, length, core):
+        self.rate = WORK
         one = jnp.ones_like(side)
         self.scalars = jnp.stack([side, 1 - side, length, 0 * one, one, core, 1 - core]).astype(jnp.int32)
 
@@ -71,7 +73,7 @@
             + [shaped(v.shape, v.dtype) for v in through],
             input_output_aliases={1 + count + len(after) + i: made + 1 + i for i in range(len(through))},
             compiler_params=pltpu.CompilerParams(vmem_limit_bytes=vmem * 2**20),
-            cost_estimate=pl.CostEstimate(flops=int(work * WORK), bytes_accessed=1, transcendentals=0),
+            cost_estimate=pl.CostEstimate(flops=int(work * self.rate) + 1, bytes_accessed=1, transcendentals=0),
             name=name,
         )(self.scalars, *operands, *after, *through)
         self.scalars = results[made]
@@ -305,33 +307,45 @@
 PAIR = 2 * TILE
 
 
-def swiglu_kernel(place_ref, second_own, second_other, back_own, back_other, weight_ref, out_ref):
+def swiglu_kernel(place_ref, second_own, second_other, back_own, back_other, pair_ref, down_ref, grad_ref, hidden_ref):
     half = second_own.shape[0]
     for at, second_ref, back_ref in ((0, second_own, back_own), (half, second_other, back_other)):
         rows = slice(at, at + half)
-        pair = mm(second_ref[...], weight_ref[:, :PAIR])
-        d_hidden = mm(back_ref[...], weight_ref[:, PAIR:])
+        pair = mm(second_ref[...], pair_ref[...])
+        d_hidden = mm(back_ref[...], down_ref[...])
         gate, up = pair[:, :TILE], pair[:, TILE:]
         sigmoid = 1.0 / (1.0 + jnp.exp(-gate))
         silu = gate * sigmoid
         d_gate = d_hidden * up * (sigmoid * (1.0 + gate * (1.0 - sigmoid)))
-        out_ref[rows, :TILE] = d_gate.astype(BF)
-        out_ref[rows, TILE:PAIR] = (d_hidden * silu).astype(BF)
-        out_ref[rows, PAIR:] = (silu * up).astype(BF)
-
-
-def swiglu(order, second, back, weights, first_tile, tiles, after=(), through=()):
+        grad_ref[rows, :TILE] = d_gate.astype(BF)
+        grad_ref[rows, TILE:] = (d_hidden * silu).astype(BF)
+        hidden_ref[rows, :] = (silu * up).astype(BF)
+
+
+def swiglu(order, second, back, weights, count, tiles, after=(), through=()):
     half, width = second[0].shape
     rows = held((half, width))
+    pair_at = lambda j: j // tiles * (3 * tiles // 2) + j % tiles
+    down_at = lambda j: j // tiles * (3 * tiles) + 2 * tiles + j % tiles
     return order.call(
         swiglu_kernel,
-        (tiles,),
-        [rows, rows, rows, rows, pl.BlockSpec((width, WIDE), lambda j, s: (0, first_tile + j))],
-        [(pl.BlockSpec((2 * half, WIDE), lambda j, s: (0, j)), shaped((2 * half, tiles * WIDE), BF))],
-        (*second, *back, weights),
+        (count * tiles,),
+        [
+            rows,
+            rows,
+            rows,
+            rows,
+            pl.BlockSpec((width, PAIR), lambda j, s: (0, pair_at(j))),
+            pl.BlockSpec((width, TILE), lambda j, s: (0, down_at(j))),
+        ],
+        [
+            (pl.BlockSpec((2 * half, PAIR), lambda j, s: (0, j)), shaped((2 * half, count * tiles * PAIR), BF)),
+            (pl.BlockSpec((2 * half, TILE), lambda j, s: (0, j)), shaped((2 * half, count * tiles * TILE), BF)),
+        ],
+        (*second, *back, weights, weights),
         after=after,
         through=through,
-        work=5 * tiles,
+        work=5 * count * tiles,
         name="swiglu",
     )
 
@@ -376,12 +390,15 @@
     return keep_cols, send_cols
 
 
-def weight_grad_kernel(splits, place_ref, *refs):
-    lefts, (own_ref, other_ref, *outs) = refs[: 2 * len(splits)], refs[2 * len(splits) :]
-    half = lefts[0].shape[0] // 2
-    for i, (first, last) in enumerate(splits):
-        cols = slice(first, last)
-        product = mm(lefts[2 * i][...], own_ref[:, cols]) + mm(lefts[2 * i + 1][...], other_ref[:, cols])
+def weight_grad_kernel(widths, place_ref, *refs):
+    outs = refs[4 * len(widths) :]
+    half = refs[0].shape[0] // 2
+    first = 0
+    for i, width in enumerate(widths):
+        left, far_left, right, far_right = refs[4 * i : 4 * i + 4]
+        cols = slice(first, first + width)
+        first += width
+        product = mm(left[...], right[...]) + mm(far_left[...], far_right[...])
         if len(outs) == 2:
             outs[0][:, cols] = product[:half].astype(BF)
             outs[1][:, cols] = product[half:].astype(BF)
@@ -392,57 +409,90 @@
             outs[0][at + owned : at + 2 * owned, cols] = product[half + line * owned : half + (line + 1) * owned].astype(BF)
 
 
-def weight_grad(order, lefts, splits, own, other, step, by_line=False, after=(), through=()):
-    rows, cap = lefts[0][0].shape
-    cols = own.shape[1]
-    right = pl.BlockSpec((cap, step), lambda j, s: (0, j))
-    outs = [(pl.BlockSpec((rows // 2, step), lambda j, s: (0, j)), shaped((rows // 2, cols), BF))] * 2
-    if by_line:
-        outs = [(pl.BlockSpec((rows, step), lambda j, s: (0, j)), shaped((rows, cols), BF))]
-    return order.call(
-        functools.partial(weight_grad_kernel, splits),
-        (cols // step,),
-        [held((rows, cap))] * (2 * len(lefts)) + [right, right],
-        outs,
-        (*[part for pair in lefts for part in pair], own, other),
+def weight_grad(order, items, by_line=False, after=()):
+    rows, cap = items[0][0][0].shape
+    widths = [width for _, _, width, _, _ in items]
+    steps, step = items[0][4], sum(widths)
+    out_rows = rows if by_line else rows // 2
+    out = (pl.BlockSpec((out_rows, step), lambda j, s: (0, j)), shaped((out_rows, steps * step), BF))
+    ins = []
+    for _, _, width, first, _ in items:
+        ins += [held((rows, cap))] * 2
+        ins += [pl.BlockSpec((cap, width), functools.partial(lambda first, j, s: (0, first + j), first))] * 2
+    return order.call(
+        functools.partial(weight_grad_kernel, widths),
+        (steps,),
+        ins,
+        [out] if by_line else [out, out],
+        [part for left, right, *_ in items for part in (*left, *right)],
         after=after,
-        through=through,
-        work=cols // 160,
+        work=steps * step // 160,
         name="weight_grad",
     )
 
 
-def contract_kernel(count, ranges, adds, place_ref, *refs):
-    outs = refs[2 * count + adds :]
-    for out_ref, spans in zip(outs, ranges, strict=True):
-        total = 0.0
-        for i in range(count):
-            for first, last in spans:
-                total = total + mm(refs[i][:, first:last], refs[count + i][:, first:last], NT)
-        for i in range(adds):
-            total = total + refs[2 * count + i][...].astype(F32)
-        out_ref[...] = total.astype(out_ref.dtype)
-
-
-def contract(order, which, lefts, weights, ranges, dtypes, adds=(), after=()):
-    half, step = lefts[0].shape[0] // 2, 256
-    width = weights[0][0].shape[0]
-    ins = [pl.BlockSpec((half, a.shape[1]), lambda j, s: (s[which], 0), pipeline_mode=pl.Buffered(1)) for a in lefts]
-    ins += [
-        pl.BlockSpec((step, a.shape[1]), functools.partial(lambda block, j, s: (j, block), block))
-        for a, (_, block) in zip(lefts, weights, strict=True)
+def contract_kernel(count, adds, place_ref, *refs):
+    total = 0.0
+    for i in range(count):
+        total = total + mm(refs[i][...], refs[count + i][...], NT)
+    for i in range(adds):
+        total = total + refs[2 * count + i][...].astype(F32)
+    refs[-1][...] = total.astype(refs[-1].dtype)
+
+
+def contract(order, which, pairs, dtype, adds=(), after=()):
+    half, width = pairs[0][0].shape[0] // 2, pairs[0][2].shape[0]
+    step = 512
+    ins = [
+        pl.BlockSpec((half, BLOCK), functools.partial(lambda at, j, s: (s[which], at), at), pipeline_mode=pl.Buffered(1))
+        for _, at, _, _ in pairs
     ]
+    ins += [pl.BlockSpec((step, BLOCK), functools.partial(lambda at, j, s: (j, at), at)) for _, _, _, at in pairs]
     across = pl.BlockSpec((half, step), lambda j, s: (0, j))
-    ins += [across] * len(adds)
-    return order.call(
-        functools.partial(contract_kernel, len(lefts), ranges, len(adds)),
+    return order.call(
+        functools.partial(contract_kernel, len(pairs), len(adds)),
+        (width // step,),
+        ins + [across] * len(adds),
+        [(across, shaped((half, width), dtype))],
+        (*[left for left, _, _, _ in pairs], *[weights for _, _, weights, _ in pairs], *adds),
+        after=after,
+        work=8 * len(pairs),
+        name="contract",
+    )[0]
+
+
+def contract_both_kernel(which, count, place_ref, *refs):
+    total = 0.0
+    for i in range(count):
+        total = total + mm(refs[i][...], refs[count + i][...], NT)
+    half = total.shape[0] // 2
+    first, second = total[:half], total[half:]
+    here_ref, there_ref = refs[-2:]
+    if which == FIRST:
+        here_ref[...], there_ref[...] = first, second.astype(BF)
+        return
+    here = place_ref[which] == 0
+    here_ref[...] = jnp.where(here, first, second)
+    there_ref[...] = jnp.where(here, second, first).astype(BF)
+
+
+def contract_both(order, which, pairs):
+    rows, width = pairs[0][0].shape[0], pairs[0][2].shape[0]
+    step = 512
+    ins = [
+        pl.BlockSpec((rows, BLOCK), functools.partial(lambda at, j, s: (0, at), at), pipeline_mode=pl.Buffered(1))
+        for _, at, _, _ in pairs
+    ]
+    ins += [pl.BlockSpec((step, BLOCK), functools.partial(lambda at, j, s: (j, at), at)) for _, _, _, at in pairs]
+    across = pl.BlockSpec((rows // 2, step), lambda j, s: (0, j))
+    return order.call(
+        functools.partial(contract_both_kernel, which, len(pairs)),
         (width // step,),
         ins,
-        [(across, shaped((half, width), t)) for t in dtypes],
-        (*lefts, *[w for w, _ in weights], *adds),
-        after=after,
-        work=sum(a.shape[1] for a in lefts) // 400,
-        name="contract",
+        [(across, shaped((rows // 2, width), F32)), (across, shaped((rows // 2, width), BF))],
+        (*[left for left, _, _, _ in pairs], *[weights for _, _, weights, _ in pairs]),
+        work=5 * len(pairs),
+        name="contract_both",
     )
 
 
@@ -510,6 +560,17 @@
     )
 
 
+def sum_kernel(place_ref, *refs):
+    refs[-1][...] = sum(r[...].astype(F32) for r in refs[:-1])
+
+
+def sum_rows(order, *arrays):
+    rows, width = arrays[0].shape
+    spec = lines_spec(width)
+    out = (spec, shaped((rows, width), F32))
+    return order.call(sum_kernel, (rows // LINES,), [spec] * len(arrays), [out], arrays, work=4, name="sum_rows")[0]
+
+
 def add_kernel(place_ref, *refs):
     at = 0
     for i in range(len(refs) // 2):
@@ -518,7 +579,7 @@
         at += a.shape[1]
 
 
-def add_pairs(order, pairs, skip=0):
+def add_pairs(order, pairs, skip=0, after=()):
     rows = pairs[0][1].shape[0]
     lines = min(LINES, rows)
     flat = [part for pair in pairs for part in pair]
@@ -530,6 +591,7 @@
         [spec(a.shape[1], skip * (i == 0)) for pair in pairs for i, a in enumerate(pair)],
         [(spec(width, 0), shaped((rows, width), BF))],
         flat,
+        after=after,
         work=5,
         name="add_pairs",
     )[0]
@@ -547,44 +609,97 @@
     )[0]
 
 
-def beside_kernel(place_ref, *refs):
-    at = 0
-    for ref in refs[:-1]:
-        refs[-1][:, at : at + ref.shape[1]] = ref[...]
-        at += ref.shape[1]
-
-
-def beside(order, arrays):
-    rows, width = arrays[0].shape[0], sum(a.shape[1] for a in arrays)
-    whole = [pl.BlockSpec(a.shape, lambda j, s: (0, 0)) for a in arrays]
-    out = (pl.BlockSpec((rows, width), lambda j, s: (0, 0)), shaped((rows, width), arrays[0].dtype))
-    return order.call(beside_kernel, (1,), whole, [out], arrays, work=2, name="beside")
+def adam_qkv_kernel(rate, place_ref, *refs):
+    query, keyval, sums, query_out, keyval_out = refs[0:3], refs[3:6], refs[6], refs[7:10], refs[10:13]
+    width = query[0].shape[1]
+    new = adam_step(*[r[...] for r in query], sums[:, :width].astype(F32), rate, WEIGHT_DECAY)
+    for out, value in zip(query_out, new, strict=True):
+        out[...] = value
+    for i in range(2):
+        grad = sums[:, width + i * HD : width + (i + 1) * HD].astype(F32)
+        new = adam_step(*[r[:, i, :] for r in keyval], grad, rate, WEIGHT_DECAY)
+        for out, value in zip(keyval_out, new, strict=True):
+            out[:, i, :] = value
+
+
+def adam_qkv(order, query, keyval, sums, heads, rate):
+    shard, wide = query[0].shape
+    queries = pl.BlockSpec((shard, wide // heads), lambda j, s: (0, j))
+    pair = pl.BlockSpec((shard, 2, HD), lambda j, s: (0, 0, j))
+    return order.call(
+        functools.partial(adam_qkv_kernel, rate),
+        (heads,),
+        [queries] * 3 + [pair] * 3 + [pl.BlockSpec((shard, wide // heads + 2 * HD), lambda j, s: (0, j))],
+        [(queries, shaped(query[0].shape, F32))] * 3 + [(pair, shaped(keyval[0].shape, F32))] * 3,
+        (*query, *keyval, sums),
+        work=5,
+        name="adam_qkv",
+    )
+
+
+def adam_out_kernel(rate, place_ref, *refs):
+    new = adam_step(*[r[...] for r in refs[0:3]], refs[3][...].astype(F32).T, rate, WEIGHT_DECAY)
+    for out, value in zip(refs[4:7], new, strict=True):
+        out[...] = value
+
+
+def adam_out(order, weights, sums, rate):
+    tall, shard = weights[0].shape
+    block = pl.BlockSpec((256, shard), lambda j, s: (j, 0))
+    return order.call(
+        functools.partial(adam_out_kernel, rate),
+        (tall // 256,),
+        [block] * 3 + [pl.BlockSpec((shard, 256), lambda j, s: (0, j))],
+        [(block, shaped(weights[0].shape, F32))] * 3,
+        (*weights, sums),
+        work=3,
+        name="adam_out",
+    )
 
 
 def adam_kernel(rates, place_ref, *refs):
-    pair, down, sums, pair_out, down_out = refs[0:3], refs[3:6], refs[6], refs[7:10], refs[10:13]
-    for i in range(2):
-        new = adam_step(*[r[:, i, :] for r in pair], sums[:, i * TILE : (i + 1) * TILE].astype(F32), rates[0], WEIGHT_DECAY)
-        for out, value in zip(pair_out, new, strict=True):
-            out[:, i, :] = value
-    new = adam_step(*[r[...] for r in down], sums[:, PAIR:].astype(F32).T, rates[1], WEIGHT_DECAY)
+    pair, down, all_sums, (pair_out, down_out), grad_ref = refs[0:3], refs[3:6], refs[6:-7], (refs[-7:-4], refs[-4:-1]), refs[-1]
+    at = pl.program_id(0) // (pl.num_programs(0) // len(all_sums))
+    sums = all_sums[0][...]
+    for i in range(1, len(all_sums)):
+        sums = jnp.where(at == i, all_sums[i][...], sums)
+    sums = sums.astype(F32)
+    down_grads = []
+    for tile in range(2):
+        first = tile * WIDE
+        for piece in range(TILE // HD):
+            for i in range(2):
+                cols = slice(first + i * TILE + piece * HD, first + i * TILE + (piece + 1) * HD)
+                grad_ref[:, tile * 4 + piece * 2 + i, :] = sums[:, cols]
+        down_grads.append(sums[:, first + PAIR : first + WIDE].T)
+    new = adam_step(*[r[...] for r in pair], grad_ref[...], rates[0], WEIGHT_DECAY)
+    for out, value in zip(pair_out, new, strict=True):
+        out[...] = value
+    new = adam_step(*[r[...] for r in down], jnp.concatenate(down_grads, axis=0), rates[1], WEIGHT_DECAY)
     for out, value in zip(down_out, new, strict=True):
         out[...] = value
 
 
 def adam_mlp(order, pair, down, sums, rates):
     shard, _, units = pair[0].shape
-    wide = pl.BlockSpec((shard, 2, TILE), lambda j, s: (0, 0, j))
-    tall = pl.BlockSpec((TILE, shard), lambda j, s: (j, 0))
-    return order.call(
+    rows = units // HD * 2
+    seen = [v.reshape(shard, 2, units // HD, HD).transpose(0, 2, 1, 3).reshape(shard, rows, HD) for v in pair]
+    wide = pl.BlockSpec((shard, 8, HD), lambda j, s: (0, j, 0))
+    tall = pl.BlockSpec((2 * TILE, shard), lambda j, s: (j, 0))
+    steps = units // TILE // len(sums) // 2
+    part = lambda i: pl.BlockSpec((shard, 2 * WIDE), lambda j, s: (0, jnp.clip(j - i * steps, 0, steps - 1)))
+    new = order.call(
         functools.partial(adam_kernel, rates),
-        (units // TILE,),
-        [wide] * 3 + [tall] * 3 + [pl.BlockSpec((shard, WIDE), lambda j, s: (0, j))],
-        [(wide, shaped(pair[0].shape, F32))] * 3 + [(tall, shaped(down[0].shape, F32))] * 3,
-        (*pair, *down, sums),
+        (units // TILE // 2,),
+        [wide] * 3 + [tall] * 3 + [part(i) for i in range(len(sums))],
+        [(wide, shaped(seen[0].shape, F32))] * 3 + [(tall, shaped(down[0].shape, F32))] * 3,
+        (*seen, *down, *sums),
+        scratch=[pltpu.VMEM((shard, 8, HD), F32)],
         work=20,
         name="adam_mlp",
     )
+    back = lambda v: v.reshape(shard, units // HD, 2, HD).transpose(0, 2, 1, 3).reshape(shard, 2, units)
+    return [*[back(v) for v in new[:3]], *new[3:]]
 
 
 def rms_parts(values):
@@ -626,23 +741,24 @@
         keep, send = turn_columns(self.order, own, other, SIDE if in_order else None, self.axes, after)
         return keep, self.other_core(send)
 
-    def grad(self, lefts, splits, right, from_core, step, after=(), through=()):
+    def whole(self, items):
+        parts = []
+        for left, (right, _), width, first, steps in items:
+            right = right[:, first * width : (first + steps) * width]
+            parts.append(mm(left, right, TN).astype(BF).reshape(left.shape[1], -1, width))
+        return jnp.concatenate(parts, axis=2).reshape(parts[0].shape[0], -1)
+
+    def grad(self, items, after=()):
         if not self.lines:
-            tiled = right.reshape(right.shape[0], -1, step)
-            parts = [
-                mm(left, tiled[:, :, first:last].reshape(right.shape[0], -1), TN).reshape(left.shape[1], -1, last - first)
-                for left, (first, last) in zip(lefts, splits, strict=True)
-            ]
-            return jnp.concatenate(parts, axis=2).reshape(lefts[0].shape[1], -1).astype(BF), *through
-        near, keep, *handed = weight_grad(self.order, lefts, splits, right, from_core, step, after=after, through=through)
-        return keep, lax.ppermute(near, self.axes[1], [(0, 1), (1, 0)]), *handed
-
-    def grad_by_line(self, lefts, splits, right, from_core, step, after=(), through=()):
+            return (self.whole(items),)
+        near, keep = weight_grad(self.order, items, after=after)
+        return keep, lax.ppermute(near, self.axes[1], [(0, 1), (1, 0)])
+
+    def grad_by_line(self, items, after=()):
         if not self.lines:
-            first, *handed = self.grad(lefts, splits, right, from_core, step, after, through)
-            return self.finish((first,)), *handed
-        whole, *handed = weight_grad(self.order, lefts, splits, right, from_core, step, True, after, through)
-        return lax.psum_scatter(whole, self.axes[0], scatter_dimension=0, tiled=True), *handed
+            return self.finish((self.whole(items),))
+        (whole,) = weight_grad(self.order, items, True, after)
+        return lax.psum_scatter(whole, self.axes[0], scatter_dimension=0, tiled=True)
 
     def trade_by_line(self, summed):
         if not self.lines:
@@ -652,19 +768,19 @@
     def finish_by_line(self, summed, got):
         return add_pairs(self.order, [(summed, got)], 1) if self.lines else summed
 
-    def finish(self, *grads):
+    def finish(self, *grads, after=()):
         if not self.lines:
             return lax.psum_scatter(jnp.concatenate([g for g, in grads], axis=1), self.axes, scatter_dimension=0, tiled=True)
-        line = add_pairs(self.order, grads)
+        line = add_pairs(self.order, grads, after=after)
         return lax.psum_scatter(line, self.axes[0], scatter_dimension=0, tiled=True)
 
     def everywhere(self, values):
         if not self.lines:
             return lax.psum(values, (*self.axes, "tensor"))
         pair = [(0, 1), (1, 0)]
-        steps = [(self.axes[2], pair), ("tensor", pair), (self.axes[1], pair)]
+        steps = [(self.axes[2], pair), (self.axes[1], pair)]
         steps += [(self.axes[0], [(0, 1), (1, 0), (2, 3), (3, 2)]), (self.axes[0], [(0, 2), (2, 0), (1, 3), (3, 1)])]
-        for axis, pairs in steps:
+        for axis, pairs in (*steps, ("tensor", pair)):
             values = values + lax.ppermute(values, axis, pairs)
         return values
 
@@ -725,7 +841,9 @@
     out_shard = w_out.astype(BF).T
     pair_low = w_gateup.astype(BF).reshape(shard, 2, tiles, TILE)
     down_low = w_down.astype(BF).T.reshape(shard, tiles, TILE)
-    mlp_shard = jnp.concatenate([pair_low[:, 0], pair_low[:, 1], down_low], axis=2).reshape(shard, tiles * WIDE)
+    pair_low = jnp.stack([pair_low[:, 0], pair_low[:, 1]], axis=2).reshape(shard, CHUNKS, part * PAIR)
+    down_low = down_low.reshape(shard, CHUNKS, part * TILE)
+    mlp_shard = jnp.concatenate([pair_low, down_low], axis=2).reshape(shard, tiles * WIDE)
 
     stream = tokens.astype(F32)
     normed_own = (stream * rms_parts(stream) * norm_gains[0]).astype(BF)
@@ -749,56 +867,63 @@
 
     qkv, attended = attend(order, normed_own, normed_other, early, cosine, sine, head_gains, heads, group)
     attended_core = summer.other_core(attended)
-    out_block = [(early, qkv_cols // out_cols)]
-    whole_out = [[(0, out_cols)]]
-    attended_sent = swap(contract(order, OTHER_SIDE, [attended], out_block, whole_out, [BF])[0])
+    out_pair = [(attended, 0, early, qkv_cols // BLOCK)]
+    attended_sent = swap(contract(order, OTHER_SIDE, out_pair, BF))
     back_cols = summer.columns(back_own, back_other, False)
-    (attended_here,) = contract(
-        order, SIDE, [attended], out_block, whole_out, [F32], after=there(normed_cols[1], attended_core)
-    )
+    attended_here = contract(order, SIDE, out_pair, F32, after=there(normed_cols[1], attended_core))
     middle, second_own = middle_rows(order, tokens, attended_here, attended_sent, norm_gains)
 
     second = (second_own, swap(second_own))
     back = (back_own, back_other)
-    pair_spans = [(t * WIDE, t * WIDE + PAIR) for t in range(part)]
-    down_spans = [(t * WIDE + PAIR, (t + 1) * WIDE) for t in range(part)]
-    blocks = [(w, at // part) for w, at in parts]
-
-    def mlp(p, after=(), through=()):
-        piece, *handed = swiglu(order, second, back, parts[p][0], parts[p][1], part, after, through)
-        return (piece, summer.other_core(piece)), *handed
-
-    def mlp_grad(p, after=(), through=()):
-        return summer.grad([second_cols, back_cols], [(0, PAIR), (PAIR, WIDE)], *mlp_pieces[p], WIDE, after, through)
+    pair_blocks, down_blocks = part * PAIR // BLOCK, part * TILE // BLOCK
+    part_blocks = pair_blocks + down_blocks
+
+    def mlp(weights, count, after=(), through=()):
+        grads, hidden, *handed = swiglu(order, second, back, weights, count, part, after, through)
+        return ((grads, summer.other_core(grads)), (hidden, summer.other_core(hidden))), *handed
+
+    def mlp_items(p):
+        (grads, hidden), first = mlp_pieces[p // (CHUNKS - 1)], parts[p][1]
+        return [(second_cols, grads, PAIR, first, part), (back_cols, hidden, TILE, first, part)]
+
+    def second_pairs(p):
+        (grads, _), weights, at = mlp_pieces[p // (CHUNKS - 1)], parts[p][0], parts[p][1] // part
+        return [(grads[0], at * pair_blocks + b, weights, at * part_blocks + b) for b in range(pair_blocks)]
+
+    def down_pairs(p):
+        (_, hidden), weights, at = mlp_pieces[p // (CHUNKS - 1)], parts[p][0], parts[p][1] // part
+        first = at * part_blocks + pair_blocks
+        return [(hidden[0], at * down_blocks + b, weights, first + b) for b in range(down_blocks)]
+
+    all_down = lambda: [pair for p in range(CHUNKS) for pair in down_pairs(p)]
 
     out_rows = early.shape[0] // 2
     core = order.scalars[CORE]
     out_half = lax.dynamic_slice(early, (core * out_rows, qkv_cols), (out_rows, out_cols))
 
     second_cols = summer.columns(*second, False)
-    mlp_pieces = [*mlp(0, there(back_cols[1])), *mlp(1)]
-    splits = [(0, PAIR), (PAIR, WIDE)]
-    first_sum, out_half = summer.grad_by_line([second_cols, back_cols], splits, *mlp_pieces[0], WIDE, through=[out_half])
+    first_piece, out_half = mlp(most, CHUNKS - 1, there(back_cols[1]), [out_half])
     out_got = swap(out_half)
-    pieces = [piece for piece, _ in mlp_pieces]
-    (d_second_part,) = contract(order, SECOND, pieces, blocks[:2], [pair_spans], [BF])
-    mlp_grads = [mlp_grad(1)]
-    mlp_pieces += mlp(2, [out_got])
-    pieces = [piece for piece, _ in mlp_pieces]
-    d_second_sent = swap(contract(order, SECOND, pieces[2:], blocks[2:], [pair_spans], [BF], [d_second_part])[0])
+    mlp_pieces = [first_piece]
+    d_second_part = contract(order, SECOND, second_pairs(0) + second_pairs(1), BF, after=there(second_cols[1]))
+    line_sum = summer.grad_by_line(mlp_items(0))
+    mlp_grads = [summer.grad(mlp_items(1))]
+    last_piece, out_got = mlp(late, 1, through=[out_got])
+    mlp_pieces.append(last_piece)
+    d_second_sent = swap(contract(order, SECOND, second_pairs(2), BF, [d_second_part]))
     if summer.lines:
         out_other = [(out_got, 0, CORE), (summer.other_core(out_got), 0, OTHER_CORE)]
     else:
         out_other = [(swap(early[:, qkv_cols:]), 0, FIRST)]
-    mlp_grads.append(mlp_grad(2))
-    (d_second,) = contract(order, FIRST, pieces, blocks, [pair_spans], [F32])
+    mlp_grads.append(summer.grad(mlp_items(2)))
+    d_second = contract(order, FIRST, [pair for p in range(CHUNKS) for pair in second_pairs(p)], F32)
     d_middle, branch_own, branch_again, g_second_gain = norm_back(
         order, 1, d_second, d_second_sent, middle, back_own, norm_gains, 2
     )
 
     there_a, there_b = project(order, branch_own, out_other, out_cols)
     sent_a, sent_b = swap(there_a), swap(there_b)
-    mlp_sums = [summer.finish(mlp_grads[0])]
+    mlp_sums = [summer.finish(mlp_grads[0], after=[line_sum])]
     here_a, here_b, branch_again = project(
         order, branch_own, [(early, qkv_cols // out_cols, FIRST)], out_cols, [branch_again]
     )
@@ -813,57 +938,47 @@
 
     d_qkv_a, core_a, g_head_a = attention_back(0, here_a, sent_a)
     d_qkv_b, core_b, g_head_b = attention_back(1, here_b, sent_b)
-    (out_there,) = contract(order, SECOND, pieces, blocks, [down_spans], [BF])
+    qkv_grads = [
+        summer.grad([(normed_cols, (d_qkv_a, core_a), 512, 0, d_qkv_a.shape[1] // 512)]),
+        summer.grad([(normed_cols, (d_qkv_b, core_b), 512, 0, d_qkv_b.shape[1] // 512)]),
+    ]
+    mlp_sums.append(summer.finish(mlp_grads[1], after=mlp_sums[-1:]))
+    line_got = summer.trade_by_line(line_sum)
+    out_here, out_there = contract_both(order, FIRST, all_down())
     out_sent = swap(out_there)
     branch_cols = summer.columns(branch_again, branch_other, True)
-    mlp_sums.append(summer.finish(mlp_grads[1]))
-    first_got = summer.trade_by_line(first_sum)
-    qkv_grad_a = summer.grad([normed_cols], [(0, 512)], d_qkv_a, core_a, 512)
-    qkv_grad_b = summer.grad([normed_cols], [(0, 512)], d_qkv_b, core_b, 512)
-    out_grad = summer.grad([branch_cols], [(0, 512)], attended, attended_core, 512)
-    d_qkv = [d_qkv_a, d_qkv_b]
-    qkv_blocks = [(early, 0), (early, 1)]
-    whole_qkv = [[(0, qkv_cols // 2)]]
-    d_first_sent = swap(contract(order, OTHER_SIDE, d_qkv, qkv_blocks, whole_qkv, [BF])[0])
-    qkv_sum_a = summer.finish(qkv_grad_a)
-    (d_first,) = contract(order, SIDE, d_qkv, qkv_blocks, whole_qkv, [F32], after=mlp_sums[:1])
-    (layer_out,) = contract(order, FIRST, pieces, blocks, [down_spans], [F32], [middle, out_sent])
-    last_sum = summer.finish(qkv_grad_b, out_grad)
-    mlp_sums.insert(0, summer.finish_by_line(first_sum, first_got))
-    tokens_grad, g_first_gain = norm_back(order, 0, d_first, d_first_sent, tokens, d_middle, norm_gains, 0)
+    qkv_pairs = [(d_qkv_a, 0, early, 0), (d_qkv_b, 0, early, 1)]
+    d_first, d_first_there = contract_both(order, SIDE, qkv_pairs)
+    d_first_sent = swap(d_first_there)
+    mlp_sums.insert(0, summer.finish_by_line(line_sum, line_got))
+    qkv_sum = summer.finish(*qkv_grads, after=mlp_sums[-1:])
+    out_grad = summer.grad([(branch_cols, (attended, attended_core), 512, 0, out_cols // 512)])
     wide_rate = RATE_SCALE * D ** (-0.5)
     mlp_new = adam_mlp(
         order,
         (w_gateup, gateup_mean, gateup_square),
         (w_down, down_mean, down_square),
-        jnp.concatenate(mlp_sums, axis=1),
+        mlp_sums,
         (wide_rate, RATE_SCALE * FF ** (-0.5)),
     )
-    (qkv_sum,) = beside(order, [qkv_sum_a, last_sum[:, : qkv_cols // 2]])
-    out_sum = last_sum[:, qkv_cols // 2 :]
+    out_sum = summer.finish(out_grad)
+    order.rate = 0
+    tokens_grad, g_first_gain = norm_back(order, 0, d_first, d_first_sent, tokens, d_middle, norm_gains, 0)
+    qkv_new = adam_qkv(
+        order, (w_query, query_mean, query_square), (w_keyval, keyval_mean, keyval_square), qkv_sum, heads, wide_rate
+    )
+    layer_out = sum_rows(order, middle, out_here, out_sent)
+    out_new = adam_out(order, (w_out, out_mean, out_square), out_sum, RATE_SCALE * OUT_FAN ** (-0.5))
     g_head = g_head_a + g_head_b
 
-    out_sum = out_sum.astype(F32).T
-    qkv_sum = qkv_sum.astype(F32).reshape(shard, heads, (group + 2) * HD)
-    query_sum = qkv_sum[:, :, : group * HD].reshape(shard, heads * group * HD)
-    keyval_sum = jnp.stack(
-        [
-            qkv_sum[:, :, group * HD : (group + 1) * HD].reshape(shard, heads * HD),
-            qkv_sum[:, :, (group + 1) * HD :].reshape(shard, heads * HD),
-        ],
-        axis=1,
-    )
     gains_here = jnp.concatenate([g_first_gain[0], g_second_gain[0], g_head.reshape(-1)]).reshape(-1, HD)
     gain_sums = summer.everywhere(gains_here).reshape(-1)
     norm_sum = gain_sums[: 2 * D].reshape(2, D)
     head_sum = gain_sums[2 * D :].reshape(2, HD)
 
-    query_new = adam_step(w_query, query_mean, query_square, query_sum, wide_rate, WEIGHT_DECAY)
-    keyval_new = adam_step(w_keyval, keyval_mean, keyval_square, keyval_sum, wide_rate, WEIGHT_DECAY)
-    out_new = adam_step(w_out, out_mean, out_square, out_sum, RATE_SCALE * OUT_FAN ** (-0.5), WEIGHT_DECAY)
     norm_new = adam_step(norm_gains, norm_mean, norm_square, norm_sum, GAIN_RATE, 0.0)
     head_new = adam_step(head_gains, head_mean, head_square, head_sum, GAIN_RATE, 0.0)
-    return (layer_out, tokens_grad, *query_new, *keyval_new, *out_new, *mlp_new, *norm_new, *head_new)
+    return (layer_out, tokens_grad, *qkv_new, *out_new, *mlp_new, *norm_new, *head_new)
 
 
 def solution(mesh):

time: 804 us -> 714 us (0.89)
  waiting for transfers between devices: 224 us -> 187 us
  Pallas kernels: 434 us -> 403 us
  local copies, waits for them, and re-layouts: 71.4 us -> 56.6 us
  other arithmetic: 22 us -> 13.3 us
    ppermute x11, waiting for transfers between devices: 153 us -> 97.3 us  [swap(): return lax.ppermute(piece, 'tensor', [(0, 1), (1, 0)])]
    pallas_call x38 -> x37, Pallas kernels: 434 us -> 403 us  [call(): pl.pallas_call(run, grid_spec=pltpu.PrefetchScalarGridSpec(num_scalar_pre...]
    unnamed x169 -> x133, local copies, waits for them, and re-layouts: 64.2 us -> 47.3 us
    ppermute x5, waiting for transfers between devices: 0.01 us -> 16.6 us  [grad(): return (keep, lax.ppermute(near, self.axes[1], [(0, 1), (1, 0)]))]
    ppermute x1, waiting for transfers between devices: 18.1 us -> 6.25 us  [trade_by_line(): lax.ppermute(take_rows(self.order, summed), self.axes[1], [(0, 1), (1, 0)])]
    all_gather x3, waiting for transfers between devices: 31.8 us -> 42.2 us  [gather(): return lax.all_gather(shard, axes, axis=0, tiled=True)]
    ppermute x5, waiting for transfers between devices: 10.3 us -> 18.7 us  [everywhere(): values = values + lax.ppermute(values, axis, pairs)]
  transfers between devices with their start and end apart: 41 -> 42, of which waited for: 14 -> 16; matrix products, arithmetic and copies ran while one was open for 4% -> 4% of each run, Pallas kernels for 54% -> 57%
where the time goes in v2:
time: 714 us; the launch traced here: 708 us
  Pallas kernels  403 us (56%)
  waiting for transfers between devices  187 us (26%)
  local copies, waits for them, and re-layouts  56.6 us (8%)
  starting transfers between devices  31.2 us (4%)
  between operations  16.7 us (2%)
  other arithmetic  13.3 us (2%)
    pallas_call x37, Pallas kernels, call(): pl.pallas_call(run, grid_spec=pltpu.PrefetchScalarGridSpec(num_scalar_pre...  403 us
    ppermute x11, waiting for transfers between devices, swap(): return lax.ppermute(piece, 'tensor', [(0, 1), (1, 0)])  97.3 us
    unnamed x133, local copies, waits for them, and re-layouts  47.3 us
    all_gather x3, waiting for transfers between devices, gather(): return lax.all_gather(shard, axes, axis=0, tiled=True)  42.2 us
    ppermute x5, waiting for transfers between devices, everywhere(): values = values + lax.ppermute(values, axis, pairs)  18.7 us
    ppermute x5, waiting for transfers between devices, grad(): return (keep, lax.ppermute(near, self.axes[1], [(0, 1), (1, 0)]))  16.6 us
  transfers between devices with their start and end apart: 42, of which 16 were waited for; matrix products, arithmetic and copies ran while one was open for 4% of the time, Pallas kernels for 57%

profile of v2, /device:TPU:0, one launch (start us, length us, event | category | flops | bytes accessed | tf_op | source)
XLA Modules:
  0.0 708.1 jit_solution(522650655475956415)
XLA Ops:
  36.7 27.6 %collective-permute-done.refs_1_.refs_3_ = bf16[512,2048]{1,0:T(8,128)(2,1)} collective-permute-done((bf16[512,2048]{1,0:T(8,128)(2,1)}, bf16[512,2048]{1,0:T(8,128)(2,1)}, u32[]{:S(2)}, u32[]{:S(2)}) %collective-permute-start) | collective-permute-done | bytes 2097184 | tf_op jit(solution)/shard_map/ppermute | solution.py:823
  64.3 7.4 %turn_columns.4 = (bf16[1024,1024]{1,0:T(8,128)(2,1)S(1)}, bf16[1024,1024]{1,0:T(8,128)(2,1)}, s32[23]{0:T(128)S(1)}) custom-call(s32[23]{0:T(128)S(1)} %concatenate.30.scalars, bf16[512,2048]{1,0:T(8,128)(2,1)} %fusion.2.refs_0_.refs_2_, bf16[512,2048]{1,0:T(8,128)(2,1)} %collective-permute-done.refs_1_.refs_3_, bf16[512,2048]{1,0:T(8,128)(2,1)} %fusion.2.refs_0_.refs_2_, ...), custom_call_target="tpu_custom_call" | custom-call | flops 70000001024 | bytes 1 | tf_op jit(solution)/shard_map/turn_columns/pallas_call | solution.py:62
  73.1 42.2 %all-gather.4.cloned.1.call-done.refs_2_.refs_1_.refs_3_ = bf16[2048,3072]{1,0:T(8,128)(2,1)} async-done(((bf16[128,3072]{1,0:T(8,128)(2,1)}), bf16[2048,3072]{1,0:T(8,128)(2,1)}) %all-gather.4.cloned.1.call-update) | async-done | bytes 12582928 | tf_op jit(solution)/shard_map/all_gather | solution.py:829
  115.2 23.9 %attend.1 = (f32[1024,2048]{1,0:T(8,128)}, bf16[1024,1024]{1,0:T(8,128)(2,1)}, s32[7]{0:T(128)S(1)}) custom-call(s32[7]{0:T(128)S(1)} %bitcast.77, bf16[512,2048]{1,0:T(8,128)(2,1)} %fusion.2.refs_0_.refs_2_, bf16[512,2048]{1,0:T(8,128)(2,1)} %collective-permute-done.refs_1_.refs_3_, bf16[2048,3072]{1,0:T(8,128)(2,1)} %all-gather.4.cloned.1.call-done.refs_2_.refs_1_.refs_3_, ...), custom_call_target="tpu_custom_call" | custom-call | flops 240000008192 | bytes 1 | tf_op jit(solution)/shard_map/attend/pallas_call | solution.py:62
  147.7 6.7 turn_columns.5
  157.1 7.0 contract.6
  164.1 30.1 %collective-permute-done.4.refs_2_ = bf16[512,2048]{1,0:T(8,128)(2,1)} collective-permute-done((bf16[512,2048]{1,0:T(8,128)(2,1)}, bf16[512,2048]{1,0:T(8,128)(2,1)}, u32[]{:S(2)}, u32[]{:S(2)}) %collective-permute-start.4) | collective-permute-done | bytes 2097184 | tf_op jit(solution)/shard_map/ppermute | solution.py:823
  194.2 6.7 middle_rows.1
  211.8 36.4 %collective-permute-done.5.refs_1_.refs_3_ = bf16[512,2048]{1,0:T(8,128)(2,1)} collective-permute-done((bf16[512,2048]{1,0:T(8,128)(2,1)}, bf16[512,2048]{1,0:T(8,128)(2,1)}, u32[]{:S(2)}, u32[]{:S(2)}) %collective-permute-start.5) | collective-permute-done | bytes 2097184 | tf_op jit(solution)/shard_map/ppermute | solution.py:823
  248.2 7.5 %turn_columns.6 = (bf16[1024,1024]{1,0:T(8,128)(2,1)S(1)}, bf16[1024,1024]{1,0:T(8,128)(2,1)}, s32[23]{0:T(128)S(1)}) custom-call(s32[23]{0:T(128)S(1)} %add_add_fusion.1.scalars, bf16[512,2048]{1,0:T(8,128)(2,1)} %get-tuple-element.144.refs_0_.refs_2_, bf16[512,2048]{1,0:T(8,128)(2,1)} %collective-permute-done.5.refs_1_.refs_3_, ...), custom_call_target="tpu_custom_call" | custom-call | flops 70000001024 | bytes 1 | tf_op jit(solution)/shard_map/turn_columns/pallas_call | solution.py:62
  257.0 34.6 %swiglu.2 = (bf16[1024,4096]{1,0:T(8,128)(2,1)}, bf16[1024,2048]{1,0:T(8,128)(2,1)}, s32[7]{0:T(128)S(1)}, bf16[1024,1024]{1,0:T(8,128)(2,1)}) custom-call(s32[7]{0:T(128)S(1)} %bitcast.76, bf16[512,2048]{1,0:T(8,128)(2,1)} %get-tuple-element.144.refs_0_.refs_2_, ...), custom_call_target="tpu_custom_call", output_to_operand_aliasing={{3}: (8, {})} | custom-call | flops 399999991808 | bytes 1 | tf_op jit(solution)/shard_map/swiglu/pallas_call | solution.py:62
  293.7 14.8 %contract.7 = (bf16[512,2048]{1,0:T(8,128)(2,1)S(1)}, s32[7]{0:T(128)S(1)}) custom-call(s32[7]{0:T(128)S(1)} %get-tuple-element.147.scalars, bf16[1024,4096]{1,0:T(8,128)(2,1)} %get-tuple-element.148.refs_0_.refs_1_.refs_2_.refs_3_, bf16[1024,4096]{1,0:T(8,128)(2,1)} %get-tuple-element.148.refs_0_.refs_1_.refs_2_.refs_3_, ...), custom_call_target="tpu_custom_call" | custom-call | flops 320000000000 | bytes 1 | tf_op jit(solution)/shard_map/contract/pallas_call | solution.py:62
  312.9 19.9 %weight_grad.6 = (bf16[1024,3072]{1,0:T(8,128)(2,1)}, s32[7]{0:T(128)S(1)}) custom-call(s32[7]{0:T(128)S(1)} %get-tuple-element.150.scalars, bf16[1024,1024]{1,0:T(8,128)(2,1)S(1)} %copy-done.41, bf16[1024,1024]{1,0:T(8,128)(2,1)} %collective-permute-done.7.refs_8_.refs_1_, bf16[1024,4096]{1,0:T(8,128)(2,1)} %get-tuple-element.148.refs_0_.refs_1_.refs_2_.refs_3_, ...), custom_call_target="tpu_custom_call" | custom-call | flops 190000005120 | bytes 1 | tf_op jit(solution)/shard_map/weight_grad/pallas_call | solution.py:62
  334.9 19.6 %weight_grad.7 = (bf16[512,3072]{1,0:T(8,128)(2,1)}, bf16[512,3072]{1,0:T(8,128)(2,1)}, s32[7]{0:T(128)S(1)}) custom-call(s32[7]{0:T(128)S(1)} %get-tuple-element.154.scalars, bf16[1024,1024]{1,0:T(8,128)(2,1)S(1)} %copy-done.42, bf16[1024,1024]{1,0:T(8,128)(2,1)} %collective-permute-done.7.refs_8_.refs_1_, ...), custom_call_target="tpu_custom_call" | custom-call | flops 190000005120 | bytes 1 | tf_op jit(solution)/shard_map/weight_grad/pallas_call | solution.py:62
  354.5 20.8 %swiglu.3 = (bf16[1024,2048]{1,0:T(8,128)(2,1)}, bf16[1024,1024]{1,0:T(8,128)(2,1)}, s32[7]{0:T(128)S(1)}, bf16[1024,1024]{1,0:T(8,128)(2,1)}) custom-call(s32[7]{0:T(128)S(1)} %get-tuple-element.155.scalars, bf16[512,2048]{1,0:T(8,128)(2,1)} %get-tuple-element.144.refs_0_.refs_2_, ...), custom_call_target="tpu_custom_call", output_to_operand_aliasing={{3}: (7, {})} | custom-call | flops 199999995904 | bytes 1 | tf_op jit(solution)/shard_map/swiglu/pallas_call | solution.py:62
  375.8 9.4 %contract.8 = (bf16[512,2048]{1,0:T(8,128)(2,1)}, s32[7]{0:T(128)S(1)}) custom-call(s32[7]{0:T(128)S(1)} %get-tuple-element.157.scalars, bf16[1024,2048]{1,0:T(8,128)(2,1)} %get-tuple-element.158.refs_0_.refs_1_.refs_2_.refs_4_.refs_5_, bf16[1024,2048]{1,0:T(8,128)(2,1)} %get-tuple-element.158.refs_0_.refs_1_.refs_2_.refs_4_.refs_5_, ...), custom_call_target="tpu_custom_call" | custom-call | flops 160000000000 | bytes 1 | tf_op jit(solution)/shard_map/contract/pallas_call | solution.py:62
  387.9 19.6 %weight_grad.8 = (bf16[512,3072]{1,0:T(8,128)(2,1)}, bf16[512,3072]{1,0:T(8,128)(2,1)}, s32[7]{0:T(128)S(1)}) custom-call(s32[7]{0:T(128)S(1)} %get-tuple-element.160.scalars, bf16[1024,1024]{1,0:T(8,128)(2,1)S(1)} %copy-done.43, bf16[1024,1024]{1,0:T(8,128)(2,1)} %collective-permute-done.7.refs_8_.refs_1_, ...), custom_call_target="tpu_custom_call" | custom-call | flops 190000005120 | bytes 1 | tf_op jit(solution)/shard_map/weight_grad/pallas_call | solution.py:62
  407.5 20.7 %contract.9 = (f32[512,2048]{1,0:T(8,128)S(1)}, s32[7]{0:T(128)S(1)}) custom-call(s32[7]{0:T(128)S(1)} %get-tuple-element.162.scalars, bf16[1024,4096]{1,0:T(8,128)(2,1)} %get-tuple-element.148.refs_0_.refs_1_.refs_2_.refs_3_, bf16[1024,4096]{1,0:T(8,128)(2,1)} %get-tuple-element.148.refs_0_.refs_1_.refs_2_.refs_3_, ...), custom_call_target="tpu_custom_call" | custom-call | flops 480000016384 | bytes 1 | tf_op jit(solution)/shard_map/contract/pallas_call | solution.py:62
  433.5 9.2 %norm_back.2 = (f32[512,2048]{1,0:T(8,128)}, bf16[512,2048]{1,0:T(8,128)(2,1)S(1)}, bf16[512,2048]{1,0:T(8,128)(2,1)}, f32[8,2048]{1,0:T(8,128)S(1)}, s32[7]{0:T(128)S(1)}) custom-call(s32[7]{0:T(128)S(1)} %get-tuple-element.163.scalars, f32[512,2048]{1,0:T(8,128)} %copy-done.34, bf16[512,2048]{1,0:T(8,128)(2,1)} %collective-permute-done.13.refs_1_, ...), custom_call_target="tpu_custom_call" | custom-call | flops 80000000000 | bytes 1 | tf_op jit(solution)/shard_map/norm_back/pallas_call | solution.py:62
  473.5 16.4 %attend_back.2 = (bf16[1024,1024]{1,0:T(8,128)(2,1)}, f32[8,128]{1,0:T(8,128)S(1)}, s32[7]{0:T(128)S(1)}) custom-call(s32[7]{0:T(128)S(1)} %get-tuple-element.176.scalars, f32[1024,2048]{1,0:T(8,128)} %get-tuple-element.177.refs_0_, bf16[512,512]{1,0:T(8,128)(2,1)S(1)} %get-tuple-element.178.refs_1_, bf16[512,512]{1,0:T(8,128)(2,1)} %collective-permute-done.16.refs_2_, ...), custom_call_target="tpu_custom_call" | custom-call | flops 170000007168 | bytes 1 | tf_op jit(solution)/shard_map/attend_back/pallas_call | solution.py:62
  490.0 16.5 %attend_back.3 = (bf16[1024,1024]{1,0:T(8,128)(2,1)S(1)}, f32[8,128]{1,0:T(8,128)S(1)}, s32[7]{0:T(128)S(1)}) custom-call(s32[7]{0:T(128)S(1)} %get-tuple-element.180.scalars, f32[1024,2048]{1,0:T(8,128)} %get-tuple-element.177.refs_0_, bf16[512,512]{1,0:T(8,128)(2,1)S(1)} %get-tuple-element.181.refs_1_, bf16[512,512]{1,0:T(8,128)(2,1)} %collective-permute-done.17.refs_2_, ...), custom_call_target="tpu_custom_call" | custom-call | flops 170000007168 | bytes 1 | tf_op jit(solution)/shard_map/attend_back/pallas_call | solution.py:62
  508.5 8.5 %weight_grad.9 = (bf16[512,1024]{1,0:T(8,128)(2,1)}, bf16[512,1024]{1,0:T(8,128)(2,1)S(1)}, s32[7]{0:T(128)S(1)}) custom-call(s32[7]{0:T(128)S(1)} %get-tuple-element.183.scalars, bf16[1024,1024]{1,0:T(8,128)(2,1)S(1)} %copy-done.36, bf16[1024,1024]{1,0:T(8,128)(2,1)} %collective-permute-done.2.refs_2_.refs_1_, ...), custom_call_target="tpu_custom_call" | custom-call | flops 60000002048 | bytes 1 | tf_op jit(solution)/shard_map/weight_grad/pallas_call | solution.py:62
  518.3 8.5 %weight_grad.10 = (bf16[512,1024]{1,0:T(8,128)(2,1)}, bf16[512,1024]{1,0:T(8,128)(2,1)S(1)}, s32[7]{0:T(128)S(1)}) custom-call(s32[7]{0:T(128)S(1)} %get-tuple-element.186.scalars, bf16[1024,1024]{1,0:T(8,128)(2,1)S(1)} %copy-done.36, bf16[1024,1024]{1,0:T(8,128)(2,1)} %collective-permute-done.2.refs_2_.refs_1_, bf16[1024,1024]{1,0:T(8,128)(2,1)} %copy-done.22, ...), custom_call_target="tpu_custom_call" | custom-call | flops 60000002048 | bytes 1 | tf_op jit(solution)/shard_map/weight_grad/pallas_call | solution.py:62
  541.8 20.3 %contract_both.2 = (f32[512,2048]{1,0:T(8,128)}, bf16[512,2048]{1,0:T(8,128)(2,1)}, s32[7]{0:T(128)S(1)}) custom-call(s32[7]{0:T(128)S(1)} %get-tuple-element.193.scalars, bf16[1024,2048]{1,0:T(8,128)(2,1)} %get-tuple-element.153.refs_6_.refs_0_.refs_1_, bf16[1024,2048]{1,0:T(8,128)(2,1)} %get-tuple-element.153.refs_6_.refs_0_.refs_1_, ...), custom_call_target="tpu_custom_call" | custom-call | flops 149999992832 | bytes 1 | tf_op jit(solution)/shard_map/contract_both/pallas_call | solution.py:62
  562.2 7.4 %turn_columns.7 = (bf16[1024,1024]{1,0:T(8,128)(2,1)S(1)}, bf16[1024,1024]{1,0:T(8,128)(2,1)}, s32[23]{0:T(128)S(1)}) custom-call(s32[23]{0:T(128)S(1)} %add_add_fusion.2.scalars, bf16[512,2048]{1,0:T(8,128)(2,1)} %get-tuple-element.195.refs_0_.refs_2_, bf16[512,2048]{1,0:T(8,128)(2,1)} %collective-permute-done.21.refs_1_.refs_3_, ...), custom_call_target="tpu_custom_call" | custom-call | flops 70000001024 | bytes 1 | tf_op jit(solution)/shard_map/turn_columns/pallas_call | solution.py:62
  571.0 14.3 %contract_both.3 = (f32[512,2048]{1,0:T(8,128)}, bf16[512,2048]{1,0:T(8,128)(2,1)}, s32[7]{0:T(128)S(1)}) custom-call(s32[7]{0:T(128)S(1)} %bitcast.79, bf16[1024,1024]{1,0:T(8,128)(2,1)} %get-tuple-element.185.refs_2_.refs_0_, bf16[1024,1024]{1,0:T(8,128)(2,1)} %copy-done.22, bf16[2048,3072]{1,0:T(8,128)(2,1)} %all-gather.4.cloned.1.call-done.refs_2_.refs_1_.refs_3_, ...), custom_call_target="tpu_custom_call" | custom-call | flops 99999997952 | bytes 1 | tf_op jit(solution)/shard_map/contract_both/pallas_call | solution.py:62
  606.1 8.7 %weight_grad.11 = (bf16[512,1024]{1,0:T(8,128)(2,1)}, bf16[512,1024]{1,0:T(8,128)(2,1)S(1)}, s32[7]{0:T(128)S(1)}) custom-call(s32[7]{0:T(128)S(1)} %get-tuple-element.205.scalars, bf16[1024,1024]{1,0:T(8,128)(2,1)S(1)} %copy-done.38, bf16[1024,1024]{1,0:T(8,128)(2,1)} %collective-permute-done.25.refs_1_, ...), custom_call_target="tpu_custom_call" | custom-call | flops 60000002048 | bytes 1 | tf_op jit(solution)/shard_map/weight_grad/pallas_call | solution.py:62
  616.4 12.7 %adam_mlp.1 = (f32[128,48,128]{2,1,0:T(8,128)}, f32[128,48,128]{2,1,0:T(8,128)}, f32[128,48,128]{2,1,0:T(8,128)}, f32[3072,128]{1,0:T(8,128)}, f32[3072,128]{1,0...) custom-call(s32[7]{0:T(128)S(1)} %get-tuple-element.208.scalars, f32[128,48,128]{2,1,0:T(8,128)} %bitcast.84, ...), custom_call_target="tpu_custom_call" | custom-call | flops 199999995904 | bytes 1 | tf_op jit(solution)/shard_map/adam_mlp/pallas_call | solution.py:62
  629.1 10.8 %collective-permute-done.26.refs_1_ = bf16[512,1024]{1,0:T(8,128)(2,1)} collective-permute-done((bf16[512,1024]{1,0:T(8,128)(2,1)}, bf16[512,1024]{1,0:T(8,128)(2,1)}, u32[]{:S(2)}, u32[]{:S(2)}) %collective-permute-start.26) | collective-permute-done | bytes 1048608 | tf_op jit(solution)/shard_map/ppermute | solution.py:755
  644.1 7.9 %norm_back.3 = (f32[512,2048]{1,0:T(8,128)}, f32[8,2048]{1,0:T(8,128)S(1)}, s32[7]{0:T(128)S(1)}) custom-call(s32[7]{0:T(128)S(1)} %get-tuple-element.213.scalars, f32[512,2048]{1,0:T(8,128)} %get-tuple-element.214.refs_0_, bf16[512,2048]{1,0:T(8,128)(2,1)} %collective-permute-done.27.refs_1_, bf16[512,2048]{1,0:T(8,128)(2,1)S(1)} %copy-done, ...), custom_call_target="tpu_custom_call" | custom-call | flops 1 | bytes 1 | tf_op jit(solution)/shard_map/norm_back/pallas_call | solution.py:62
  669.4 8.1 %collective-permute-done.33 = f32[34,128]{1,0:T(8,128)S(1)} collective-permute-done((f32[34,128]{1,0:T(8,128)S(1)}, f32[34,128]{1,0:T(8,128)S(1)}, u32[]{:S(2)}, u32[]{:S(2)}) %collective-permute-start.33) | collective-permute-done | bytes 17440 | tf_op jit(solution)/shard_map/ppermute | solution.py:784
  689.4 6.8 sum_rows.1
  (275 shorter events, 180.5 us)
Async XLA Ops:
  7.2 108.0 %all-gather.4.cloned.1.call-start = ((), (), s32[]{:S(2)}) async-start(), calls=%async_computation.5 | async-start | bytes 13369344 | tf_op jit(solution)/shard_map/all_gather | solution.py:829
  11.6 245.4 %all-gather.6.cloned.1.call-start = ((), (), s32[]{:S(2)}) async-start(), calls=%async_computation.6 | async-start | bytes 26738688 | tf_op jit(solution)/shard_map/all_gather | solution.py:829
  14.6 49.7 %collective-permute-start = (bf16[512,2048]{1,0:T(8,128)(2,1)}, bf16[512,2048]{1,0:T(8,128)(2,1)}, u32[]{:S(2)}, u32[]{:S(2)}) collective-permute-start(bf16[512,2048]{1,0:T(8,128)(2,1)} %fusion.2.refs_0_.refs_2_), channel_id=1, source_target_pairs={{0,1},{1,0},{2,3},{3,2},{4,5},{5,4},{6,7},{7,6},{8,9},{9,8},{10,11... | collective-permute-start | bytes 6291464 | tf_op jit(solution)/shard_map/ppermute | solution.py:823
  21.4 126.2 %collective-permute-start.1 = (bf16[512,2048]{1,0:T(8,128)(2,1)}, bf16[512,2048]{1,0:T(8,128)(2,1)}, u32[]{:S(2)}, u32[]{:S(2)}) collective-permute-start(bf16[512,2048]{1,0:T(8,128)(2,1)} %broadcast_select_fusion.refs_0_.refs_2_.refs_3_), channel_id=1, source_target_pairs={{0,1},{1,0},{2,3},{3,2},{4,5},{5,4},{6,7},{7,6},{8,9},{9,8},{10,11... | collective-permute-start | bytes 6291464 | tf_op jit(solution)/shard_map/ppermute | solution.py:823
  34.0 320.5 %all-gather.8.cloned.1.call-start = ((), (), s32[]{:S(2)}) async-start(), calls=%async_computation.7 | async-start | bytes 13369344 | tf_op jit(solution)/shard_map/all_gather | solution.py:829
  73.1 84.0 %collective-permute-start.2 = (bf16[1024,1024]{1,0:T(8,128)(2,1)}, bf16[1024,1024]{1,0:T(8,128)(2,1)}, u32[]{:S(2)}, u32[]{:S(2)}) collective-permute-start(bf16[1024,1024]{1,0:T(8,128)(2,1)} %get-tuple-element.139), channel_id=1, source_target_pairs={{0,2},{2,0},{1,3},{3,1},{4,6},{6,4},{5,7},{7,5},{8,10},{10,8},{9,1... | collective-permute-start | bytes 6291464 | tf_op jit(solution)/shard_map/ppermute | solution.py:733
  146.1 48.1 %collective-permute-start.4 = (bf16[512,2048]{1,0:T(8,128)(2,1)}, bf16[512,2048]{1,0:T(8,128)(2,1)}, u32[]{:S(2)}, u32[]{:S(2)}) collective-permute-start(bf16[512,2048]{1,0:T(8,128)(2,1)} %get-tuple-element.142), channel_id=1, source_target_pairs={{0,1},{1,0},{2,3},{3,2},{4,5},{5,4},{6,7},{7,6},{8,9},{9,8},{10,11... | collective-permute-start | bytes 6291464 | tf_op jit(solution)/shard_map/ppermute | solution.py:823
  200.9 47.3 %collective-permute-start.5 = (bf16[512,2048]{1,0:T(8,128)(2,1)}, bf16[512,2048]{1,0:T(8,128)(2,1)}, u32[]{:S(2)}, u32[]{:S(2)}) collective-permute-start(bf16[512,2048]{1,0:T(8,128)(2,1)} %get-tuple-element.144.refs_0_.refs_2_), channel_id=1, source_target_pairs={{0,1},{1,0},{2,3},{3,2},{4,5},{5,4},{6,7},{7,6},{8,9},{9,8},{10,11... | collective-permute-start | bytes 6291464 | tf_op jit(solution)/shard_map/ppermute | solution.py:823
  206.8 252.1 %reduce-scatter.6.cloned.1.call-start = ((), (), s32[]{:S(2)}) async-start(), calls=%async_computation.8 | async-start | bytes 7864320 | tf_op jit(solution)/shard_map/reduce_scatter | solution.py:761
  207.1 49.9 %collective-permute-start.6 = (bf16[1024,1024]{1,0:T(8,128)(2,1)}, bf16[1024,1024]{1,0:T(8,128)(2,1)}, u32[]{:S(2)}, u32[]{:S(2)}) collective-permute-start(bf16[1024,1024]{1,0:T(8,128)(2,1)} %copy-done.23), channel_id=1, source_target_pairs={{0,2},{2,0},{1,3},{3,1},{4,6},{6,4},{5,7},{7,5},{8,10},{10,8},{9,1... | collective-permute-start | bytes 6291464 | tf_op jit(solution)/shard_map/ppermute | solution.py:733
  257.0 36.6 %collective-permute-start.7 = (bf16[1024,1024]{1,0:T(8,128)(2,1)}, bf16[1024,1024]{1,0:T(8,128)(2,1)}, u32[]{:S(2)}, u32[]{:S(2)}) collective-permute-start(bf16[1024,1024]{1,0:T(8,128)(2,1)} %get-tuple-element.149), channel_id=1, source_target_pairs={{0,2},{2,0},{1,3},{3,1},{4,6},{6,4},{5,7},{7,5},{8,10},{10,8},{9,1... | collective-permute-start | bytes 6291464 | tf_op jit(solution)/shard_map/ppermute | solution.py:733
  291.7 62.9 %collective-permute-start.10 = (bf16[1024,1024]{1,0:T(8,128)(2,1)}, bf16[1024,1024]{1,0:T(8,128)(2,1)}, u32[]{:S(2)}, u32[]{:S(2)}) collective-permute-start(bf16[1024,1024]{1,0:T(8,128)(2,1)} %get-tuple-element.156), channel_id=1, source_target_pairs={{0,1},{1,0},{2,3},{3,2},{4,5},{5,4},{6,7},{7,6},{8,9},{9,8},{10,11... | collective-permute-start | bytes 6291464 | tf_op jit(solution)/shard_map/ppermute | solution.py:823
  293.4 19.6 %collective-permute-start.8 = (bf16[1024,4096]{1,0:T(8,128)(2,1)}, bf16[1024,4096]{1,0:T(8,128)(2,1)}, u32[]{:S(2)}, u32[]{:S(2)}) collective-permute-start(bf16[1024,4096]{1,0:T(8,128)(2,1)} %get-tuple-element.148.refs_0_.refs_1_.refs_2_.refs_3_), channel_id=1, source_target_pairs={{0,2},{2,0},{1,3},{3,1},{4,6},{6,4},{5,7},{7,5},{8,10},{10,8},{9,1... | collective-permute-start | bytes 25165832 | tf_op jit(solution)/shard_map/ppermute | solution.py:733
  332.8 197.0 %reduce-scatter.8.cloned.1.call-start = ((), (), s32[]{:S(2)}) async-start(), calls=%async_computation.9 | async-start | bytes 3932160 | tf_op jit(solution)/shard_map/reduce_scatter | solution.py:775
  385.2 48.2 %collective-permute-start.13 = (bf16[512,2048]{1,0:T(8,128)(2,1)}, bf16[512,2048]{1,0:T(8,128)(2,1)}, u32[]{:S(2)}, u32[]{:S(2)}) collective-permute-start(bf16[512,2048]{1,0:T(8,128)(2,1)} %get-tuple-element.165), channel_id=1, source_target_pairs={{0,1},{1,0},{2,3},{3,2},{4,5},{5,4},{6,7},{7,6},{8,9},{9,8},{10,11... | collective-permute-start | bytes 6291464 | tf_op jit(solution)/shard_map/ppermute | solution.py:823
  386.5 56.2 %collective-permute-start.14 = (bf16[1024,1024]{1,0:T(8,128)(2,1)}, bf16[1024,1024]{1,0:T(8,128)(2,1)}, u32[]{:S(2)}, u32[]{:S(2)}) collective-permute-start(bf16[1024,1024]{1,0:T(8,128)(2,1)} %get-tuple-element.169.refs_2_), channel_id=1, source_target_pairs={{0,2},{2,0},{1,3},{3,1},{4,6},{6,4},{5,7},{7,5},{8,10},{10,8},{9,1... | collective-permute-start | bytes 6291464 | tf_op jit(solution)/shard_map/ppermute | solution.py:733
  386.6 71.2 %collective-permute-start.15 = (bf16[512,3072]{1,0:T(8,128)(2,1)}, bf16[512,3072]{1,0:T(8,128)(2,1)}, u32[]{:S(2)}, u32[]{:S(2)}) collective-permute-start(bf16[512,3072]{1,0:T(8,128)(2,1)} %get-tuple-element.172), channel_id=1, source_target_pairs={{0,4},{4,0},{1,5},{5,1},{2,6},{6,2},{3,7},{7,3},{8,12},{12,8},{9,1... | collective-permute-start | bytes 9437192 | tf_op jit(solution)/shard_map/ppermute | solution.py:755
  448.8 24.7 %collective-permute-start.16 = (bf16[512,512]{1,0:T(8,128)(2,1)}, bf16[512,512]{1,0:T(8,128)(2,1)}, u32[]{:S(2)}, u32[]{:S(2)}) collective-permute-start(bf16[512,512]{1,0:T(8,128)(2,1)} %get-tuple-element.179), channel_id=1, source_target_pairs={{0,1},{1,0},{2,3},{3,2},{4,5},{5,4},{6,7},{7,6},{8,9},{9,8},{10,11... | collective-permute-start | bytes 1572872 | tf_op jit(solution)/shard_map/ppermute | solution.py:823
  450.1 39.8 %collective-permute-start.17 = (bf16[512,512]{1,0:T(8,128)(2,1)}, bf16[512,512]{1,0:T(8,128)(2,1)}, u32[]{:S(2)}, u32[]{:S(2)}) collective-permute-start(bf16[512,512]{1,0:T(8,128)(2,1)} %get-tuple-element.182), channel_id=1, source_target_pairs={{0,1},{1,0},{2,3},{3,2},{4,5},{5,4},{6,7},{7,6},{8,9},{9,8},{10,11... | collective-permute-start | bytes 1572872 | tf_op jit(solution)/shard_map/ppermute | solution.py:823
  450.9 78.9 %collective-permute-start.20 = (bf16[512,3072]{1,0:T(8,128)(2,1)}, bf16[512,3072]{1,0:T(8,128)(2,1)}, u32[]{:S(2)}, u32[]{:S(2)}) collective-permute-start(bf16[512,3072]{1,0:T(8,128)(2,1)} %get-tuple-element.190), channel_id=1, source_target_pairs={{0,4},{4,0},{1,5},{5,1},{2,6},{6,2},{3,7},{7,3},{8,12},{12,8},{9,1... | collective-permute-start | bytes 9437192 | tf_op jit(solution)/shard_map/ppermute | solution.py:755
  466.8 130.8 %reduce-scatter.10.cloned.1.call-start = ((), (), s32[]{:S(2)}) async-start(), calls=%async_computation.10 | async-start | bytes 3932160 | tf_op jit(solution)/shard_map/reduce_scatter | solution.py:775
  489.9 18.6 %collective-permute-start.18 = (bf16[1024,1024]{1,0:T(8,128)(2,1)}, bf16[1024,1024]{1,0:T(8,128)(2,1)}, u32[]{:S(2)}, u32[]{:S(2)}) collective-permute-start(bf16[1024,1024]{1,0:T(8,128)(2,1)} %get-tuple-element.185.refs_2_.refs_0_), channel_id=1, source_target_pairs={{0,2},{2,0},{1,3},{3,1},{4,6},{6,4},{5,7},{7,5},{8,10},{10,8},{9,1... | collective-permute-start | bytes 6291464 | tf_op jit(solution)/shard_map/ppermute | solution.py:733
  507.0 55.2 %collective-permute-start.21 = (bf16[512,2048]{1,0:T(8,128)(2,1)}, bf16[512,2048]{1,0:T(8,128)(2,1)}, u32[]{:S(2)}, u32[]{:S(2)}) collective-permute-start(bf16[512,2048]{1,0:T(8,128)(2,1)} %get-tuple-element.195.refs_0_.refs_2_), channel_id=1, source_target_pairs={{0,1},{1,0},{2,3},{3,2},{4,5},{5,4},{6,7},{7,6},{8,9},{9,8},{10,11... | collective-permute-start | bytes 6291464 | tf_op jit(solution)/shard_map/ppermute | solution.py:823
  527.8 68.3 %collective-permute-start.24 = (bf16[512,1024]{1,0:T(8,128)(2,1)}, bf16[512,1024]{1,0:T(8,128)(2,1)}, u32[]{:S(2)}, u32[]{:S(2)}) collective-permute-start(bf16[512,1024]{1,0:T(8,128)(2,1)} %get-tuple-element.203), channel_id=1, source_target_pairs={{0,4},{4,0},{1,5},{5,1},{2,6},{6,2},{3,7},{7,3},{8,12},{12,8},{9,1... | collective-permute-start | bytes 3145736 | tf_op jit(solution)/shard_map/ppermute | solution.py:755
  529.3 66.8 %collective-permute-start.23 = (bf16[512,1024]{1,0:T(8,128)(2,1)}, bf16[512,1024]{1,0:T(8,128)(2,1)}, u32[]{:S(2)}, u32[]{:S(2)}) collective-permute-start(bf16[512,1024]{1,0:T(8,128)(2,1)} %get-tuple-element.201), channel_id=1, source_target_pairs={{0,4},{4,0},{1,5},{5,1},{2,6},{6,2},{3,7},{7,3},{8,12},{12,8},{9,1... | collective-permute-start | bytes 3145736 | tf_op jit(solution)/shard_map/ppermute | solution.py:755
  537.3 141.5 %reduce-scatter.12.cloned.1.call-start = ((), (), s32[]{:S(2)}) async-start(), calls=%async_computation.11 | async-start | bytes 2621440 | tf_op jit(solution)/shard_map/reduce_scatter | solution.py:775
  540.3 52.0 %collective-permute-start.22 = (bf16[128,3072]{1,0:T(8,128)(2,1)}, bf16[128,3072]{1,0:T(8,128)(2,1)}, u32[]{:S(2)}, u32[]{:S(2)}) collective-permute-start(bf16[128,3072]{1,0:T(8,128)(2,1)} %get-tuple-element.198), channel_id=1, source_target_pairs={{0,4},{4,0},{1,5},{5,1},{2,6},{6,2},{3,7},{7,3},{8,12},{12,8},{9,1... | collective-permute-start | bytes 2359304 | tf_op jit(solution)/shard_map/ppermute | solution.py:766
  585.2 58.8 %collective-permute-start.27 = (bf16[512,2048]{1,0:T(8,128)(2,1)}, bf16[512,2048]{1,0:T(8,128)(2,1)}, u32[]{:S(2)}, u32[]{:S(2)}) collective-permute-start(bf16[512,2048]{1,0:T(8,128)(2,1)} %get-tuple-element.215), channel_id=1, source_target_pairs={{0,1},{1,0},{2,3},{3,2},{4,5},{5,4},{6,7},{7,6},{8,9},{9,8},{10,11... | collective-permute-start | bytes 6291464 | tf_op jit(solution)/shard_map/ppermute | solution.py:823
  586.0 18.5 %collective-permute-start.25 = (bf16[1024,1024]{1,0:T(8,128)(2,1)}, bf16[1024,1024]{1,0:T(8,128)(2,1)}, u32[]{:S(2)}, u32[]{:S(2)}) collective-permute-start(bf16[1024,1024]{1,0:T(8,128)(2,1)} %get-tuple-element.207), channel_id=1, source_target_pairs={{0,2},{2,0},{1,3},{3,1},{4,6},{6,4},{5,7},{7,5},{8,10},{10,8},{9,1... | collective-permute-start | bytes 6291464 | tf_op jit(solution)/shard_map/ppermute | solution.py:733
  592.3 97.1 %collective-permute-start.28 = (bf16[512,2048]{1,0:T(8,128)(2,1)}, bf16[512,2048]{1,0:T(8,128)(2,1)}, u32[]{:S(2)}, u32[]{:S(2)}) collective-permute-start(bf16[512,2048]{1,0:T(8,128)(2,1)} %get-tuple-element.221), channel_id=1, source_target_pairs={{0,1},{1,0},{2,3},{3,2},{4,5},{5,4},{6,7},{7,6},{8,9},{9,8},{10,11... | collective-permute-start | bytes 6291464 | tf_op jit(solution)/shard_map/ppermute | solution.py:823
  604.4 91.7 %reduce-scatter.14.cloned.1.call-start = ((), (), s32[]{:S(2)}) async-start(), calls=%async_computation.12 | async-start | bytes 1310720 | tf_op jit(solution)/shard_map/reduce_scatter | solution.py:775
  614.8 25.1 %collective-permute-start.26 = (bf16[512,1024]{1,0:T(8,128)(2,1)}, bf16[512,1024]{1,0:T(8,128)(2,1)}, u32[]{:S(2)}, u32[]{:S(2)}) collective-permute-start(bf16[512,1024]{1,0:T(8,128)(2,1)} %get-tuple-element.212), channel_id=1, source_target_pairs={{0,4},{4,0},{1,5},{5,1},{2,6},{6,2},{3,7},{7,3},{8,12},{12,8},{9,1... | collective-permute-start | bytes 3145736 | tf_op jit(solution)/shard_map/ppermute | solution.py:755
  (75 other events, 775.4 us)
Sparse Core Ops, SparseCore 0:
  11.7 103.4 all-gather.3
  117.4 126.7 all-gather.5
  247.1 100.7 all-gather.7
  350.0 108.9 reduce-scatter.5
  466.9 60.7 reduce-scatter.7
  537.5 60.0 reduce-scatter.9
  604.5 43.8 reduce-scatter.11
  650.9 27.3 reduce-scatter.13

commit v3 on v2

--- a/solution.py
+++ b/solution.py
@@ -593,7 +593,7 @@
         flat,
         after=after,
         work=5,
-        name="add_pairs",
+        vmem=62, name="add_pairs",
     )[0]
 
 
@@ -605,7 +605,7 @@
     rows, width = array.shape
     block = pl.BlockSpec((rows // 2, width), lambda j, s: (0, 0))
     return order.call(
-        take_kernel, (1,), [block], [(block, shaped((rows // 2, width), array.dtype))], [array], work=2, name="take_rows"
+        take_kernel, (1,), [block], [(block, shaped((rows // 2, width), array.dtype))], [array], work=2, vmem=62, name="take_rows"
     )[0]
 
 
@@ -633,7 +633,7 @@
         [(queries, shaped(query[0].shape, F32))] * 3 + [(pair, shaped(keyval[0].shape, F32))] * 3,
         (*query, *keyval, sums),
         work=5,
-        name="adam_qkv",
+        vmem=62, name="adam_qkv",
     )
 
 
@@ -653,7 +653,7 @@
         [(block, shaped(weights[0].shape, F32))] * 3,
         (*weights, sums),
         work=3,
-        name="adam_out",
+        vmem=62, name="adam_out",
     )
 
 
@@ -962,11 +962,11 @@
         (wide_rate, RATE_SCALE * FF ** (-0.5)),
     )
     out_sum = summer.finish(out_grad)
+    qkv_new = adam_qkv(
+        order, (w_query, query_mean, query_square), (w_keyval, keyval_mean, keyval_square), qkv_sum, heads, wide_rate
+    )
     order.rate = 0
     tokens_grad, g_first_gain = norm_back(order, 0, d_first, d_first_sent, tokens, d_middle, norm_gains, 0)
-    qkv_new = adam_qkv(
-        order, (w_query, query_mean, query_square), (w_keyval, keyval_mean, keyval_square), qkv_sum, heads, wide_rate
-    )
     layer_out = sum_rows(order, middle, out_here, out_sent)
     out_new = adam_out(order, (w_out, out_mean, out_square), out_sum, RATE_SCALE * OUT_FAN ** (-0.5))
     g_head = g_head_a + g_head_b

time: 714 us -> 704 us (0.986)
  local copies, waits for them, and re-layouts: 56.6 us -> 45.4 us
  Pallas kernels: 403 us -> 412 us
    unnamed x133 -> x117, local copies, waits for them, and re-layouts: 47.3 us -> 35.4 us
    pallas_call x37, Pallas kernels: 403 us -> 412 us  [call(): pl.pallas_call(run, grid_spec=pltpu.PrefetchScalarGridSpec(num_scalar_pre...]
    ppermute x5, waiting for transfers between devices: 18.7 us -> 10.2 us  [everywhere(): values = values + lax.ppermute(values, axis, pairs)]
  transfers between devices with their start and end apart: 42 -> 42, of which waited for: 16 -> 15; matrix products, arithmetic and copies ran while one was open for 4% -> 4% of each run, Pallas kernels for 57% -> 59%
where the time goes in v3:
time: 704 us; the launch traced here: 699 us
  Pallas kernels  412 us (59%)
  waiting for transfers between devices  183 us (26%)
  local copies, waits for them, and re-layouts  45.4 us (6%)
  starting transfers between devices  28.1 us (4%)
  between operations  16.6 us (2%)
  other arithmetic  13.9 us (2%)
    pallas_call x37, Pallas kernels, call(): pl.pallas_call(run, grid_spec=pltpu.PrefetchScalarGridSpec(num_scalar_pre...  412 us
    ppermute x11, waiting for transfers between devices, swap(): return lax.ppermute(piece, 'tensor', [(0, 1), (1, 0)])  97.6 us
    all_gather x3, waiting for transfers between devices, gather(): return lax.all_gather(shard, axes, axis=0, tiled=True)  42.2 us
    unnamed x117, local copies, waits for them, and re-layouts  35.4 us
    ppermute x5, waiting for transfers between devices, grad(): return (keep, lax.ppermute(near, self.axes[1], [(0, 1), (1, 0)]))  14.3 us
  transfers between devices with their start and end apart: 42, of which 15 were waited for; matrix products, arithmetic and copies ran while one was open for 4% of the time, Pallas kernels for 59%

profile of v3, /device:TPU:0, one launch (start us, length us, event | category | flops | bytes accessed | tf_op | source)
XLA Modules:
  0.0 698.5 jit_solution(12523095950906079615)
XLA Ops:
  37.1 27.2 %collective-permute-done.refs_1_.refs_3_ = bf16[512,2048]{1,0:T(8,128)(2,1)} collective-permute-done((bf16[512,2048]{1,0:T(8,128)(2,1)}, bf16[512,2048]{1,0:T(8,128)(2,1)}, u32[]{:S(2)}, u32[]{:S(2)}) %collective-permute-start) | collective-permute-done | bytes 2097184 | tf_op jit(solution)/shard_map/ppermute | solution.py:823
  64.3 7.4 %turn_columns.4 = (bf16[1024,1024]{1,0:T(8,128)(2,1)S(1)}, bf16[1024,1024]{1,0:T(8,128)(2,1)}, s32[23]{0:T(128)S(1)}) custom-call(s32[23]{0:T(128)S(1)} %concatenate.30.scalars, bf16[512,2048]{1,0:T(8,128)(2,1)} %fusion.2.refs_0_.refs_2_, bf16[512,2048]{1,0:T(8,128)(2,1)} %collective-permute-done.refs_1_.refs_3_, bf16[512,2048]{1,0:T(8,128)(2,1)} %fusion.2.refs_0_.refs_2_, ...), custom_call_target="tpu_custom_call" | custom-call | flops 70000001024 | bytes 1 | tf_op jit(solution)/shard_map/turn_columns/pallas_call | solution.py:62
  73.1 42.2 %all-gather.4.cloned.1.call-done.refs_2_.refs_1_.refs_3_ = bf16[2048,3072]{1,0:T(8,128)(2,1)} async-done(((bf16[128,3072]{1,0:T(8,128)(2,1)}), bf16[2048,3072]{1,0:T(8,128)(2,1)}) %all-gather.4.cloned.1.call-update) | async-done | bytes 12582928 | tf_op jit(solution)/shard_map/all_gather | solution.py:829
  115.2 23.9 %attend.1 = (f32[1024,2048]{1,0:T(8,128)}, bf16[1024,1024]{1,0:T(8,128)(2,1)}, s32[7]{0:T(128)S(1)}) custom-call(s32[7]{0:T(128)S(1)} %bitcast.77, bf16[512,2048]{1,0:T(8,128)(2,1)} %fusion.2.refs_0_.refs_2_, bf16[512,2048]{1,0:T(8,128)(2,1)} %collective-permute-done.refs_1_.refs_3_, bf16[2048,3072]{1,0:T(8,128)(2,1)} %all-gather.4.cloned.1.call-done.refs_2_.refs_1_.refs_3_, ...), custom_call_target="tpu_custom_call" | custom-call | flops 240000008192 | bytes 1 | tf_op jit(solution)/shard_map/attend/pallas_call | solution.py:62
  147.6 6.7 turn_columns.5
  157.1 7.0 %contract.6 = (f32[512,2048]{1,0:T(8,128)}, s32[7]{0:T(128)S(1)}) custom-call(s32[7]{0:T(128)S(1)} %bitcast.78, bf16[1024,1024]{1,0:T(8,128)(2,1)} %get-tuple-element.136.refs_0_.refs_2_, bf16[2048,3072]{1,0:T(8,128)(2,1)} %all-gather.4.cloned.1.call-done.refs_2_.refs_1_.refs_3_, bf16[1024,1024]{1,0:T(8,128)(2,1)} %collective-permute-done.2.refs_2_.refs_1_, ...), custom_call_target="tpu_custom_call" | custom-call | flops 80000000000 | bytes 1 | tf_op jit(solution)/shard_map/contract/pallas_call | solution.py:62
  164.1 30.1 %collective-permute-done.4.refs_2_ = bf16[512,2048]{1,0:T(8,128)(2,1)} collective-permute-done((bf16[512,2048]{1,0:T(8,128)(2,1)}, bf16[512,2048]{1,0:T(8,128)(2,1)}, u32[]{:S(2)}, u32[]{:S(2)}) %collective-permute-start.4) | collective-permute-done | bytes 2097184 | tf_op jit(solution)/shard_map/ppermute | solution.py:823
  194.2 6.7 middle_rows.1
  211.8 36.4 %collective-permute-done.5.refs_1_.refs_3_ = bf16[512,2048]{1,0:T(8,128)(2,1)} collective-permute-done((bf16[512,2048]{1,0:T(8,128)(2,1)}, bf16[512,2048]{1,0:T(8,128)(2,1)}, u32[]{:S(2)}, u32[]{:S(2)}) %collective-permute-start.5) | collective-permute-done | bytes 2097184 | tf_op jit(solution)/shard_map/ppermute | solution.py:823
  248.2 7.5 %turn_columns.6 = (bf16[1024,1024]{1,0:T(8,128)(2,1)S(1)}, bf16[1024,1024]{1,0:T(8,128)(2,1)}, s32[23]{0:T(128)S(1)}) custom-call(s32[23]{0:T(128)S(1)} %add_add_fusion.1.scalars, bf16[512,2048]{1,0:T(8,128)(2,1)} %get-tuple-element.144.refs_0_.refs_2_, bf16[512,2048]{1,0:T(8,128)(2,1)} %collective-permute-done.5.refs_1_.refs_3_, ...), custom_call_target="tpu_custom_call" | custom-call | flops 70000001024 | bytes 1 | tf_op jit(solution)/shard_map/turn_columns/pallas_call | solution.py:62
  257.0 34.7 %swiglu.2 = (bf16[1024,4096]{1,0:T(8,128)(2,1)}, bf16[1024,2048]{1,0:T(8,128)(2,1)}, s32[7]{0:T(128)S(1)}, bf16[1024,1024]{1,0:T(8,128)(2,1)}) custom-call(s32[7]{0:T(128)S(1)} %bitcast.76, bf16[512,2048]{1,0:T(8,128)(2,1)} %get-tuple-element.144.refs_0_.refs_2_, ...), custom_call_target="tpu_custom_call", output_to_operand_aliasing={{3}: (8, {})} | custom-call | flops 399999991808 | bytes 1 | tf_op jit(solution)/shard_map/swiglu/pallas_call | solution.py:62
  293.7 14.8 %contract.7 = (bf16[512,2048]{1,0:T(8,128)(2,1)S(1)}, s32[7]{0:T(128)S(1)}) custom-call(s32[7]{0:T(128)S(1)} %get-tuple-element.147.scalars, bf16[1024,4096]{1,0:T(8,128)(2,1)} %get-tuple-element.148.refs_0_.refs_1_.refs_2_.refs_3_, bf16[1024,4096]{1,0:T(8,128)(2,1)} %get-tuple-element.148.refs_0_.refs_1_.refs_2_.refs_3_, ...), custom_call_target="tpu_custom_call" | custom-call | flops 320000000000 | bytes 1 | tf_op jit(solution)/shard_map/contract/pallas_call | solution.py:62
  312.9 19.7 %weight_grad.6 = (bf16[1024,3072]{1,0:T(8,128)(2,1)}, s32[7]{0:T(128)S(1)}) custom-call(s32[7]{0:T(128)S(1)} %get-tuple-element.150.scalars, bf16[1024,1024]{1,0:T(8,128)(2,1)S(1)} %copy-done.25, bf16[1024,1024]{1,0:T(8,128)(2,1)} %collective-permute-done.7.refs_8_.refs_1_, bf16[1024,4096]{1,0:T(8,128)(2,1)} %get-tuple-element.148.refs_0_.refs_1_.refs_2_.refs_3_, ...), custom_call_target="tpu_custom_call" | custom-call | flops 190000005120 | bytes 1 | tf_op jit(solution)/shard_map/weight_grad/pallas_call | solution.py:62
  333.2 19.7 %weight_grad.7 = (bf16[512,3072]{1,0:T(8,128)(2,1)}, bf16[512,3072]{1,0:T(8,128)(2,1)}, s32[7]{0:T(128)S(1)}) custom-call(s32[7]{0:T(128)S(1)} %get-tuple-element.154.scalars, bf16[1024,1024]{1,0:T(8,128)(2,1)S(1)} %copy-done.25, bf16[1024,1024]{1,0:T(8,128)(2,1)} %collective-permute-done.7.refs_8_.refs_1_, ...), custom_call_target="tpu_custom_call" | custom-call | flops 190000005120 | bytes 1 | tf_op jit(solution)/shard_map/weight_grad/pallas_call | solution.py:62
  352.9 21.5 %swiglu.3 = (bf16[1024,2048]{1,0:T(8,128)(2,1)}, bf16[1024,1024]{1,0:T(8,128)(2,1)}, s32[7]{0:T(128)S(1)}, bf16[1024,1024]{1,0:T(8,128)(2,1)}) custom-call(s32[7]{0:T(128)S(1)} %get-tuple-element.155.scalars, bf16[512,2048]{1,0:T(8,128)(2,1)} %get-tuple-element.144.refs_0_.refs_2_, ...), custom_call_target="tpu_custom_call", output_to_operand_aliasing={{3}: (7, {})} | custom-call | flops 199999995904 | bytes 1 | tf_op jit(solution)/shard_map/swiglu/pallas_call | solution.py:62
  375.0 9.4 %contract.8 = (bf16[512,2048]{1,0:T(8,128)(2,1)}, s32[7]{0:T(128)S(1)}) custom-call(s32[7]{0:T(128)S(1)} %get-tuple-element.157.scalars, bf16[1024,2048]{1,0:T(8,128)(2,1)} %get-tuple-element.158.refs_0_.refs_1_.refs_2_.refs_4_.refs_5_, bf16[1024,2048]{1,0:T(8,128)(2,1)} %get-tuple-element.158.refs_0_.refs_1_.refs_2_.refs_4_.refs_5_, ...), custom_call_target="tpu_custom_call" | custom-call | flops 160000000000 | bytes 1 | tf_op jit(solution)/shard_map/contract/pallas_call | solution.py:62
  386.3 19.6 %weight_grad.8 = (bf16[512,3072]{1,0:T(8,128)(2,1)}, bf16[512,3072]{1,0:T(8,128)(2,1)}, s32[7]{0:T(128)S(1)}) custom-call(s32[7]{0:T(128)S(1)} %get-tuple-element.160.scalars, bf16[1024,1024]{1,0:T(8,128)(2,1)S(1)} %copy-done.25, bf16[1024,1024]{1,0:T(8,128)(2,1)} %collective-permute-done.7.refs_8_.refs_1_, ...), custom_call_target="tpu_custom_call" | custom-call | flops 190000005120 | bytes 1 | tf_op jit(solution)/shard_map/weight_grad/pallas_call | solution.py:62
  405.8 20.7 %contract.9 = (f32[512,2048]{1,0:T(8,128)S(1)}, s32[7]{0:T(128)S(1)}) custom-call(s32[7]{0:T(128)S(1)} %get-tuple-element.162.scalars, bf16[1024,4096]{1,0:T(8,128)(2,1)} %get-tuple-element.148.refs_0_.refs_1_.refs_2_.refs_3_, bf16[1024,4096]{1,0:T(8,128)(2,1)} %get-tuple-element.148.refs_0_.refs_1_.refs_2_.refs_3_, ...), custom_call_target="tpu_custom_call" | custom-call | flops 480000016384 | bytes 1 | tf_op jit(solution)/shard_map/contract/pallas_call | solution.py:62
  432.4 9.3 %norm_back.2 = (f32[512,2048]{1,0:T(8,128)}, bf16[512,2048]{1,0:T(8,128)(2,1)S(1)}, bf16[512,2048]{1,0:T(8,128)(2,1)}, f32[8,2048]{1,0:T(8,128)S(1)}, s32[7]{0:T(128)S(1)}) custom-call(s32[7]{0:T(128)S(1)} %get-tuple-element.163.scalars, f32[512,2048]{1,0:T(8,128)} %copy-done.18, bf16[512,2048]{1,0:T(8,128)(2,1)} %collective-permute-done.13.refs_1_, ...), custom_call_target="tpu_custom_call" | custom-call | flops 80000000000 | bytes 1 | tf_op jit(solution)/shard_map/norm_back/pallas_call | solution.py:62
  472.1 16.4 %attend_back.2 = (bf16[1024,1024]{1,0:T(8,128)(2,1)}, f32[8,128]{1,0:T(8,128)S(1)}, s32[7]{0:T(128)S(1)}) custom-call(s32[7]{0:T(128)S(1)} %get-tuple-element.176.scalars, f32[1024,2048]{1,0:T(8,128)} %get-tuple-element.177.refs_0_, bf16[512,512]{1,0:T(8,128)(2,1)S(1)} %get-tuple-element.178.refs_1_, bf16[512,512]{1,0:T(8,128)(2,1)S(1)} %collective-permute-done.16.refs_2_, ...), custom_call_target="tpu_custom_call" | custom-call | flops 170000007168 | bytes 1 | tf_op jit(solution)/shard_map/attend_back/pallas_call | solution.py:62
  488.5 16.5 %attend_back.3 = (bf16[1024,1024]{1,0:T(8,128)(2,1)S(1)}, f32[8,128]{1,0:T(8,128)S(1)}, s32[7]{0:T(128)S(1)}) custom-call(s32[7]{0:T(128)S(1)} %get-tuple-element.180.scalars, f32[1024,2048]{1,0:T(8,128)} %get-tuple-element.177.refs_0_, bf16[512,512]{1,0:T(8,128)(2,1)S(1)} %get-tuple-element.181.refs_1_, bf16[512,512]{1,0:T(8,128)(2,1)} %collective-permute-done.17.refs_2_, ...), custom_call_target="tpu_custom_call" | custom-call | flops 170000007168 | bytes 1 | tf_op jit(solution)/shard_map/attend_back/pallas_call | solution.py:62
  507.6 8.5 %weight_grad.9 = (bf16[512,1024]{1,0:T(8,128)(2,1)}, bf16[512,1024]{1,0:T(8,128)(2,1)S(1)}, s32[7]{0:T(128)S(1)}) custom-call(s32[7]{0:T(128)S(1)} %get-tuple-element.183.scalars, bf16[1024,1024]{1,0:T(8,128)(2,1)S(1)} %copy-done.20, bf16[1024,1024]{1,0:T(8,128)(2,1)} %collective-permute-done.2.refs_2_.refs_1_, ...), custom_call_target="tpu_custom_call" | custom-call | flops 60000002048 | bytes 1 | tf_op jit(solution)/shard_map/weight_grad/pallas_call | solution.py:62
  518.4 8.5 %weight_grad.10 = (bf16[512,1024]{1,0:T(8,128)(2,1)}, bf16[512,1024]{1,0:T(8,128)(2,1)S(1)}, s32[7]{0:T(128)S(1)}) custom-call(s32[7]{0:T(128)S(1)} %get-tuple-element.186.scalars, bf16[1024,1024]{1,0:T(8,128)(2,1)S(1)} %copy-done.20, bf16[1024,1024]{1,0:T(8,128)(2,1)} %collective-permute-done.2.refs_2_.refs_1_, bf16[1024,1024]{1,0:T(8,128)(2,1)} %copy-done.10, ...), custom_call_target="tpu_custom_call" | custom-call | flops 60000002048 | bytes 1 | tf_op jit(solution)/shard_map/weight_grad/pallas_call | solution.py:62
  541.2 20.0 %contract_both.2 = (f32[512,2048]{1,0:T(8,128)}, bf16[512,2048]{1,0:T(8,128)(2,1)}, s32[7]{0:T(128)S(1)}) custom-call(s32[7]{0:T(128)S(1)} %copy-done.32, bf16[1024,2048]{1,0:T(8,128)(2,1)} %get-tuple-element.153.refs_6_.refs_0_.refs_1_, bf16[1024,2048]{1,0:T(8,128)(2,1)} %get-tuple-element.153.refs_6_.refs_0_.refs_1_, ...), custom_call_target="tpu_custom_call" | custom-call | flops 149999992832 | bytes 1 | tf_op jit(solution)/shard_map/contract_both/pallas_call | solution.py:62
  561.3 7.4 %turn_columns.7 = (bf16[1024,1024]{1,0:T(8,128)(2,1)S(1)}, bf16[1024,1024]{1,0:T(8,128)(2,1)}, s32[23]{0:T(128)S(1)}) custom-call(s32[23]{0:T(128)S(1)} %add_add_fusion.2.scalars, bf16[512,2048]{1,0:T(8,128)(2,1)} %get-tuple-element.195.refs_0_.refs_2_, bf16[512,2048]{1,0:T(8,128)(2,1)} %collective-permute-done.21.refs_1_.refs_3_, ...), custom_call_target="tpu_custom_call" | custom-call | flops 70000001024 | bytes 1 | tf_op jit(solution)/shard_map/turn_columns/pallas_call | solution.py:62
  570.0 14.3 %contract_both.3 = (f32[512,2048]{1,0:T(8,128)}, bf16[512,2048]{1,0:T(8,128)(2,1)}, s32[7]{0:T(128)S(1)}) custom-call(s32[7]{0:T(128)S(1)} %bitcast.79, bf16[1024,1024]{1,0:T(8,128)(2,1)} %get-tuple-element.185.refs_2_.refs_0_, bf16[1024,1024]{1,0:T(8,128)(2,1)} %copy-done.10, bf16[2048,3072]{1,0:T(8,128)(2,1)} %all-gather.4.cloned.1.call-done.refs_2_.refs_1_.refs_3_, ...), custom_call_target="tpu_custom_call" | custom-call | flops 99999997952 | bytes 1 | tf_op jit(solution)/shard_map/contract_both/pallas_call | solution.py:62
  585.8 7.1 %collective-permute-done.22.refs_1_ = bf16[128,3072]{1,0:T(8,128)(2,1)} collective-permute-done((bf16[128,3072]{1,0:T(8,128)(2,1)}, bf16[128,3072]{1,0:T(8,128)(2,1)}, u32[]{:S(2)}, u32[]{:S(2)}) %collective-permute-start.22) | collective-permute-done | bytes 786464 | tf_op jit(solution)/shard_map/ppermute | solution.py:766
  603.4 8.8 %weight_grad.11 = (bf16[512,1024]{1,0:T(8,128)(2,1)}, bf16[512,1024]{1,0:T(8,128)(2,1)S(1)}, s32[7]{0:T(128)S(1)}) custom-call(s32[7]{0:T(128)S(1)} %copy-done.36, bf16[1024,1024]{1,0:T(8,128)(2,1)S(1)} %copy-done.22, bf16[1024,1024]{1,0:T(8,128)(2,1)} %collective-permute-done.25.refs_1_, bf16[1024,1024]{1,0:T(8,128)(2,1)} %get-tuple-element.136.refs_0_.refs_2_, ...), custom_call_target="tpu_custom_call" | custom-call | flops 60000002048 | bytes 1 | tf_op jit(solution)/shard_map/weight_grad/pallas_call | solution.py:62
  613.7 12.8 %adam_mlp.1 = (f32[128,48,128]{2,1,0:T(8,128)}, f32[128,48,128]{2,1,0:T(8,128)}, f32[128,48,128]{2,1,0:T(8,128)}, f32[3072,128]{1,0:T(8,128)}, f32[3072,128]{1,0...) custom-call(s32[7]{0:T(128)S(1)} %get-tuple-element.208.scalars, f32[128,48,128]{2,1,0:T(8,128)} %bitcast.84, ...), custom_call_target="tpu_custom_call" | custom-call | flops 199999995904 | bytes 1 | tf_op jit(solution)/shard_map/adam_mlp/pallas_call | solution.py:62
  627.1 9.6 %collective-permute-done.26.refs_1_ = bf16[512,1024]{1,0:T(8,128)(2,1)} collective-permute-done((bf16[512,1024]{1,0:T(8,128)(2,1)}, bf16[512,1024]{1,0:T(8,128)(2,1)}, u32[]{:S(2)}, u32[]{:S(2)}) %collective-permute-start.26) | collective-permute-done | bytes 1048608 | tf_op jit(solution)/shard_map/ppermute | solution.py:755
  655.2 7.9 %norm_back.3 = (f32[512,2048]{1,0:T(8,128)}, f32[8,2048]{1,0:T(8,128)S(1)}, s32[7]{0:T(128)S(1)}) custom-call(s32[7]{0:T(128)S(1)} %copy-done.8, f32[512,2048]{1,0:T(8,128)} %get-tuple-element.216.refs_0_, bf16[512,2048]{1,0:T(8,128)(2,1)} %collective-permute-done.27.refs_1_, bf16[512,2048]{1,0:T(8,128)(2,1)S(1)} %copy-done.1, ...), custom_call_target="tpu_custom_call" | custom-call | flops 1 | bytes 1 | tf_op jit(solution)/shard_map/norm_back/pallas_call | solution.py:62
  678.0 6.8 sum_rows.1
  (259 shorter events, 172.9 us)
Async XLA Ops:
  7.2 108.0 %all-gather.4.cloned.1.call-start = ((), (), s32[]{:S(2)}) async-start(), calls=%async_computation.5 | async-start | bytes 13369344 | tf_op jit(solution)/shard_map/all_gather | solution.py:829
  11.6 245.4 %all-gather.6.cloned.1.call-start = ((), (), s32[]{:S(2)}) async-start(), calls=%async_computation.6 | async-start | bytes 26738688 | tf_op jit(solution)/shard_map/all_gather | solution.py:829
  14.6 49.7 %collective-permute-start = (bf16[512,2048]{1,0:T(8,128)(2,1)}, bf16[512,2048]{1,0:T(8,128)(2,1)}, u32[]{:S(2)}, u32[]{:S(2)}) collective-permute-start(bf16[512,2048]{1,0:T(8,128)(2,1)} %fusion.2.refs_0_.refs_2_), channel_id=1, source_target_pairs={{0,1},{1,0},{2,3},{3,2},{4,5},{5,4},{6,7},{7,6},{8,9},{9,8},{10,11... | collective-permute-start | bytes 6291464 | tf_op jit(solution)/shard_map/ppermute | solution.py:823
  21.5 126.2 %collective-permute-start.1 = (bf16[512,2048]{1,0:T(8,128)(2,1)}, bf16[512,2048]{1,0:T(8,128)(2,1)}, u32[]{:S(2)}, u32[]{:S(2)}) collective-permute-start(bf16[512,2048]{1,0:T(8,128)(2,1)} %broadcast_select_fusion.refs_0_.refs_2_.refs_3_), channel_id=1, source_target_pairs={{0,1},{1,0},{2,3},{3,2},{4,5},{5,4},{6,7},{7,6},{8,9},{9,8},{10,11... | collective-permute-start | bytes 6291464 | tf_op jit(solution)/shard_map/ppermute | solution.py:823
  34.0 318.9 %all-gather.8.cloned.1.call-start = ((), (), s32[]{:S(2)}) async-start(), calls=%async_computation.7 | async-start | bytes 13369344 | tf_op jit(solution)/shard_map/all_gather | solution.py:829
  73.1 84.0 %collective-permute-start.2 = (bf16[1024,1024]{1,0:T(8,128)(2,1)}, bf16[1024,1024]{1,0:T(8,128)(2,1)}, u32[]{:S(2)}, u32[]{:S(2)}) collective-permute-start(bf16[1024,1024]{1,0:T(8,128)(2,1)} %get-tuple-element.139), channel_id=1, source_target_pairs={{0,2},{2,0},{1,3},{3,1},{4,6},{6,4},{5,7},{7,5},{8,10},{10,8},{9,1... | collective-permute-start | bytes 6291464 | tf_op jit(solution)/shard_map/ppermute | solution.py:733
  139.1 17.9 %collective-permute-start.3 = (bf16[1024,1024]{1,0:T(8,128)(2,1)}, bf16[1024,1024]{1,0:T(8,128)(2,1)}, u32[]{:S(2)}, u32[]{:S(2)}) collective-permute-start(bf16[1024,1024]{1,0:T(8,128)(2,1)} %get-tuple-element.136.refs_0_.refs_2_), channel_id=1, source_target_pairs={{0,2},{2,0},{1,3},{3,1},{4,6},{6,4},{5,7},{7,5},{8,10},{10,8},{9,1... | collective-permute-start | bytes 6291464 | tf_op jit(solution)/shard_map/ppermute | solution.py:733
  146.1 48.1 %collective-permute-start.4 = (bf16[512,2048]{1,0:T(8,128)(2,1)}, bf16[512,2048]{1,0:T(8,128)(2,1)}, u32[]{:S(2)}, u32[]{:S(2)}) collective-permute-start(bf16[512,2048]{1,0:T(8,128)(2,1)} %get-tuple-element.142), channel_id=1, source_target_pairs={{0,1},{1,0},{2,3},{3,2},{4,5},{5,4},{6,7},{7,6},{8,9},{9,8},{10,11... | collective-permute-start | bytes 6291464 | tf_op jit(solution)/shard_map/ppermute | solution.py:823
  200.9 47.3 %collective-permute-start.5 = (bf16[512,2048]{1,0:T(8,128)(2,1)}, bf16[512,2048]{1,0:T(8,128)(2,1)}, u32[]{:S(2)}, u32[]{:S(2)}) collective-permute-start(bf16[512,2048]{1,0:T(8,128)(2,1)} %get-tuple-element.144.refs_0_.refs_2_), channel_id=1, source_target_pairs={{0,1},{1,0},{2,3},{3,2},{4,5},{5,4},{6,7},{7,6},{8,9},{9,8},{10,11... | collective-permute-start | bytes 6291464 | tf_op jit(solution)/shard_map/ppermute | solution.py:823
  206.8 252.1 %reduce-scatter.6.cloned.1.call-start = ((), (), s32[]{:S(2)}) async-start(), calls=%async_computation.8 | async-start | bytes 7864320 | tf_op jit(solution)/shard_map/reduce_scatter | solution.py:761
  207.2 49.8 %collective-permute-start.6 = (bf16[1024,1024]{1,0:T(8,128)(2,1)S(1)}, bf16[1024,1024]{1,0:T(8,128)(2,1)}, u32[]{:S(2)}, u32[]{:S(2)}) collective-permute-start(bf16[1024,1024]{1,0:T(8,128)(2,1)S(1)} %copy-done.12), channel_id=1, source_target_pairs={{0,2},{2,0},{1,3},{3,1},{4,6},{6,4},{5,7},{7,5},{8,10},{10,8},{9,1... | collective-permute-start | bytes 6291464 | tf_op jit(solution)/shard_map/ppermute | solution.py:733
  257.0 36.7 %collective-permute-start.7 = (bf16[1024,1024]{1,0:T(8,128)(2,1)}, bf16[1024,1024]{1,0:T(8,128)(2,1)}, u32[]{:S(2)}, u32[]{:S(2)}) collective-permute-start(bf16[1024,1024]{1,0:T(8,128)(2,1)} %get-tuple-element.149), channel_id=1, source_target_pairs={{0,2},{2,0},{1,3},{3,1},{4,6},{6,4},{5,7},{7,5},{8,10},{10,8},{9,1... | collective-permute-start | bytes 6291464 | tf_op jit(solution)/shard_map/ppermute | solution.py:733
  291.7 61.3 %collective-permute-start.10 = (bf16[1024,1024]{1,0:T(8,128)(2,1)}, bf16[1024,1024]{1,0:T(8,128)(2,1)}, u32[]{:S(2)}, u32[]{:S(2)}) collective-permute-start(bf16[1024,1024]{1,0:T(8,128)(2,1)} %get-tuple-element.156), channel_id=1, source_target_pairs={{0,1},{1,0},{2,3},{3,2},{4,5},{5,4},{6,7},{7,6},{8,9},{9,8},{10,11... | collective-permute-start | bytes 6291464 | tf_op jit(solution)/shard_map/ppermute | solution.py:823
  293.4 19.5 %collective-permute-start.8 = (bf16[1024,4096]{1,0:T(8,128)(2,1)}, bf16[1024,4096]{1,0:T(8,128)(2,1)}, u32[]{:S(2)}, u32[]{:S(2)}) collective-permute-start(bf16[1024,4096]{1,0:T(8,128)(2,1)} %get-tuple-element.148.refs_0_.refs_1_.refs_2_.refs_3_), channel_id=1, source_target_pairs={{0,2},{2,0},{1,3},{3,1},{4,6},{6,4},{5,7},{7,5},{8,10},{10,8},{9,1... | collective-permute-start | bytes 25165832 | tf_op jit(solution)/shard_map/ppermute | solution.py:733
  332.7 197.7 %reduce-scatter.8.cloned.1.call-start = ((), (), s32[]{:S(2)}) async-start(), calls=%async_computation.9 | async-start | bytes 3932160 | tf_op jit(solution)/shard_map/reduce_scatter | solution.py:775
  384.3 48.0 %collective-permute-start.13 = (bf16[512,2048]{1,0:T(8,128)(2,1)}, bf16[512,2048]{1,0:T(8,128)(2,1)}, u32[]{:S(2)}, u32[]{:S(2)}) collective-permute-start(bf16[512,2048]{1,0:T(8,128)(2,1)} %get-tuple-element.165), channel_id=1, source_target_pairs={{0,1},{1,0},{2,3},{3,2},{4,5},{5,4},{6,7},{7,6},{8,9},{9,8},{10,11... | collective-permute-start | bytes 6291464 | tf_op jit(solution)/shard_map/ppermute | solution.py:823
  384.9 57.5 %collective-permute-start.14 = (bf16[1024,1024]{1,0:T(8,128)(2,1)}, bf16[1024,1024]{1,0:T(8,128)(2,1)}, u32[]{:S(2)}, u32[]{:S(2)}) collective-permute-start(bf16[1024,1024]{1,0:T(8,128)(2,1)} %get-tuple-element.169.refs_2_), channel_id=1, source_target_pairs={{0,2},{2,0},{1,3},{3,1},{4,6},{6,4},{5,7},{7,5},{8,10},{10,8},{9,1... | collective-permute-start | bytes 6291464 | tf_op jit(solution)/shard_map/ppermute | solution.py:733
  384.9 71.2 %collective-permute-start.15 = (bf16[512,3072]{1,0:T(8,128)(2,1)}, bf16[512,3072]{1,0:T(8,128)(2,1)}, u32[]{:S(2)}, u32[]{:S(2)}) collective-permute-start(bf16[512,3072]{1,0:T(8,128)(2,1)} %get-tuple-element.172), channel_id=1, source_target_pairs={{0,4},{4,0},{1,5},{5,1},{2,6},{6,2},{3,7},{7,3},{8,12},{12,8},{9,1... | collective-permute-start | bytes 9437192 | tf_op jit(solution)/shard_map/ppermute | solution.py:755
  448.8 23.2 %collective-permute-start.16 = (bf16[512,512]{1,0:T(8,128)(2,1)}, bf16[512,512]{1,0:T(8,128)(2,1)S(1)}, u32[]{:S(2)}, u32[]{:S(2)}) collective-permute-start(bf16[512,512]{1,0:T(8,128)(2,1)} %get-tuple-element.179), channel_id=1, source_target_pairs={{0,1},{1,0},{2,3},{3,2},{4,5},{5,4},{6,7},{7,6},{8,9},{9,8},{10,11... | collective-permute-start | bytes 1572872 | tf_op jit(solution)/shard_map/ppermute | solution.py:823
  449.3 39.2 %collective-permute-start.17 = (bf16[512,512]{1,0:T(8,128)(2,1)}, bf16[512,512]{1,0:T(8,128)(2,1)}, u32[]{:S(2)}, u32[]{:S(2)}) collective-permute-start(bf16[512,512]{1,0:T(8,128)(2,1)} %get-tuple-element.182), channel_id=1, source_target_pairs={{0,1},{1,0},{2,3},{3,2},{4,5},{5,4},{6,7},{7,6},{8,9},{9,8},{10,11... | collective-permute-start | bytes 1572872 | tf_op jit(solution)/shard_map/ppermute | solution.py:823
  450.8 79.5 %collective-permute-start.20 = (bf16[512,3072]{1,0:T(8,128)(2,1)}, bf16[512,3072]{1,0:T(8,128)(2,1)}, u32[]{:S(2)}, u32[]{:S(2)}) collective-permute-start(bf16[512,3072]{1,0:T(8,128)(2,1)} %get-tuple-element.190), channel_id=1, source_target_pairs={{0,4},{4,0},{1,5},{5,1},{2,6},{6,2},{3,7},{7,3},{8,12},{12,8},{9,1... | collective-permute-start | bytes 9437192 | tf_op jit(solution)/shard_map/ppermute | solution.py:755
  464.8 132.1 %reduce-scatter.10.cloned.1.call-start = ((), (), s32[]{:S(2)}) async-start(), calls=%async_computation.10 | async-start | bytes 3932160 | tf_op jit(solution)/shard_map/reduce_scatter | solution.py:775
  488.5 19.1 %collective-permute-start.18 = (bf16[1024,1024]{1,0:T(8,128)(2,1)}, bf16[1024,1024]{1,0:T(8,128)(2,1)}, u32[]{:S(2)}, u32[]{:S(2)}) collective-permute-start(bf16[1024,1024]{1,0:T(8,128)(2,1)} %get-tuple-element.185.refs_2_.refs_0_), channel_id=1, source_target_pairs={{0,2},{2,0},{1,3},{3,1},{4,6},{6,4},{5,7},{7,5},{8,10},{10,8},{9,1... | collective-permute-start | bytes 6291464 | tf_op jit(solution)/shard_map/ppermute | solution.py:733
  505.6 55.7 %collective-permute-start.21 = (bf16[512,2048]{1,0:T(8,128)(2,1)}, bf16[512,2048]{1,0:T(8,128)(2,1)}, u32[]{:S(2)}, u32[]{:S(2)}) collective-permute-start(bf16[512,2048]{1,0:T(8,128)(2,1)} %get-tuple-element.195.refs_0_.refs_2_), channel_id=1, source_target_pairs={{0,1},{1,0},{2,3},{3,2},{4,5},{5,4},{6,7},{7,6},{8,9},{9,8},{10,11... | collective-permute-start | bytes 6291464 | tf_op jit(solution)/shard_map/ppermute | solution.py:823
  528.4 68.4 %collective-permute-start.24 = (bf16[512,1024]{1,0:T(8,128)(2,1)}, bf16[512,1024]{1,0:T(8,128)(2,1)}, u32[]{:S(2)}, u32[]{:S(2)}) collective-permute-start(bf16[512,1024]{1,0:T(8,128)(2,1)} %get-tuple-element.203), channel_id=1, source_target_pairs={{0,4},{4,0},{1,5},{5,1},{2,6},{6,2},{3,7},{7,3},{8,12},{12,8},{9,1... | collective-permute-start | bytes 3145736 | tf_op jit(solution)/shard_map/ppermute | solution.py:755
  529.8 67.0 %collective-permute-start.23 = (bf16[512,1024]{1,0:T(8,128)(2,1)}, bf16[512,1024]{1,0:T(8,128)(2,1)}, u32[]{:S(2)}, u32[]{:S(2)}) collective-permute-start(bf16[512,1024]{1,0:T(8,128)(2,1)} %get-tuple-element.201), channel_id=1, source_target_pairs={{0,4},{4,0},{1,5},{5,1},{2,6},{6,2},{3,7},{7,3},{8,12},{12,8},{9,1... | collective-permute-start | bytes 3145736 | tf_op jit(solution)/shard_map/ppermute | solution.py:755
  536.2 109.9 %reduce-scatter.12.cloned.1.call-start = ((), (), s32[]{:S(2)}) async-start(), calls=%async_computation.11 | async-start | bytes 2621440 | tf_op jit(solution)/shard_map/reduce_scatter | solution.py:775
  539.0 53.9 %collective-permute-start.22 = (bf16[128,3072]{1,0:T(8,128)(2,1)}, bf16[128,3072]{1,0:T(8,128)(2,1)}, u32[]{:S(2)}, u32[]{:S(2)}) collective-permute-start(bf16[128,3072]{1,0:T(8,128)(2,1)} %get-tuple-element.198), channel_id=1, source_target_pairs={{0,4},{4,0},{1,5},{5,1},{2,6},{6,2},{3,7},{7,3},{8,12},{12,8},{9,1... | collective-permute-start | bytes 2359304 | tf_op jit(solution)/shard_map/ppermute | solution.py:766
  584.8 67.9 %collective-permute-start.27 = (bf16[512,2048]{1,0:T(8,128)(2,1)}, bf16[512,2048]{1,0:T(8,128)(2,1)}, u32[]{:S(2)}, u32[]{:S(2)}) collective-permute-start(bf16[512,2048]{1,0:T(8,128)(2,1)} %get-tuple-element.217), channel_id=1, source_target_pairs={{0,1},{1,0},{2,3},{3,2},{4,5},{5,4},{6,7},{7,6},{8,9},{9,8},{10,11... | collective-permute-start | bytes 6291464 | tf_op jit(solution)/shard_map/ppermute | solution.py:823
  592.9 85.1 %collective-permute-start.28 = (bf16[512,2048]{1,0:T(8,128)(2,1)}, bf16[512,2048]{1,0:T(8,128)(2,1)}, u32[]{:S(2)}, u32[]{:S(2)}) collective-permute-start(bf16[512,2048]{1,0:T(8,128)(2,1)} %get-tuple-element.221), channel_id=1, source_target_pairs={{0,1},{1,0},{2,3},{3,2},{4,5},{5,4},{6,7},{7,6},{8,9},{9,8},{10,11... | collective-permute-start | bytes 6291464 | tf_op jit(solution)/shard_map/ppermute | solution.py:823
  601.8 83.0 %reduce-scatter.14.cloned.1.call-start = ((), (), s32[]{:S(2)}) async-start(), calls=%async_computation.12 | async-start | bytes 1310720 | tf_op jit(solution)/shard_map/reduce_scatter | solution.py:775
  612.2 24.4 %collective-permute-start.26 = (bf16[512,1024]{1,0:T(8,128)(2,1)}, bf16[512,1024]{1,0:T(8,128)(2,1)}, u32[]{:S(2)}, u32[]{:S(2)}) collective-permute-start(bf16[512,1024]{1,0:T(8,128)(2,1)} %get-tuple-element.212), channel_id=1, source_target_pairs={{0,4},{4,0},{1,5},{5,1},{2,6},{6,2},{3,7},{7,3},{8,12},{12,8},{9,1... | collective-permute-start | bytes 3145736 | tf_op jit(solution)/shard_map/ppermute | solution.py:755
  (67 other events, 567.8 us)
Sparse Core Ops, SparseCore 0:
  11.7 103.4 all-gather.3
  117.4 126.7 all-gather.5
  247.1 100.7 all-gather.7
  350.0 108.9 reduce-scatter.5
  464.9 60.7 reduce-scatter.7
  536.3 59.8 reduce-scatter.9
  601.9 44.1 reduce-scatter.11
  648.5 26.9 reduce-scatter.13

commit v4 on v3

--- a/solution.py
+++ b/solution.py
@@ -923,11 +923,11 @@
 
     there_a, there_b = project(order, branch_own, out_other, out_cols)
     sent_a, sent_b = swap(there_a), swap(there_b)
-    mlp_sums = [summer.finish(mlp_grads[0], after=[line_sum])]
     here_a, here_b, branch_again = project(
         order, branch_own, [(early, qkv_cols // out_cols, FIRST)], out_cols, [branch_again]
     )
     branch_other = swap(branch_again)
+    mlp_sums = [summer.finish(mlp_grads[0], after=[line_sum])]
 
     def attention_back(half, here, sent, after=(), through=()):
         span = (half * heads // 2, heads // 2)

time: 704 us -> 703 us (level)
    unnamed x117 -> x121, local copies, waits for them, and re-layouts: 35.4 us -> 35.8 us
where the time goes in v4:
time: 703 us; the launch traced here: 697 us
  Pallas kernels  412 us (59%)
  waiting for transfers between devices  180 us (26%)
  local copies, waits for them, and re-layouts  45.6 us (6%)
  starting transfers between devices  28.5 us (4%)
  between operations  16.6 us (2%)
  other arithmetic  14 us (2%)
    pallas_call x37, Pallas kernels, call(): pl.pallas_call(run, grid_spec=pltpu.PrefetchScalarGridSpec(num_scalar_pre...  412 us
    ppermute x11, waiting for transfers between devices, swap(): return lax.ppermute(piece, 'tensor', [(0, 1), (1, 0)])  97.8 us
    all_gather x3, waiting for transfers between devices, gather(): return lax.all_gather(shard, axes, axis=0, tiled=True)  42.2 us
    unnamed x121, local copies, waits for them, and re-layouts  35.8 us
    ppermute x5, waiting for transfers between devices, grad(): return (keep, lax.ppermute(near, self.axes[1], [(0, 1), (1, 0)]))  16.4 us
  transfers between devices with their start and end apart: 42, of which 15 were waited for; matrix products, arithmetic and copies ran while one was open for 4% of the time, Pallas kernels for 59%

profile of v4, /device:TPU:0, one launch (start us, length us, event | category | flops | bytes accessed | tf_op | source)
XLA Modules:
  0.0 697.3 jit_solution(1571403784996669482)
XLA Ops:
  37.1 27.2 %collective-permute-done.refs_1_.refs_3_ = bf16[512,2048]{1,0:T(8,128)(2,1)} collective-permute-done((bf16[512,2048]{1,0:T(8,128)(2,1)}, bf16[512,2048]{1,0:T(8,128)(2,1)}, u32[]{:S(2)}, u32[]{:S(2)}) %collective-permute-start) | collective-permute-done | bytes 2097184 | tf_op jit(solution)/shard_map/ppermute | solution.py:823
  64.3 7.4 %turn_columns.4 = (bf16[1024,1024]{1,0:T(8,128)(2,1)S(1)}, bf16[1024,1024]{1,0:T(8,128)(2,1)}, s32[23]{0:T(128)S(1)}) custom-call(s32[23]{0:T(128)S(1)} %concatenate.30.scalars, bf16[512,2048]{1,0:T(8,128)(2,1)} %fusion.2.refs_0_.refs_2_, bf16[512,2048]{1,0:T(8,128)(2,1)} %collective-permute-done.refs_1_.refs_3_, bf16[512,2048]{1,0:T(8,128)(2,1)} %fusion.2.refs_0_.refs_2_, ...), custom_call_target="tpu_custom_call" | custom-call | flops 70000001024 | bytes 1 | tf_op jit(solution)/shard_map/turn_columns/pallas_call | solution.py:62
  73.1 42.2 %all-gather.4.cloned.1.call-done.refs_2_.refs_1_.refs_3_ = bf16[2048,3072]{1,0:T(8,128)(2,1)} async-done(((bf16[128,3072]{1,0:T(8,128)(2,1)}), bf16[2048,3072]{1,0:T(8,128)(2,1)}) %all-gather.4.cloned.1.call-update) | async-done | bytes 12582928 | tf_op jit(solution)/shard_map/all_gather | solution.py:829
  115.2 23.9 %attend.1 = (f32[1024,2048]{1,0:T(8,128)}, bf16[1024,1024]{1,0:T(8,128)(2,1)}, s32[7]{0:T(128)S(1)}) custom-call(s32[7]{0:T(128)S(1)} %bitcast.77, bf16[512,2048]{1,0:T(8,128)(2,1)} %fusion.2.refs_0_.refs_2_, bf16[512,2048]{1,0:T(8,128)(2,1)} %collective-permute-done.refs_1_.refs_3_, bf16[2048,3072]{1,0:T(8,128)(2,1)} %all-gather.4.cloned.1.call-done.refs_2_.refs_1_.refs_3_, ...), custom_call_target="tpu_custom_call" | custom-call | flops 240000008192 | bytes 1 | tf_op jit(solution)/shard_map/attend/pallas_call | solution.py:62
  139.4 6.7 contract.5
  147.6 6.7 turn_columns.5
  157.0 7.0 %contract.6 = (f32[512,2048]{1,0:T(8,128)}, s32[7]{0:T(128)S(1)}) custom-call(s32[7]{0:T(128)S(1)} %bitcast.78, bf16[1024,1024]{1,0:T(8,128)(2,1)} %get-tuple-element.136.refs_0_.refs_2_, bf16[2048,3072]{1,0:T(8,128)(2,1)} %all-gather.4.cloned.1.call-done.refs_2_.refs_1_.refs_3_, bf16[1024,1024]{1,0:T(8,128)(2,1)} %collective-permute-done.2.refs_2_.refs_1_, ...), custom_call_target="tpu_custom_call" | custom-call | flops 80000000000 | bytes 1 | tf_op jit(solution)/shard_map/contract/pallas_call | solution.py:62
  164.0 30.1 %collective-permute-done.4.refs_2_ = bf16[512,2048]{1,0:T(8,128)(2,1)} collective-permute-done((bf16[512,2048]{1,0:T(8,128)(2,1)}, bf16[512,2048]{1,0:T(8,128)(2,1)}, u32[]{:S(2)}, u32[]{:S(2)}) %collective-permute-start.4) | collective-permute-done | bytes 2097184 | tf_op jit(solution)/shard_map/ppermute | solution.py:823
  194.2 6.7 middle_rows.1
  211.8 36.4 %collective-permute-done.5.refs_1_.refs_3_ = bf16[512,2048]{1,0:T(8,128)(2,1)} collective-permute-done((bf16[512,2048]{1,0:T(8,128)(2,1)}, bf16[512,2048]{1,0:T(8,128)(2,1)}, u32[]{:S(2)}, u32[]{:S(2)}) %collective-permute-start.5) | collective-permute-done | bytes 2097184 | tf_op jit(solution)/shard_map/ppermute | solution.py:823
  248.2 7.5 %turn_columns.6 = (bf16[1024,1024]{1,0:T(8,128)(2,1)S(1)}, bf16[1024,1024]{1,0:T(8,128)(2,1)}, s32[23]{0:T(128)S(1)}) custom-call(s32[23]{0:T(128)S(1)} %add_add_fusion.1.scalars, bf16[512,2048]{1,0:T(8,128)(2,1)} %get-tuple-element.144.refs_0_.refs_2_, bf16[512,2048]{1,0:T(8,128)(2,1)} %collective-permute-done.5.refs_1_.refs_3_, ...), custom_call_target="tpu_custom_call" | custom-call | flops 70000001024 | bytes 1 | tf_op jit(solution)/shard_map/turn_columns/pallas_call | solution.py:62
  257.0 34.8 %swiglu.2 = (bf16[1024,4096]{1,0:T(8,128)(2,1)}, bf16[1024,2048]{1,0:T(8,128)(2,1)}, s32[7]{0:T(128)S(1)}, bf16[1024,1024]{1,0:T(8,128)(2,1)}) custom-call(s32[7]{0:T(128)S(1)} %bitcast.76, bf16[512,2048]{1,0:T(8,128)(2,1)} %get-tuple-element.144.refs_0_.refs_2_, ...), custom_call_target="tpu_custom_call", output_to_operand_aliasing={{3}: (8, {})} | custom-call | flops 399999991808 | bytes 1 | tf_op jit(solution)/shard_map/swiglu/pallas_call | solution.py:62
  293.8 14.8 %contract.7 = (bf16[512,2048]{1,0:T(8,128)(2,1)S(1)}, s32[7]{0:T(128)S(1)}) custom-call(s32[7]{0:T(128)S(1)} %get-tuple-element.147.scalars, bf16[1024,4096]{1,0:T(8,128)(2,1)} %get-tuple-element.148.refs_0_.refs_1_.refs_2_.refs_3_, bf16[1024,4096]{1,0:T(8,128)(2,1)} %get-tuple-element.148.refs_0_.refs_1_.refs_2_.refs_3_, ...), custom_call_target="tpu_custom_call" | custom-call | flops 320000000000 | bytes 1 | tf_op jit(solution)/shard_map/contract/pallas_call | solution.py:62
  313.2 19.7 %weight_grad.6 = (bf16[1024,3072]{1,0:T(8,128)(2,1)}, s32[7]{0:T(128)S(1)}) custom-call(s32[7]{0:T(128)S(1)} %get-tuple-element.150.scalars, bf16[1024,1024]{1,0:T(8,128)(2,1)S(1)} %copy-done.23, bf16[1024,1024]{1,0:T(8,128)(2,1)} %collective-permute-done.7.refs_8_.refs_1_, bf16[1024,4096]{1,0:T(8,128)(2,1)} %get-tuple-element.148.refs_0_.refs_1_.refs_2_.refs_3_, ...), custom_call_target="tpu_custom_call" | custom-call | flops 190000005120 | bytes 1 | tf_op jit(solution)/shard_map/weight_grad/pallas_call | solution.py:62
  333.4 19.7 %weight_grad.7 = (bf16[512,3072]{1,0:T(8,128)(2,1)}, bf16[512,3072]{1,0:T(8,128)(2,1)}, s32[7]{0:T(128)S(1)}) custom-call(s32[7]{0:T(128)S(1)} %get-tuple-element.154.scalars, bf16[1024,1024]{1,0:T(8,128)(2,1)S(1)} %copy-done.23, bf16[1024,1024]{1,0:T(8,128)(2,1)} %collective-permute-done.7.refs_8_.refs_1_, ...), custom_call_target="tpu_custom_call" | custom-call | flops 190000005120 | bytes 1 | tf_op jit(solution)/shard_map/weight_grad/pallas_call | solution.py:62
  353.2 21.5 %swiglu.3 = (bf16[1024,2048]{1,0:T(8,128)(2,1)}, bf16[1024,1024]{1,0:T(8,128)(2,1)}, s32[7]{0:T(128)S(1)}, bf16[1024,1024]{1,0:T(8,128)(2,1)}) custom-call(s32[7]{0:T(128)S(1)} %get-tuple-element.155.scalars, bf16[512,2048]{1,0:T(8,128)(2,1)} %get-tuple-element.144.refs_0_.refs_2_, ...), custom_call_target="tpu_custom_call", output_to_operand_aliasing={{3}: (7, {})} | custom-call | flops 199999995904 | bytes 1 | tf_op jit(solution)/shard_map/swiglu/pallas_call | solution.py:62
  375.1 9.4 %contract.8 = (bf16[512,2048]{1,0:T(8,128)(2,1)}, s32[7]{0:T(128)S(1)}) custom-call(s32[7]{0:T(128)S(1)} %get-tuple-element.157.scalars, bf16[1024,2048]{1,0:T(8,128)(2,1)} %get-tuple-element.158.refs_0_.refs_1_.refs_2_.refs_4_.refs_5_, bf16[1024,2048]{1,0:T(8,128)(2,1)} %get-tuple-element.158.refs_0_.refs_1_.refs_2_.refs_4_.refs_5_, ...), custom_call_target="tpu_custom_call" | custom-call | flops 160000000000 | bytes 1 | tf_op jit(solution)/shard_map/contract/pallas_call | solution.py:62
  386.2 19.6 %weight_grad.8 = (bf16[512,3072]{1,0:T(8,128)(2,1)}, bf16[512,3072]{1,0:T(8,128)(2,1)}, s32[7]{0:T(128)S(1)}) custom-call(s32[7]{0:T(128)S(1)} %get-tuple-element.160.scalars, bf16[1024,1024]{1,0:T(8,128)(2,1)S(1)} %copy-done.23, bf16[1024,1024]{1,0:T(8,128)(2,1)} %collective-permute-done.7.refs_8_.refs_1_, ...), custom_call_target="tpu_custom_call" | custom-call | flops 190000005120 | bytes 1 | tf_op jit(solution)/shard_map/weight_grad/pallas_call | solution.py:62
  405.8 20.7 %contract.9 = (f32[512,2048]{1,0:T(8,128)S(1)}, s32[7]{0:T(128)S(1)}) custom-call(s32[7]{0:T(128)S(1)} %get-tuple-element.162.scalars, bf16[1024,4096]{1,0:T(8,128)(2,1)} %get-tuple-element.148.refs_0_.refs_1_.refs_2_.refs_3_, bf16[1024,4096]{1,0:T(8,128)(2,1)} %get-tuple-element.148.refs_0_.refs_1_.refs_2_.refs_3_, ...), custom_call_target="tpu_custom_call" | custom-call | flops 480000016384 | bytes 1 | tf_op jit(solution)/shard_map/contract/pallas_call | solution.py:62
  432.5 9.3 %norm_back.2 = (f32[512,2048]{1,0:T(8,128)}, bf16[512,2048]{1,0:T(8,128)(2,1)S(1)}, bf16[512,2048]{1,0:T(8,128)(2,1)}, f32[8,2048]{1,0:T(8,128)S(1)}, s32[7]{0:T(128)S(1)}) custom-call(s32[7]{0:T(128)S(1)} %get-tuple-element.163.scalars, f32[512,2048]{1,0:T(8,128)} %copy-done.16, bf16[512,2048]{1,0:T(8,128)(2,1)} %collective-permute-done.13.refs_1_, ...), custom_call_target="tpu_custom_call" | custom-call | flops 80000000000 | bytes 1 | tf_op jit(solution)/shard_map/norm_back/pallas_call | solution.py:62
  466.3 16.4 %attend_back.2 = (bf16[1024,1024]{1,0:T(8,128)(2,1)}, f32[8,128]{1,0:T(8,128)S(1)}, s32[7]{0:T(128)S(1)}) custom-call(s32[7]{0:T(128)S(1)} %copy-done.36, f32[1024,2048]{1,0:T(8,128)} %get-tuple-element.177.refs_0_, bf16[512,512]{1,0:T(8,128)(2,1)S(1)} %copy-done.31, bf16[512,512]{1,0:T(8,128)(2,1)S(1)} %collective-permute-done.16.refs_2_, ...), custom_call_target="tpu_custom_call" | custom-call | flops 170000007168 | bytes 1 | tf_op jit(solution)/shard_map/attend_back/pallas_call | solution.py:62
  482.7 16.5 %attend_back.3 = (bf16[1024,1024]{1,0:T(8,128)(2,1)S(1)}, f32[8,128]{1,0:T(8,128)S(1)}, s32[7]{0:T(128)S(1)}) custom-call(s32[7]{0:T(128)S(1)} %get-tuple-element.180.scalars, f32[1024,2048]{1,0:T(8,128)} %get-tuple-element.177.refs_0_, bf16[512,512]{1,0:T(8,128)(2,1)S(1)} %copy-done.29, bf16[512,512]{1,0:T(8,128)(2,1)} %collective-permute-done.17.refs_2_, ...), custom_call_target="tpu_custom_call" | custom-call | flops 170000007168 | bytes 1 | tf_op jit(solution)/shard_map/attend_back/pallas_call | solution.py:62
  500.5 8.6 %weight_grad.9 = (bf16[512,1024]{1,0:T(8,128)(2,1)}, bf16[512,1024]{1,0:T(8,128)(2,1)S(1)}, s32[7]{0:T(128)S(1)}) custom-call(s32[7]{0:T(128)S(1)} %get-tuple-element.183.scalars, bf16[1024,1024]{1,0:T(8,128)(2,1)S(1)} %copy-done.18, bf16[1024,1024]{1,0:T(8,128)(2,1)} %collective-permute-done.2.refs_2_.refs_1_, ...), custom_call_target="tpu_custom_call" | custom-call | flops 60000002048 | bytes 1 | tf_op jit(solution)/shard_map/weight_grad/pallas_call | solution.py:62
  511.3 8.6 %weight_grad.10 = (bf16[512,1024]{1,0:T(8,128)(2,1)}, bf16[512,1024]{1,0:T(8,128)(2,1)S(1)}, s32[7]{0:T(128)S(1)}) custom-call(s32[7]{0:T(128)S(1)} %get-tuple-element.186.scalars, bf16[1024,1024]{1,0:T(8,128)(2,1)S(1)} %copy-done.18, bf16[1024,1024]{1,0:T(8,128)(2,1)} %collective-permute-done.2.refs_2_.refs_1_, bf16[1024,1024]{1,0:T(8,128)(2,1)} %copy-done.10, ...), custom_call_target="tpu_custom_call" | custom-call | flops 60000002048 | bytes 1 | tf_op jit(solution)/shard_map/weight_grad/pallas_call | solution.py:62
  540.1 20.2 %contract_both.2 = (f32[512,2048]{1,0:T(8,128)}, bf16[512,2048]{1,0:T(8,128)(2,1)}, s32[7]{0:T(128)S(1)}) custom-call(s32[7]{0:T(128)S(1)} %copy-done.34, bf16[1024,2048]{1,0:T(8,128)(2,1)} %get-tuple-element.153.refs_6_.refs_0_.refs_1_, bf16[1024,2048]{1,0:T(8,128)(2,1)} %get-tuple-element.153.refs_6_.refs_0_.refs_1_, ...), custom_call_target="tpu_custom_call" | custom-call | flops 149999992832 | bytes 1 | tf_op jit(solution)/shard_map/contract_both/pallas_call | solution.py:62
  560.5 7.4 %turn_columns.7 = (bf16[1024,1024]{1,0:T(8,128)(2,1)S(1)}, bf16[1024,1024]{1,0:T(8,128)(2,1)}, s32[23]{0:T(128)S(1)}) custom-call(s32[23]{0:T(128)S(1)} %add_add_fusion.2.scalars, bf16[512,2048]{1,0:T(8,128)(2,1)} %get-tuple-element.195.refs_0_.refs_2_, bf16[512,2048]{1,0:T(8,128)(2,1)} %collective-permute-done.21.refs_1_.refs_3_, ...), custom_call_target="tpu_custom_call" | custom-call | flops 70000001024 | bytes 1 | tf_op jit(solution)/shard_map/turn_columns/pallas_call | solution.py:62
  569.2 14.3 %contract_both.3 = (f32[512,2048]{1,0:T(8,128)}, bf16[512,2048]{1,0:T(8,128)(2,1)}, s32[7]{0:T(128)S(1)}) custom-call(s32[7]{0:T(128)S(1)} %bitcast.79, bf16[1024,1024]{1,0:T(8,128)(2,1)} %get-tuple-element.185.refs_2_.refs_0_, bf16[1024,1024]{1,0:T(8,128)(2,1)} %copy-done.10, bf16[2048,3072]{1,0:T(8,128)(2,1)} %all-gather.4.cloned.1.call-done.refs_2_.refs_1_.refs_3_, ...), custom_call_target="tpu_custom_call" | custom-call | flops 99999997952 | bytes 1 | tf_op jit(solution)/shard_map/contract_both/pallas_call | solution.py:62
  602.2 8.8 %weight_grad.11 = (bf16[512,1024]{1,0:T(8,128)(2,1)}, bf16[512,1024]{1,0:T(8,128)(2,1)S(1)}, s32[7]{0:T(128)S(1)}) custom-call(s32[7]{0:T(128)S(1)} %copy-done.38, bf16[1024,1024]{1,0:T(8,128)(2,1)S(1)} %copy-done.20, bf16[1024,1024]{1,0:T(8,128)(2,1)} %collective-permute-done.25.refs_1_, bf16[1024,1024]{1,0:T(8,128)(2,1)} %get-tuple-element.136.refs_0_.refs_2_, ...), custom_call_target="tpu_custom_call" | custom-call | flops 60000002048 | bytes 1 | tf_op jit(solution)/shard_map/weight_grad/pallas_call | solution.py:62
  612.5 12.7 %adam_mlp.1 = (f32[128,48,128]{2,1,0:T(8,128)}, f32[128,48,128]{2,1,0:T(8,128)}, f32[128,48,128]{2,1,0:T(8,128)}, f32[3072,128]{1,0:T(8,128)}, f32[3072,128]{1,0...) custom-call(s32[7]{0:T(128)S(1)} %get-tuple-element.208.scalars, f32[128,48,128]{2,1,0:T(8,128)} %bitcast.84, ...), custom_call_target="tpu_custom_call" | custom-call | flops 199999995904 | bytes 1 | tf_op jit(solution)/shard_map/adam_mlp/pallas_call | solution.py:62
  625.8 10.3 %collective-permute-done.26.refs_1_ = bf16[512,1024]{1,0:T(8,128)(2,1)} collective-permute-done((bf16[512,1024]{1,0:T(8,128)(2,1)}, bf16[512,1024]{1,0:T(8,128)(2,1)}, u32[]{:S(2)}, u32[]{:S(2)}) %collective-permute-start.26) | collective-permute-done | bytes 1048608 | tf_op jit(solution)/shard_map/ppermute | solution.py:755
  653.7 7.9 %norm_back.3 = (f32[512,2048]{1,0:T(8,128)}, f32[8,2048]{1,0:T(8,128)S(1)}, s32[7]{0:T(128)S(1)}) custom-call(s32[7]{0:T(128)S(1)} %copy-done.8, f32[512,2048]{1,0:T(8,128)} %get-tuple-element.216.refs_0_, bf16[512,2048]{1,0:T(8,128)(2,1)} %collective-permute-done.27.refs_1_, bf16[512,2048]{1,0:T(8,128)(2,1)S(1)} %copy-done.1, ...), custom_call_target="tpu_custom_call" | custom-call | flops 1 | bytes 1 | tf_op jit(solution)/shard_map/norm_back/pallas_call | solution.py:62
  676.8 6.8 sum_rows.1
  (263 shorter events, 171.1 us)
Async XLA Ops:
  7.2 108.0 %all-gather.4.cloned.1.call-start = ((), (), s32[]{:S(2)}) async-start(), calls=%async_computation.5 | async-start | bytes 13369344 | tf_op jit(solution)/shard_map/all_gather | solution.py:829
  11.6 245.4 %all-gather.6.cloned.1.call-start = ((), (), s32[]{:S(2)}) async-start(), calls=%async_computation.6 | async-start | bytes 26738688 | tf_op jit(solution)/shard_map/all_gather | solution.py:829
  14.6 49.7 %collective-permute-start = (bf16[512,2048]{1,0:T(8,128)(2,1)}, bf16[512,2048]{1,0:T(8,128)(2,1)}, u32[]{:S(2)}, u32[]{:S(2)}) collective-permute-start(bf16[512,2048]{1,0:T(8,128)(2,1)} %fusion.2.refs_0_.refs_2_), channel_id=1, source_target_pairs={{0,1},{1,0},{2,3},{3,2},{4,5},{5,4},{6,7},{7,6},{8,9},{9,8},{10,11... | collective-permute-start | bytes 6291464 | tf_op jit(solution)/shard_map/ppermute | solution.py:823
  21.5 126.2 %collective-permute-start.1 = (bf16[512,2048]{1,0:T(8,128)(2,1)}, bf16[512,2048]{1,0:T(8,128)(2,1)}, u32[]{:S(2)}, u32[]{:S(2)}) collective-permute-start(bf16[512,2048]{1,0:T(8,128)(2,1)} %broadcast_select_fusion.refs_0_.refs_2_.refs_3_), channel_id=1, source_target_pairs={{0,1},{1,0},{2,3},{3,2},{4,5},{5,4},{6,7},{7,6},{8,9},{9,8},{10,11... | collective-permute-start | bytes 6291464 | tf_op jit(solution)/shard_map/ppermute | solution.py:823
  34.0 319.1 %all-gather.8.cloned.1.call-start = ((), (), s32[]{:S(2)}) async-start(), calls=%async_computation.7 | async-start | bytes 13369344 | tf_op jit(solution)/shard_map/all_gather | solution.py:829
  73.1 83.9 %collective-permute-start.2 = (bf16[1024,1024]{1,0:T(8,128)(2,1)}, bf16[1024,1024]{1,0:T(8,128)(2,1)}, u32[]{:S(2)}, u32[]{:S(2)}) collective-permute-start(bf16[1024,1024]{1,0:T(8,128)(2,1)} %get-tuple-element.139), channel_id=1, source_target_pairs={{0,2},{2,0},{1,3},{3,1},{4,6},{6,4},{5,7},{7,5},{8,10},{10,8},{9,1... | collective-permute-start | bytes 6291464 | tf_op jit(solution)/shard_map/ppermute | solution.py:733
  139.1 17.9 %collective-permute-start.3 = (bf16[1024,1024]{1,0:T(8,128)(2,1)}, bf16[1024,1024]{1,0:T(8,128)(2,1)}, u32[]{:S(2)}, u32[]{:S(2)}) collective-permute-start(bf16[1024,1024]{1,0:T(8,128)(2,1)} %get-tuple-element.136.refs_0_.refs_2_), channel_id=1, source_target_pairs={{0,2},{2,0},{1,3},{3,1},{4,6},{6,4},{5,7},{7,5},{8,10},{10,8},{9,1... | collective-permute-start | bytes 6291464 | tf_op jit(solution)/shard_map/ppermute | solution.py:733
  146.1 48.1 %collective-permute-start.4 = (bf16[512,2048]{1,0:T(8,128)(2,1)}, bf16[512,2048]{1,0:T(8,128)(2,1)}, u32[]{:S(2)}, u32[]{:S(2)}) collective-permute-start(bf16[512,2048]{1,0:T(8,128)(2,1)} %get-tuple-element.142), channel_id=1, source_target_pairs={{0,1},{1,0},{2,3},{3,2},{4,5},{5,4},{6,7},{7,6},{8,9},{9,8},{10,11... | collective-permute-start | bytes 6291464 | tf_op jit(solution)/shard_map/ppermute | solution.py:823
  200.9 47.3 %collective-permute-start.5 = (bf16[512,2048]{1,0:T(8,128)(2,1)}, bf16[512,2048]{1,0:T(8,128)(2,1)}, u32[]{:S(2)}, u32[]{:S(2)}) collective-permute-start(bf16[512,2048]{1,0:T(8,128)(2,1)} %get-tuple-element.144.refs_0_.refs_2_), channel_id=1, source_target_pairs={{0,1},{1,0},{2,3},{3,2},{4,5},{5,4},{6,7},{7,6},{8,9},{9,8},{10,11... | collective-permute-start | bytes 6291464 | tf_op jit(solution)/shard_map/ppermute | solution.py:823
  206.8 252.6 %reduce-scatter.6.cloned.1.call-start = ((), (), s32[]{:S(2)}) async-start(), calls=%async_computation.8 | async-start | bytes 7864320 | tf_op jit(solution)/shard_map/reduce_scatter | solution.py:761
  207.2 49.8 %collective-permute-start.6 = (bf16[1024,1024]{1,0:T(8,128)(2,1)S(1)}, bf16[1024,1024]{1,0:T(8,128)(2,1)}, u32[]{:S(2)}, u32[]{:S(2)}) collective-permute-start(bf16[1024,1024]{1,0:T(8,128)(2,1)S(1)} %copy-done.12), channel_id=1, source_target_pairs={{0,2},{2,0},{1,3},{3,1},{4,6},{6,4},{5,7},{7,5},{8,10},{10,8},{9,1... | collective-permute-start | bytes 6291464 | tf_op jit(solution)/shard_map/ppermute | solution.py:733
  257.0 36.8 %collective-permute-start.7 = (bf16[1024,1024]{1,0:T(8,128)(2,1)}, bf16[1024,1024]{1,0:T(8,128)(2,1)}, u32[]{:S(2)}, u32[]{:S(2)}) collective-permute-start(bf16[1024,1024]{1,0:T(8,128)(2,1)} %get-tuple-element.149), channel_id=1, source_target_pairs={{0,2},{2,0},{1,3},{3,1},{4,6},{6,4},{5,7},{7,5},{8,10},{10,8},{9,1... | collective-permute-start | bytes 6291464 | tf_op jit(solution)/shard_map/ppermute | solution.py:733
  291.8 61.4 %collective-permute-start.10 = (bf16[1024,1024]{1,0:T(8,128)(2,1)}, bf16[1024,1024]{1,0:T(8,128)(2,1)}, u32[]{:S(2)}, u32[]{:S(2)}) collective-permute-start(bf16[1024,1024]{1,0:T(8,128)(2,1)} %get-tuple-element.156), channel_id=1, source_target_pairs={{0,1},{1,0},{2,3},{3,2},{4,5},{5,4},{6,7},{7,6},{8,9},{9,8},{10,11... | collective-permute-start | bytes 6291464 | tf_op jit(solution)/shard_map/ppermute | solution.py:823
  293.5 19.7 %collective-permute-start.8 = (bf16[1024,4096]{1,0:T(8,128)(2,1)}, bf16[1024,4096]{1,0:T(8,128)(2,1)}, u32[]{:S(2)}, u32[]{:S(2)}) collective-permute-start(bf16[1024,4096]{1,0:T(8,128)(2,1)} %get-tuple-element.148.refs_0_.refs_1_.refs_2_.refs_3_), channel_id=1, source_target_pairs={{0,2},{2,0},{1,3},{3,1},{4,6},{6,4},{5,7},{7,5},{8,10},{10,8},{9,1... | collective-permute-start | bytes 25165832 | tf_op jit(solution)/shard_map/ppermute | solution.py:733
  332.9 196.6 %reduce-scatter.8.cloned.1.call-start = ((), (), s32[]{:S(2)}) async-start(), calls=%async_computation.9 | async-start | bytes 3932160 | tf_op jit(solution)/shard_map/reduce_scatter | solution.py:775
  384.5 48.0 %collective-permute-start.13 = (bf16[512,2048]{1,0:T(8,128)(2,1)}, bf16[512,2048]{1,0:T(8,128)(2,1)}, u32[]{:S(2)}, u32[]{:S(2)}) collective-permute-start(bf16[512,2048]{1,0:T(8,128)(2,1)} %get-tuple-element.165), channel_id=1, source_target_pairs={{0,1},{1,0},{2,3},{3,2},{4,5},{5,4},{6,7},{7,6},{8,9},{9,8},{10,11... | collective-permute-start | bytes 6291464 | tf_op jit(solution)/shard_map/ppermute | solution.py:823
  385.0 57.4 %collective-permute-start.14 = (bf16[1024,1024]{1,0:T(8,128)(2,1)}, bf16[1024,1024]{1,0:T(8,128)(2,1)}, u32[]{:S(2)}, u32[]{:S(2)}) collective-permute-start(bf16[1024,1024]{1,0:T(8,128)(2,1)} %get-tuple-element.169.refs_2_), channel_id=1, source_target_pairs={{0,2},{2,0},{1,3},{3,1},{4,6},{6,4},{5,7},{7,5},{8,10},{10,8},{9,1... | collective-permute-start | bytes 6291464 | tf_op jit(solution)/shard_map/ppermute | solution.py:733
  385.0 74.5 %collective-permute-start.15 = (bf16[512,3072]{1,0:T(8,128)(2,1)}, bf16[512,3072]{1,0:T(8,128)(2,1)}, u32[]{:S(2)}, u32[]{:S(2)}) collective-permute-start(bf16[512,3072]{1,0:T(8,128)(2,1)} %get-tuple-element.174), channel_id=1, source_target_pairs={{0,4},{4,0},{1,5},{5,1},{2,6},{6,2},{3,7},{7,3},{8,12},{12,8},{9,1... | collective-permute-start | bytes 9437192 | tf_op jit(solution)/shard_map/ppermute | solution.py:755
  448.4 17.0 %collective-permute-start.16 = (bf16[512,512]{1,0:T(8,128)(2,1)}, bf16[512,512]{1,0:T(8,128)(2,1)S(1)}, u32[]{:S(2)}, u32[]{:S(2)}) collective-permute-start(bf16[512,512]{1,0:T(8,128)(2,1)} %get-tuple-element.179), channel_id=1, source_target_pairs={{0,1},{1,0},{2,3},{3,2},{4,5},{5,4},{6,7},{7,6},{8,9},{9,8},{10,11... | collective-permute-start | bytes 1572872 | tf_op jit(solution)/shard_map/ppermute | solution.py:823
  448.8 33.9 %collective-permute-start.17 = (bf16[512,512]{1,0:T(8,128)(2,1)}, bf16[512,512]{1,0:T(8,128)(2,1)}, u32[]{:S(2)}, u32[]{:S(2)}) collective-permute-start(bf16[512,512]{1,0:T(8,128)(2,1)} %get-tuple-element.182), channel_id=1, source_target_pairs={{0,1},{1,0},{2,3},{3,2},{4,5},{5,4},{6,7},{7,6},{8,9},{9,8},{10,11... | collective-permute-start | bytes 1572872 | tf_op jit(solution)/shard_map/ppermute | solution.py:823
  457.7 102.8 %collective-permute-start.21 = (bf16[512,2048]{1,0:T(8,128)(2,1)}, bf16[512,2048]{1,0:T(8,128)(2,1)}, u32[]{:S(2)}, u32[]{:S(2)}) collective-permute-start(bf16[512,2048]{1,0:T(8,128)(2,1)} %get-tuple-element.195.refs_0_.refs_2_), channel_id=1, source_target_pairs={{0,1},{1,0},{2,3},{3,2},{4,5},{5,4},{6,7},{7,6},{8,9},{9,8},{10,11... | collective-permute-start | bytes 6291464 | tf_op jit(solution)/shard_map/ppermute | solution.py:823
  458.1 71.4 %collective-permute-start.20 = (bf16[512,3072]{1,0:T(8,128)(2,1)}, bf16[512,3072]{1,0:T(8,128)(2,1)}, u32[]{:S(2)}, u32[]{:S(2)}) collective-permute-start(bf16[512,3072]{1,0:T(8,128)(2,1)} %get-tuple-element.190), channel_id=1, source_target_pairs={{0,4},{4,0},{1,5},{5,1},{2,6},{6,2},{3,7},{7,3},{8,12},{12,8},{9,1... | collective-permute-start | bytes 9437192 | tf_op jit(solution)/shard_map/ppermute | solution.py:755
  465.3 130.3 %reduce-scatter.10.cloned.1.call-start = ((), (), s32[]{:S(2)}) async-start(), calls=%async_computation.10 | async-start | bytes 3932160 | tf_op jit(solution)/shard_map/reduce_scatter | solution.py:775
  482.7 17.8 %collective-permute-start.18 = (bf16[1024,1024]{1,0:T(8,128)(2,1)}, bf16[1024,1024]{1,0:T(8,128)(2,1)}, u32[]{:S(2)}, u32[]{:S(2)}) collective-permute-start(bf16[1024,1024]{1,0:T(8,128)(2,1)} %get-tuple-element.185.refs_2_.refs_0_), channel_id=1, source_target_pairs={{0,2},{2,0},{1,3},{3,1},{4,6},{6,4},{5,7},{7,5},{8,10},{10,8},{9,1... | collective-permute-start | bytes 6291464 | tf_op jit(solution)/shard_map/ppermute | solution.py:733
  521.4 72.1 %collective-permute-start.24 = (bf16[512,1024]{1,0:T(8,128)(2,1)}, bf16[512,1024]{1,0:T(8,128)(2,1)}, u32[]{:S(2)}, u32[]{:S(2)}) collective-permute-start(bf16[512,1024]{1,0:T(8,128)(2,1)} %get-tuple-element.203), channel_id=1, source_target_pairs={{0,4},{4,0},{1,5},{5,1},{2,6},{6,2},{3,7},{7,3},{8,12},{12,8},{9,1... | collective-permute-start | bytes 3145736 | tf_op jit(solution)/shard_map/ppermute | solution.py:755
  522.4 71.1 %collective-permute-start.23 = (bf16[512,1024]{1,0:T(8,128)(2,1)}, bf16[512,1024]{1,0:T(8,128)(2,1)}, u32[]{:S(2)}, u32[]{:S(2)}) collective-permute-start(bf16[512,1024]{1,0:T(8,128)(2,1)} %get-tuple-element.201), channel_id=1, source_target_pairs={{0,4},{4,0},{1,5},{5,1},{2,6},{6,2},{3,7},{7,3},{8,12},{12,8},{9,1... | collective-permute-start | bytes 3145736 | tf_op jit(solution)/shard_map/ppermute | solution.py:755
  535.3 109.3 %reduce-scatter.12.cloned.1.call-start = ((), (), s32[]{:S(2)}) async-start(), calls=%async_computation.11 | async-start | bytes 2621440 | tf_op jit(solution)/shard_map/reduce_scatter | solution.py:775
  538.1 50.7 %collective-permute-start.22 = (bf16[128,3072]{1,0:T(8,128)(2,1)}, bf16[128,3072]{1,0:T(8,128)(2,1)}, u32[]{:S(2)}, u32[]{:S(2)}) collective-permute-start(bf16[128,3072]{1,0:T(8,128)(2,1)} %get-tuple-element.198), channel_id=1, source_target_pairs={{0,4},{4,0},{1,5},{5,1},{2,6},{6,2},{3,7},{7,3},{8,12},{12,8},{9,1... | collective-permute-start | bytes 2359304 | tf_op jit(solution)/shard_map/ppermute | solution.py:766
  584.0 67.3 %collective-permute-start.27 = (bf16[512,2048]{1,0:T(8,128)(2,1)}, bf16[512,2048]{1,0:T(8,128)(2,1)}, u32[]{:S(2)}, u32[]{:S(2)}) collective-permute-start(bf16[512,2048]{1,0:T(8,128)(2,1)} %get-tuple-element.217), channel_id=1, source_target_pairs={{0,1},{1,0},{2,3},{3,2},{4,5},{5,4},{6,7},{7,6},{8,9},{9,8},{10,11... | collective-permute-start | bytes 6291464 | tf_op jit(solution)/shard_map/ppermute | solution.py:823
  588.8 88.0 %collective-permute-start.28 = (bf16[512,2048]{1,0:T(8,128)(2,1)}, bf16[512,2048]{1,0:T(8,128)(2,1)}, u32[]{:S(2)}, u32[]{:S(2)}) collective-permute-start(bf16[512,2048]{1,0:T(8,128)(2,1)} %get-tuple-element.221), channel_id=1, source_target_pairs={{0,1},{1,0},{2,3},{3,2},{4,5},{5,4},{6,7},{7,6},{8,9},{9,8},{10,11... | collective-permute-start | bytes 6291464 | tf_op jit(solution)/shard_map/ppermute | solution.py:823
  600.6 83.0 %reduce-scatter.14.cloned.1.call-start = ((), (), s32[]{:S(2)}) async-start(), calls=%async_computation.12 | async-start | bytes 1310720 | tf_op jit(solution)/shard_map/reduce_scatter | solution.py:775
  610.9 25.1 %collective-permute-start.26 = (bf16[512,1024]{1,0:T(8,128)(2,1)}, bf16[512,1024]{1,0:T(8,128)(2,1)}, u32[]{:S(2)}, u32[]{:S(2)}) collective-permute-start(bf16[512,1024]{1,0:T(8,128)(2,1)} %get-tuple-element.212), channel_id=1, source_target_pairs={{0,4},{4,0},{1,5},{5,1},{2,6},{6,2},{3,7},{7,3},{8,12},{12,8},{9,1... | collective-permute-start | bytes 3145736 | tf_op jit(solution)/shard_map/ppermute | solution.py:755
  (69 other events, 575.5 us)
Sparse Core Ops, SparseCore 0:
  11.7 103.4 all-gather.3
  117.4 126.7 all-gather.5
  247.1 100.7 all-gather.7
  350.0 108.9 reduce-scatter.5
  465.4 60.2 reduce-scatter.7
  535.4 60.1 reduce-scatter.9
  600.7 43.8 reduce-scatter.11
  647.0 26.9 reduce-scatter.13
